TPU v7x, 32 devices: a whole 2x2x4 slice. The times are simulated.
32 devices in a mesh: sect: 2 (over x), lon: 4 (over z), lat: 4 (over y, core).
Axes of the slice: x: 2, y: 2, z: 4, core: 2. Of those that a mesh axis runs over, the one named last changes fastest.
Arguments:
- fields: float32 [2, 6, 16, 32, 512], P('sect', None, None, 'lat', 'lon'), may hold values from -3 to 3, as said below
- levels: int32 [32, 512], P('lat', 'lon'), may hold values from 0 to 16, as said below
Outputs:
- new_fields: float32 [2, 6, 16, 32, 512], P('sect', None, None, 'lat', 'lon')
Inputs may be any that keep to these rules, and one draw needn't show every extreme that they name: `fields`: section 0: velocities of magnitude below 0.95, temperature and salinity, lateral viscosity between 0.02 and 0.2, background diffusivity between 0.05 and 2. Later sections: tracers. In each device's block of 8 x 128 columns at most 768 columns have levels above 0, and some block has exactly 768; the value 16 occurs in every draw.
All inputs are finite; a program needn't handle non-finite values.
Results may differ from a plain program's by a relative error of at most 0.00002.
Values sent between devices are 32-bit elements; how exact they have to be, the bound alone decides.
No kernel may reach another device: no remote copies, remote signals or barrier semaphores. Data moves between devices by JAX's collectives and lax.ppermute only.
A program may use at most 64 MiB of HBM per device.

v0:
```python
import jax
import jax.numpy as jnp
from jax import lax
from jax.sharding import PartitionSpec as P

NSUB = 2


TIME_STEP = 1.0
CORIOLIS = 0.3
THERMAL = 0.2
HALINE = 0.15
GRAVITY_SCALE = 0.05
MIX_BOOST = 4.0
RICHARDSON = 1.0


def with_halo(cells, sides, width):
    for axis, dim in sides:
        count = lax.axis_size(axis)
        head = lax.slice_in_dim(cells, 0, width, axis=dim)
        tail = lax.slice_in_dim(cells, cells.shape[dim] - width, cells.shape[dim], axis=dim)
        cells = jnp.concatenate(
            [
                lax.ppermute(tail, axis, [(i, (i + 1) % count) for i in range(count)]),
                cells,
                lax.ppermute(head, axis, [((i + 1) % count, i) for i in range(count)]),
            ],
            axis=dim,
        )
    return cells


def broadcast(shard, axis, root):
    mine = lax.axis_index(axis) == root
    return lax.psum(jnp.where(mine, shard, jnp.zeros_like(shard)), axis)


def centre(extended):
    return extended[..., 1:-1, 1:-1]


def to_east(extended):
    return extended[..., 1:-1, 2:]


def to_west(extended):
    return extended[..., 1:-1, :-2]


def to_north(extended):
    return extended[..., 2:, 1:-1]


def to_south(extended):
    return extended[..., :-2, 1:-1]


def clear_edges(extended, rim_width):
    row_total = extended.shape[-2]
    row_ids = lax.broadcasted_iota(jnp.int32, (row_total, 1), 0)
    position = lax.axis_index("lat")
    lat_total = lax.axis_size("lat")
    low_bad = (position == 0) & (row_ids < rim_width)
    high_bad = (position == lat_total - 1) & (row_ids >= row_total - rim_width)
    return jnp.where(low_bad | high_bad, 0.0, extended)


def physics(extended, background):
    zonal_vel, merid_vel, temper, saline, viscosity, wetness = extended
    wet_mid = centre(wetness)
    mask_east = wet_mid * to_east(wetness)
    mask_west = to_west(wetness) * wet_mid
    mask_north = wet_mid * to_north(wetness)
    mask_south = to_south(wetness) * wet_mid
    flow_east = centre(zonal_vel) * mask_east
    flow_west = to_west(zonal_vel) * mask_west
    flow_north = centre(merid_vel) * mask_north
    flow_south = to_south(merid_vel) * mask_south
    divergence = flow_east - flow_west + (flow_north - flow_south)
    column_sum = jnp.cumsum(divergence[::-1], axis=0)[::-1]
    vertical = jnp.concatenate([jnp.zeros_like(column_sum[:1]), -column_sum[1:]], axis=0)
    visc_mid = centre(viscosity)
    coef_east = 0.5 * (visc_mid + to_east(viscosity)) * mask_east
    coef_west = 0.5 * (to_west(viscosity) + visc_mid) * mask_west
    coef_north = 0.5 * (visc_mid + to_north(viscosity)) * mask_north
    coef_south = 0.5 * (to_south(viscosity) + visc_mid) * mask_south

    def diffuse(quantity):
        middle = centre(quantity)
        return (
            coef_east * (to_east(quantity) - middle)
            - coef_west * (middle - to_west(quantity))
            + coef_north * (to_north(quantity) - middle)
            - coef_south * (middle - to_south(quantity))
        )

    density = HALINE * saline - THERMAL * temper
    pressure = GRAVITY_SCALE * jnp.cumsum(density * wetness, axis=0)
    press_mid = centre(pressure)
    zonal_new = (
        centre(zonal_vel)
        + TIME_STEP
        * (diffuse(zonal_vel) + CORIOLIS * centre(merid_vel) - (to_east(pressure) - press_mid))
    ) * mask_east
    merid_new = (
        centre(merid_vel)
        + TIME_STEP
        * (diffuse(merid_vel) - CORIOLIS * centre(zonal_vel) - (to_north(pressure) - press_mid))
    ) * mask_north
    temper_new = centre(temper) + TIME_STEP * diffuse(temper)
    saline_new = centre(saline) + TIME_STEP * diffuse(saline)
    temp_jump = THERMAL * (temper_new[:-1] - temper_new[1:])
    mixing = (
        background[1:]
        * (1.0 + MIX_BOOST / (1.0 + RICHARDSON * temp_jump * temp_jump))
        * wet_mid[1:]
    )
    diffusivity = jnp.concatenate([jnp.zeros_like(mixing[:1]), mixing], axis=0)
    return (
        (zonal_new, merid_new, temper_new, saline_new, vertical, diffusivity),
        (flow_east, flow_north, vertical, diffusivity),
    )


def advect(tracer_ext, east_ext, north_ext, step_size):
    east_mid = centre(east_ext)
    east_side = to_west(east_ext)
    north_mid = centre(north_ext)
    north_side = to_south(north_ext)
    middle = centre(tracer_ext)
    flux_east = jnp.maximum(east_mid, 0.0) * middle + jnp.minimum(east_mid, 0.0) * to_east(
        tracer_ext
    )
    flux_west = (
        jnp.maximum(east_side, 0.0) * to_west(tracer_ext) + jnp.minimum(east_side, 0.0) * middle
    )
    flux_north = jnp.maximum(north_mid, 0.0) * middle + jnp.minimum(north_mid, 0.0) * to_north(
        tracer_ext
    )
    flux_south = (
        jnp.maximum(north_side, 0.0) * to_south(tracer_ext) + jnp.minimum(north_side, 0.0) * middle
    )
    return middle - step_size * (flux_east - flux_west + (flux_north - flux_south))


def vertical_factor(vertical, diffusivity):
    up_part = jnp.maximum(vertical, 0.0) + diffusivity
    down_part = jnp.minimum(vertical, 0.0) - diffusivity
    zero_row = jnp.zeros_like(up_part[:1])
    up_next = jnp.concatenate([up_part[1:], zero_row], axis=0)
    down_next = jnp.concatenate([down_part[1:], zero_row], axis=0)
    lower_band = TIME_STEP * down_part
    diagonal = 1.0 + TIME_STEP * (up_part - down_next)
    upper_band = -TIME_STEP * up_next
    ratios = []
    inverses = []
    for index_k in range(vertical.shape[0]):
        pivot_value = diagonal[index_k]
        if index_k > 0:
            pivot_value = pivot_value - lower_band[index_k] * ratios[-1]
        inverse = 1.0 / pivot_value
        ratios.append(upper_band[index_k] * inverse)
        inverses.append(inverse)
    return (lower_band, ratios, inverses)


def thomas_solve(lower_band, ratios, inverses, rhs):
    level_count = rhs.shape[-2]
    forward = [rhs[..., 0, :] * inverses[0]]
    for index_k in range(1, level_count):
        forward.append(
            (rhs[..., index_k, :] - lower_band[index_k] * forward[-1]) * inverses[index_k]
        )
    result = [forward[-1]]
    for index_k in range(level_count - 2, -1, -1):
        result.append(forward[index_k] - ratios[index_k] * result[-1])
    return jnp.stack(result[::-1], axis=-2)


def on_device(fields, levels):
    own_slot = fields[0]
    field_count = own_slot.shape[0]
    layers = own_slot.shape[1]
    lat_rows = levels.shape[0]
    lon_cols = levels.shape[1]
    depth_ids = lax.broadcasted_iota(jnp.int32, (layers, lat_rows, lon_cols), 0)
    wetness = (depth_ids < levels[None]).astype(jnp.float32)
    dyn_ext = with_halo(
        jnp.concatenate([own_slot[:5], wetness[None]], axis=0), (("lon", 3), ("lat", 2)), 1
    )
    dyn_ext = clear_edges(dyn_ext, 1)
    outputs, flow_parts = physics(dyn_ext, own_slot[5])
    flow_stack = broadcast(jnp.stack(flow_parts), "sect", 0)
    sub_step = TIME_STEP / NSUB
    moving = jnp.concatenate([own_slot, flow_stack[0:2]], axis=0)
    extended = clear_edges(with_halo(moving, (("lon", 3), ("lat", 2)), NSUB), NSUB)
    tracer_ext = extended[:field_count]
    east_ext = extended[field_count]
    north_ext = extended[field_count + 1]
    current = tracer_ext
    for substep in range(NSUB):
        current = advect(current, east_ext, north_ext, sub_step)
        east_ext = centre(east_ext)
        north_ext = centre(north_ext)
    total_cols = lat_rows * lon_cols
    vert_flat = flow_stack[2].reshape(layers, total_cols)
    kappa_flat = flow_stack[3].reshape(layers, total_cols)
    flat_rhs = current.reshape(field_count, layers, total_cols)
    lower_band, ratios, inverses = vertical_factor(vert_flat, kappa_flat)
    solved = thomas_solve(lower_band, ratios, inverses, flat_rhs)
    tracer_out = solved.reshape(current.shape) * wetness
    is_physics = lax.axis_index("sect") == 0
    return jnp.where(is_physics, jnp.stack(outputs), tracer_out)[None]


def solution(mesh):
    return jax.shard_map(
        on_device,
        mesh=mesh,
        in_specs=(P("sect", None, None, "lat", "lon"), P("lat", "lon")),
        out_specs=P("sect", None, None, "lat", "lon"),
        check_vma=False,
    )
```

profile of v0, /device:TPU:0, one launch (start us, length us, event | category | flops | bytes accessed | tf_op | source)
XLA Modules:
  0.0 113.9 jit_solution(6585772947945353434)
XLA Ops:
  6.5 0.8 fusion.75
  7.3 1.0 slice_bitcast_fusion
  8.3 0.2 slice_maximum_fusion.1
  8.5 5.1 %collective-permute-start.1 = (f32[6,16,8,1]{3,2,1,0:T(8,128)S(1)}, f32[6,16,8,1]{3,2,1,0:T(8,128)S(1)}, u32[]{:S(2)}, u32[]{:S(2)}) collective-permute-start(f32[6,16,8,1]{3,2,1,0:T(8,128)S(1)} %get-tuple-element.85), channel_id=1, source_target_pairs={{4,0},{8,4},{12,8},{0,12},{5,1},{9,5},{13,9},{1,13},{6,2},{10,6},{... | collective-permute-start | bytes 9224 | tf_op jit(solution)/shard_map/ppermute | solution.py:27
  13.6 9.5 %collective-permute-done.1 = f32[6,16,8,1]{3,2,1,0:T(8,128)S(1)} collective-permute-done((f32[6,16,8,1]{3,2,1,0:T(8,128)S(1)}, f32[6,16,8,1]{3,2,1,0:T(8,128)S(1)}, u32[]{:S(2)}, u32[]{:S(2)}) %collective-permute-start.1) | collective-permute-done | bytes 3104 | tf_op jit(solution)/shard_map/ppermute | solution.py:27
  23.1 8.2 %collective-permute-done = f32[6,16,8,1]{3,2,1,0:T(8,128)S(1)} collective-permute-done((f32[6,16,8,1]{3,2,1,0:T(8,128)S(1)}, f32[6,16,8,1]{3,2,1,0:T(8,128)S(1)}, u32[]{:S(2)}, u32[]{:S(2)}) %collective-permute-start) | collective-permute-done | bytes 3104 | tf_op jit(solution)/shard_map/ppermute | solution.py:25
  31.3 0.7 pad_maximum_fusion.9
  32.0 0.1 collective-permute-start.3
  32.1 0.4 collective-permute-start.2
  32.5 1.8 %collective-permute-done.3 = f32[6,16,1,130]{3,2,1,0:T(1,128)S(1)} collective-permute-done((f32[6,16,1,130]{3,2,1,0:T(1,128)S(1)}, f32[6,16,1,130]{3,2,1,0:T(1,128)S(1)}, u32[]{:S(2)}, u32[]{:S(2)}) %collective-permute-start.3) | collective-permute-done | bytes 49952 | tf_op jit(solution)/shard_map/ppermute | solution.py:27
  34.4 2.8 %collective-permute-done.2 = f32[6,16,1,130]{3,2,1,0:T(1,128)S(1)} collective-permute-done((f32[6,16,1,130]{3,2,1,0:T(1,128)S(1)}, f32[6,16,1,130]{3,2,1,0:T(1,128)S(1)}, u32[]{:S(2)}, u32[]{:S(2)}) %collective-permute-start.2) | collective-permute-done | bytes 49952 | tf_op jit(solution)/shard_map/ppermute | solution.py:25
  37.2 0.8 maximum_select_fusion.1
  38.0 0.1 slice_bitcast_fusion.4
  38.1 0.1 reduce-window_multiply_fusion
  38.3 0.2 fusion.84
  38.4 0.2 subtract_add_fusion
  38.6 0.7 fusion.144
  39.3 0.3 fusion.59
  39.6 0.2 fusion.47
  39.8 0.1 bitcast_dynamic-update-slice_fusion.2
  40.0 0.3 copy-done
  40.3 0.1 slice_multiply_fusion.12
  40.4 0.7 maximum_select_fusion.2
  41.2 0.1 fusion.29
  41.3 21.6 %all-reduce.6.cloned.1.call-done = f32[4,16,8,128]{3,2,1,0:T(8,128)} async-done(((f32[4,16,8,128]{3,2,1,0:T(8,128)}), f32[4,16,8,128]{3,2,1,0:T(8,128)}) %all-reduce.6.cloned.1.call-update) | async-done | bytes 262160 | tf_op jit(solution)/shard_map/psum | solution.py:36
  62.9 0.9 minimum_subtract_fusion
  64.0 0.9 slice.741
  64.9 0.2 slice_maximum_fusion
  65.1 3.4 %collective-permute-start.5 = (f32[8,16,8,2]{3,2,1,0:T(8,128)S(1)}, f32[8,16,8,2]{3,2,1,0:T(8,128)S(1)}, u32[]{:S(2)}, u32[]{:S(2)}) collective-permute-start(f32[8,16,8,2]{3,2,1,0:T(8,128)S(1)} %get-tuple-element.83), channel_id=1, source_target_pairs={{4,0},{8,4},{12,8},{0,12},{5,1},{9,5},{13,9},{1,13},{6,2},{10,6},{... | collective-permute-start | bytes 24584 | tf_op jit(solution)/shard_map/ppermute | solution.py:27
  68.5 12.3 %collective-permute-done.5 = f32[8,16,8,2]{3,2,1,0:T(8,128)S(1)} collective-permute-done((f32[8,16,8,2]{3,2,1,0:T(8,128)S(1)}, f32[8,16,8,2]{3,2,1,0:T(8,128)S(1)}, u32[]{:S(2)}, u32[]{:S(2)}) %collective-permute-start.5) | collective-permute-done | bytes 8224 | tf_op jit(solution)/shard_map/ppermute | solution.py:27
  80.9 10.6 %collective-permute-done.4 = f32[8,16,8,2]{3,2,1,0:T(8,128)S(1)} collective-permute-done((f32[8,16,8,2]{3,2,1,0:T(8,128)S(1)}, f32[8,16,8,2]{3,2,1,0:T(8,128)S(1)}, u32[]{:S(2)}, u32[]{:S(2)}) %collective-permute-start.4) | collective-permute-done | bytes 8224 | tf_op jit(solution)/shard_map/ppermute | solution.py:25
  91.4 0.9 pad_maximum_fusion.5
  92.3 0.1 collective-permute-start.7
  92.4 0.5 collective-permute-start.6
  92.9 0.2 fusion.100
  93.1 5.1 %collective-permute-done.7 = f32[8,16,2,132]{3,2,1,0:T(2,128)S(1)} collective-permute-done((f32[8,16,2,132]{3,2,1,0:T(2,128)S(1)}, f32[8,16,2,132]{3,2,1,0:T(2,128)S(1)}, u32[]{:S(2)}, u32[]{:S(2)}) %collective-permute-start.7) | collective-permute-done | bytes 135200 | tf_op jit(solution)/shard_map/ppermute | solution.py:27
  98.1 2.9 %collective-permute-done.6 = f32[8,16,2,132]{3,2,1,0:T(2,128)S(1)} collective-permute-done((f32[8,16,2,132]{3,2,1,0:T(2,128)S(1)}, f32[8,16,2,132]{3,2,1,0:T(2,128)S(1)}, u32[]{:S(2)}, u32[]{:S(2)}) %collective-permute-start.6) | collective-permute-done | bytes 135200 | tf_op jit(solution)/shard_map/ppermute | solution.py:25
  101.0 1.1 maximum_select_fusion
  102.1 0.2 slice_maximum_fusion.3
  102.4 0.1 slice_maximum_fusion.7
  102.5 0.2 slice_maximum_fusion.5
  102.7 0.1 slice_maximum_fusion.9
  102.8 1.7 %fusion.4 = f32[6,16,10,130]{3,2,1,0:T(8,128)S(1)} fusion(f32[8,16,12,132]{3,2,1,0:T(8,128)S(1)} %maximum_select_fusion, f32[16,10,130]{2,1,0:T(8,128)S(1)} %get-tuple-element.100, f32[16,10,130]{2,1,0:T(8,128)S(1)} %get-tuple-element.101, f32[16,10,130]{2,1,0:T(8,128)S(1)} %get-tuple-element.99, f32[16,10,130]{2,1,0:T(8,128)S(1)} %get-tuple-element.98, ...), kind=kLoop, calls=%fused_computation.6 | loop fusion | flops 2121600 | bytes 3660800 | tf_op jit(solution)/shard_map/sub | solution.py:144
  104.5 0.5 fusion.13
  105.0 0.1 reshape.4118
  105.1 0.4 fusion.87
  105.5 0.5 multiply_subtract_fusion
  106.3 0.8 multiply_select_fusion
  (43 shorter events, 0.3 us)
Async XLA Ops:
  6.5 7.0 %copy-start.1 = (s32[8,128]{1,0:T(8,128)S(1)}, s32[8,128]{1,0:T(8,128)}, u32[]{:S(2)}) copy-start(s32[8,128]{1,0:T(8,128)} %param.3) | copy-start | bytes 12292
  6.5 56.4 %all-reduce.6.cloned.1.call-start = ((), (), s32[]{:S(2)}) async-start(), calls=%async_computation | async-start | bytes 524288 | tf_op jit(solution)/shard_map/psum | solution.py:36
  8.5 14.6 %collective-permute-start.1 = (f32[6,16,8,1]{3,2,1,0:T(8,128)S(1)}, f32[6,16,8,1]{3,2,1,0:T(8,128)S(1)}, u32[]{:S(2)}, u32[]{:S(2)}) collective-permute-start(f32[6,16,8,1]{3,2,1,0:T(8,128)S(1)} %get-tuple-element.85), channel_id=1, source_target_pairs={{4,0},{8,4},{12,8},{0,12},{5,1},{9,5},{13,9},{1,13},{6,2},{10,6},{... | collective-permute-start | bytes 9224 | tf_op jit(solution)/shard_map/ppermute | solution.py:27
  13.6 17.7 %collective-permute-start = (f32[6,16,8,1]{3,2,1,0:T(8,128)S(1)}, f32[6,16,8,1]{3,2,1,0:T(8,128)S(1)}, u32[]{:S(2)}, u32[]{:S(2)}) collective-permute-start(f32[6,16,8,1]{3,2,1,0:T(8,128)S(1)} %get-tuple-element.84), channel_id=1, source_target_pairs={{0,4},{4,8},{8,12},{12,0},{1,5},{5,9},{9,13},{13,1},{2,6},{6,10},{... | collective-permute-start | bytes 9224 | tf_op jit(solution)/shard_map/ppermute | solution.py:25
  32.0 2.4 %collective-permute-start.3 = (f32[6,16,1,130]{3,2,1,0:T(1,128)S(1)}, f32[6,16,1,130]{3,2,1,0:T(1,128)S(1)}, u32[]{:S(2)}, u32[]{:S(2)}) collective-permute-start(f32[6,16,1,130]{3,2,1,0:T(1,128)S(1)} %get-tuple-element.81), channel_id=1, source_target_pairs={{1,0},{2,1},{3,2},{0,3},{5,4},{6,5},{7,6},{4,7},{9,8},{10,9},{11,1... | collective-permute-start | bytes 149768 | tf_op jit(solution)/shard_map/ppermute | solution.py:27
  32.1 5.1 %collective-permute-start.2 = (f32[6,16,1,130]{3,2,1,0:T(1,128)S(1)}, f32[6,16,1,130]{3,2,1,0:T(1,128)S(1)}, u32[]{:S(2)}, u32[]{:S(2)}) collective-permute-start(f32[6,16,1,130]{3,2,1,0:T(1,128)S(1)} %get-tuple-element.80), channel_id=1, source_target_pairs={{0,1},{1,2},{2,3},{3,0},{4,5},{5,6},{6,7},{7,4},{8,9},{9,10},{10,1... | collective-permute-start | bytes 149768 | tf_op jit(solution)/shard_map/ppermute | solution.py:25
  39.3 1.0 copy-start
  65.1 15.8 %collective-permute-start.5 = (f32[8,16,8,2]{3,2,1,0:T(8,128)S(1)}, f32[8,16,8,2]{3,2,1,0:T(8,128)S(1)}, u32[]{:S(2)}, u32[]{:S(2)}) collective-permute-start(f32[8,16,8,2]{3,2,1,0:T(8,128)S(1)} %get-tuple-element.83), channel_id=1, source_target_pairs={{4,0},{8,4},{12,8},{0,12},{5,1},{9,5},{13,9},{1,13},{6,2},{10,6},{... | collective-permute-start | bytes 24584 | tf_op jit(solution)/shard_map/ppermute | solution.py:27
  68.5 23.0 %collective-permute-start.4 = (f32[8,16,8,2]{3,2,1,0:T(8,128)S(1)}, f32[8,16,8,2]{3,2,1,0:T(8,128)S(1)}, u32[]{:S(2)}, u32[]{:S(2)}) collective-permute-start(f32[8,16,8,2]{3,2,1,0:T(8,128)S(1)} %get-tuple-element.82), channel_id=1, source_target_pairs={{0,4},{4,8},{8,12},{12,0},{1,5},{5,9},{9,13},{13,1},{2,6},{6,10},{... | collective-permute-start | bytes 24584 | tf_op jit(solution)/shard_map/ppermute | solution.py:25
  92.3 5.8 %collective-permute-start.7 = (f32[8,16,2,132]{3,2,1,0:T(2,128)S(1)}, f32[8,16,2,132]{3,2,1,0:T(2,128)S(1)}, u32[]{:S(2)}, u32[]{:S(2)}) collective-permute-start(f32[8,16,2,132]{3,2,1,0:T(2,128)S(1)} %get-tuple-element.73), channel_id=1, source_target_pairs={{1,0},{2,1},{3,2},{0,3},{5,4},{6,5},{7,6},{4,7},{9,8},{10,9},{11,1... | collective-permute-start | bytes 405512 | tf_op jit(solution)/shard_map/ppermute | solution.py:27
  92.4 8.6 %collective-permute-start.6 = (f32[8,16,2,132]{3,2,1,0:T(2,128)S(1)}, f32[8,16,2,132]{3,2,1,0:T(2,128)S(1)}, u32[]{:S(2)}, u32[]{:S(2)}) collective-permute-start(f32[8,16,2,132]{3,2,1,0:T(2,128)S(1)} %get-tuple-element.72), channel_id=1, source_target_pairs={{0,1},{1,2},{2,3},{3,0},{4,5},{5,6},{6,7},{7,4},{8,9},{9,10},{10,1... | collective-permute-start | bytes 405512 | tf_op jit(solution)/shard_map/ppermute | solution.py:25
Sparse Core Ops, SparseCore 0:
  41.3 21.6 all-reduce.5
where the time goes:
time: 114 us
  waiting for transfers between devices  74.8 us (66%)
  between operations  13.8 us (12%)
  other arithmetic  13 us (11%)
  starting transfers between devices  9.61 us (8%)
  local copies, waits for them, and re-layouts  2.68 us (2%)
    ppermute x4, waiting for transfers between devices, with_halo(): lax.ppermute(head, axis, [((i + 1) % count, i) for i in range(count)])  28.7 us
    ppermute x4, waiting for transfers between devices, with_halo(): lax.ppermute(tail, axis, [(i, (i + 1) % count) for i in range(count)])  24.5 us
    psum x1, waiting for transfers between devices, broadcast(): return lax.psum(jnp.where(mine, shard, jnp.zeros_like(shard)), axis)  21.6 us
    ppermute x4, starting transfers between devices, with_halo(): lax.ppermute(head, axis, [((i + 1) % count, i) for i in range(count)])  8.68 us
  transfers between devices with their start and end apart: 9, of which 9 were waited for; matrix products, arithmetic and copies ran while one was open for 0% of the time, Pallas kernels for 0%

commit v1 on v0

v1 whole, which is shorter than its diff:
```python
import functools
import jax
import jax.numpy as jnp
from jax import lax
from jax.experimental import pallas as pl
from jax.experimental.pallas import tpu as pltpu
from jax.sharding import PartitionSpec as P

NSUB = 2
TIME_STEP = 1.0
CORIOLIS = 0.3
THERMAL = 0.2
HALINE = 0.15
GRAVITY_SCALE = 0.05
MIX_BOOST = 4.0
RICHARDSON = 1.0

VMEM_LIMIT = 8 * 1024 * 1024

ZONAL_ROW, MERID_ROW, MERID_ROW2, TEMPER_ROW, VISC_ROW = range(5)


def call_kernel(body, outputs, inputs, scratch=()):
    in_vmem = pl.BlockSpec(memory_space=pltpu.VMEM)
    return pl.pallas_call(
        body,
        out_shape=[jax.ShapeDtypeStruct(shape, jnp.float32) for shape in outputs],
        in_specs=[in_vmem] * len(inputs),
        out_specs=[in_vmem] * len(outputs),
        scratch_shapes=[pltpu.VMEM(shape, jnp.float32) for shape in scratch],
        compiler_params=pltpu.CompilerParams(vmem_limit_bytes=VMEM_LIMIT),
    )(*inputs)


class Sizes:
    def __init__(self, fields, levels):
        self.nf, self.lev = fields.shape[1], fields.shape[2]
        self.rows, self.cols = levels.shape
        self.slab = self.lev * self.rows


def lane_ids(shape):
    return lax.broadcasted_iota(jnp.int32, shape, 1)


def row_ids(shape):
    return lax.broadcasted_iota(jnp.int32, shape, 0)


def turn(value, shift, axis):
    size = value.shape[axis]
    shift = shift % size
    return value if shift == 0 else pltpu.roll(value, shift, axis)


def to_lane(value, source, target):
    return turn(value, target - source, 1)


def level_rows(ref, first, row, sz):
    return ref[pl.ds(first + row, sz.lev, stride=sz.rows), :]


def pack_rows(sz, fields, levels, row_a, row_b, cross_a, cross_b, bulk):
    lev = levels[...].astype(jnp.float32)
    even = lax.axis_index("lat") % 2 == 0
    top, second = sz.rows - 1, sz.rows - 2

    def fill(message, cross, near, far):
        for f in range(sz.nf):
            for r, row in enumerate((near, far)):
                at = (2 * f + r) * sz.lev
                message[at : at + sz.lev, :] = level_rows(fields, f * sz.slab, row, sz)
        at = 2 * sz.nf * sz.lev
        message[at : at + 1, :] = lev[near : near + 1, :]
        message[at + 1 : at + 2, :] = lev[far : far + 1, :]
        message[at + 2 : at + 8, :] = jnp.zeros((6, sz.cols), jnp.float32)
        for at, (f, row) in enumerate(((0, near), (1, near), (1, far), (2, near), (4, near))):
            cross[at * sz.lev : (at + 1) * sz.lev, :] = level_rows(fields, f * sz.slab, row, sz)

    @pl.when(even)
    def _():
        fill(row_a, cross_a, top, second)
        fill(row_b, cross_b, 0, 1)

    @pl.when(jnp.logical_not(even))
    def _():
        fill(row_a, cross_a, 0, 1)
        fill(row_b, cross_b, top, second)

    bulk[0 : 2 * sz.slab, :] = fields[0 : 2 * sz.slab, :]
    lane = lane_ids((sz.rows, sz.cols))
    west = jnp.zeros((sz.rows, sz.cols), jnp.float32)
    east = west
    last = sz.cols - 1
    for t, f in enumerate((2, 4)):
        for k in range(sz.lev):
            lane_at = t * sz.lev + k
            at = f * sz.slab + k * sz.rows
            moved = to_lane(fields[at : at + sz.rows, :], last, lane_at)
            east = jnp.where(lane == lane_at, moved, east)
            west = jnp.where(lane == lane_at + 1, moved, west)
    bulk[2 * sz.slab : 2 * sz.slab + sz.rows, :] = jnp.where(
        lane < 2 * sz.lev, turn(west, -1, 1), turn(east, 2 * sz.lev, 1)
    )


def pack_columns(
    sz, fields, levels, row_a, row_b, cross_a, cross_b, bulk,
    to_east, to_west, south, north, cross_south, cross_north, bulk_two,
):
    position = lax.axis_index("lat")
    even = position % 2 == 0
    has_south = position > 0
    has_north = position < lax.axis_size("lat") - 1
    for low, high, from_a, from_b in ((south, north, row_a, row_b), (cross_south, cross_north, cross_a, cross_b)):
        first, other = from_a[...], from_b[...]
        low[...] = jnp.where(has_south, jnp.where(even, other, first), 0.0)
        high[...] = jnp.where(has_north, jnp.where(even, first, other), 0.0)

    for at, f in enumerate((2, 4, 5)):
        bulk_two[at * sz.slab : (at + 1) * sz.slab, :] = fields[f * sz.slab : (f + 1) * sz.slab, :]

    tile = (sz.rows, sz.cols)
    lane = lane_ids(tile)
    zero = jnp.zeros(tile, jnp.float32)
    last = sz.cols - 1
    east_one, west_one, west_two, east_two = zero, zero, zero, zero
    for f in range(sz.nf + 2):
        for k in range(sz.lev):
            if f < sz.nf:
                at = f * sz.slab + k * sz.rows
                values = fields[at : at + sz.rows, :]
            else:
                at = (f - sz.nf) * sz.slab + k * sz.rows
                values = bulk[at : at + sz.rows, :]
            p = f * sz.lev + k
            moved = to_lane(values, last, p)
            east_one = jnp.where(lane == p, moved, east_one)
            west_one = jnp.where(lane == (p + 1) % sz.cols, moved, west_one)
            if f <= sz.nf:
                west_two = jnp.where(lane == (p + 2) % sz.cols, moved, west_two)
                east_two = jnp.where(lane == (p - 1) % sz.cols, moved, east_two)
    to_east[0 : sz.rows, :] = east_one
    to_east[sz.rows : 2 * sz.rows, :] = turn(east_two, 1, 1)
    to_west[0 : sz.rows, :] = turn(west_one, -1, 1)
    to_west[sz.rows : 2 * sz.rows, :] = turn(west_two, -2, 1)

    lev = levels[...].astype(jnp.float32)
    side = bulk[2 * sz.slab : 2 * sz.slab + sz.rows, :]
    level_row = 2 * sz.nf * sz.lev
    south_lev = south[level_row : level_row + 1, :]
    north_lev = north[level_row : level_row + 1, :]
    base = 2 * sz.lev
    for message, near, far, shift in ((to_east, last, last - 1, -base), (to_west, 0, 1, 0)):
        part = turn(side, shift, 1)
        part = jnp.where(lane == base, to_lane(lev, near, base), part)
        part = jnp.where(lane == base + 1, to_lane(lev, far, base + 1), part)
        low = jnp.broadcast_to(to_lane(south_lev, near, base + 2), tile)
        high = jnp.broadcast_to(to_lane(north_lev, near, base + 3), tile)
        part = jnp.where(lane == base + 2, low, part)
        part = jnp.where(lane == base + 3, high, part)
        message[2 * sz.rows : 3 * sz.rows, :] = part

    tall = (sz.lev, sz.cols)
    tall_lane = lane_ids(tall)
    east_corner = jnp.zeros(tall, jnp.float32)
    west_corner = east_corner
    for r, (rows, cross) in enumerate(((south, cross_south), (north, cross_north))):
        for f in range(sz.nf + 2):
            if f < sz.nf:
                values = rows[2 * f * sz.lev : (2 * f + 1) * sz.lev, :]
            else:
                at = (ZONAL_ROW, MERID_ROW)[f - sz.nf] * sz.lev
                values = cross[at : at + sz.lev, :]
            p = r * (sz.nf + 2) + f
            moved = to_lane(values, last, p)
            east_corner = jnp.where(tall_lane == p, moved, east_corner)
            west_corner = jnp.where(tall_lane == p + 1, moved, west_corner)
    to_east[3 * sz.rows : 3 * sz.rows + sz.lev, :] = east_corner
    to_west[3 * sz.rows : 3 * sz.rows + sz.lev, :] = turn(west_corner, -1, 1)


def shift_west(value, lane, edge):
    return jnp.where(lane == 0, edge, turn(value, 1, 1))


def shift_east(value, lane, edge):
    return jnp.where(lane == value.shape[1] - 1, edge, turn(value, -1, 1))


def shift_south(value, row, edge):
    return jnp.where(row == 0, edge, turn(value, 1, 0))


def shift_north(value, row, edge):
    return jnp.where(row == value.shape[0] - 1, edge, turn(value, -1, 0))


class Weights:
    def __init__(self, east, west, north, south, step):
        self.own = 1.0 - step * (
            jnp.maximum(east, 0.0) - jnp.minimum(west, 0.0) + (jnp.maximum(north, 0.0) - jnp.minimum(south, 0.0))
        )
        self.east = -step * jnp.minimum(east, 0.0)
        self.west = step * jnp.maximum(west, 0.0)
        self.north = -step * jnp.minimum(north, 0.0)
        self.south = step * jnp.maximum(south, 0.0)

    def apply(self, own, east, west, north, south):
        return self.own * own + self.east * east + self.west * west + (self.north * north + self.south * south)


def finish(
    sz, fields, levels, south, north, cross_south, cross_north, bulk, bulk_two,
    own_east, own_west, from_west, from_east,
    out, div, mix, vert, low_strip, high_strip, side_strips, ratio, forward,
):
    tile = (sz.rows, sz.cols)
    lane, row = lane_ids(tile), row_ids(tile)
    last_lane, last_row = sz.cols - 1, sz.rows - 1
    lev = levels[...].astype(jnp.float32)
    level_row = 2 * sz.nf * sz.lev
    side_base = 2 * sz.lev
    west_side = from_west[2 * sz.rows : 3 * sz.rows, :]
    east_side = from_east[2 * sz.rows : 3 * sz.rows, :]
    lev_w = shift_west(lev, lane, to_lane(west_side, side_base, 0))
    lev_e = shift_east(lev, lane, to_lane(east_side, side_base, last_lane))
    south_lev, north_lev = south[level_row : level_row + 1, :], north[level_row : level_row + 1, :]
    lev_s = shift_south(lev, row, south_lev)
    lev_n = shift_north(lev, row, north_lev)

    def masks(k):
        wet = lev > k
        return wet, wet & (lev_e > k), wet & (lev_w > k), wet & (lev_n > k), wet & (lev_s > k)

    def keep(mask, value):
        return jnp.where(mask, value, 0.0)

    is_dynamics = lax.axis_index("sect") == 0

    def physics(full):
        cross_of = {0: ZONAL_ROW, 1: MERID_ROW, 2: TEMPER_ROW, 4: VISC_ROW}

        def own(f, k):
            at = k * sz.rows
            if full:
                return fields[f * sz.slab + at : f * sz.slab + at + sz.rows, :]
            if f < 2:
                return bulk[f * sz.slab + at : f * sz.slab + at + sz.rows, :]
            at += {2: 0, 4: 1, 5: 2}[f] * sz.slab
            return bulk_two[at : at + sz.rows, :]

        def beyond_row(f, k, ref, cross):
            if full:
                at = 2 * f * sz.lev + k
                return ref[at : at + 1, :]
            at = cross_of[f] * sz.lev + k
            return cross[at : at + 1, :]

        def beyond_column(f, k, message, target):
            if full:
                return to_lane(message[0 : sz.rows, :], f * sz.lev + k, target)
            if f < 2:
                return to_lane(message[0 : sz.rows, :], (sz.nf + f) * sz.lev + k, target)
            return to_lane(message[2 * sz.rows : 3 * sz.rows, :], {2: 0, 4: 1}[f] * sz.lev + k, target)

        def west_of(value, f, k):
            return shift_west(value, lane, beyond_column(f, k, from_west, 0))

        def east_of(value, f, k):
            return shift_east(value, lane, beyond_column(f, k, from_east, last_lane))

        def south_of(value, f, k):
            return shift_south(value, row, beyond_row(f, k, south, cross_south))

        def north_of(value, f, k):
            return shift_north(value, row, beyond_row(f, k, north, cross_north))

        def around(f, k):
            value = own(f, k)
            return value, east_of(value, f, k), west_of(value, f, k), north_of(value, f, k), south_of(value, f, k)

        press = jnp.zeros(tile, jnp.float32)
        press_e, press_n, warm_above = press, press, press
        for k in range(sz.lev):
            at = k * sz.rows
            wet, wet_e, wet_w, wet_n, wet_s = masks(k)
            if full:
                zonal = around(0, k)
                merid = around(1, k)
                zonal_mid, zonal_west, merid_mid, merid_south = zonal[0], zonal[2], merid[0], merid[4]
            else:
                zonal_mid, merid_mid = own(0, k), own(1, k)
                zonal_west, merid_south = west_of(zonal_mid, 0, k), south_of(merid_mid, 1, k)
            flow_east, flow_west = keep(wet_e, zonal_mid), keep(wet_w, zonal_west)
            flow_north, flow_south = keep(wet_n, merid_mid), keep(wet_s, merid_south)
            div[at : at + sz.rows, :] = flow_east - flow_west + (flow_north - flow_south)
            visc, visc_e, visc_w, visc_n, visc_s = around(4, k)
            coef_e = keep(wet_e, 0.5 * (visc + visc_e))
            coef_w = keep(wet_w, 0.5 * (visc_w + visc))
            coef_n = keep(wet_n, 0.5 * (visc + visc_n))
            coef_s = keep(wet_s, 0.5 * (visc_s + visc))

            def diffuse(parts):
                mid, e, w, n, s = parts
                return coef_e * (e - mid) - coef_w * (mid - w) + coef_n * (n - mid) - coef_s * (mid - s)

            temper = around(2, k)
            warm = temper[0] + TIME_STEP * diffuse(temper)
            if k == 0:
                mixing = jnp.zeros(tile, jnp.float32)
            else:
                jump = THERMAL * (warm_above - warm)
                mixing = keep(wet, own(5, k) * (1.0 + MIX_BOOST / (1.0 + RICHARDSON * jump * jump)))
            warm_above = warm
            if not full:
                mix[at : at + sz.rows, :] = mixing
                continue
            saline = around(3, k)

            def weight(place, mask):
                return keep(mask, HALINE * saline[place] - THERMAL * temper[place])

            press = press + GRAVITY_SCALE * weight(0, wet)
            press_e = press_e + GRAVITY_SCALE * weight(1, lev_e > k)
            press_n = press_n + GRAVITY_SCALE * weight(3, lev_n > k)
            zonal_new = zonal_mid + TIME_STEP * (diffuse(zonal) + CORIOLIS * merid_mid - (press_e - press))
            merid_new = merid_mid + TIME_STEP * (diffuse(merid) - CORIOLIS * zonal_mid - (press_n - press))
            out[at : at + sz.rows, :] = keep(wet_e, zonal_new)
            out[sz.slab + at : sz.slab + at + sz.rows, :] = keep(wet_n, merid_new)
            out[2 * sz.slab + at : 2 * sz.slab + at + sz.rows, :] = warm
            out[3 * sz.slab + at : 3 * sz.slab + at + sz.rows, :] = saline[0] + TIME_STEP * diffuse(saline)
            out[5 * sz.slab + at : 5 * sz.slab + at + sz.rows, :] = mixing
        total = jnp.zeros(tile, jnp.float32)
        for k in range(sz.lev - 1, -1, -1):
            at = k * sz.rows
            total = total + div[at : at + sz.rows, :]
            value = -total if k > 0 else jnp.zeros(tile, jnp.float32)
            if full:
                out[4 * sz.slab + at : 4 * sz.slab + at + sz.rows, :] = value
            else:
                vert[at : at + sz.rows, :] = value

    def row_strips(step):
        tall = (sz.lev, sz.cols)
        lane16, depth = lane_ids(tall), row_ids(tall).astype(jnp.float32)

        def wet(levels_row):
            return levels_row > depth

        west_corner = from_west[3 * sz.rows : 3 * sz.rows + sz.lev, :]
        east_corner = from_east[3 * sz.rows : 3 * sz.rows + sz.lev, :]
        lane1 = lane_ids((1, sz.cols))
        for r in range(2):
            rows, cross = (south, cross_south) if r == 0 else (north, cross_north)
            strip = low_strip if r == 0 else high_strip
            edge = 0 if r == 0 else last_row
            near_lev = rows[level_row : level_row + 1, :]
            far_lev = rows[level_row + 1 : level_row + 2, :]
            own_lev = lev[edge : edge + 1, :]
            corner_lane = side_base + 2 + r
            lev_at_w = shift_west(near_lev, lane1, to_lane(west_side[0:1, :], corner_lane, 0))
            lev_at_e = shift_east(near_lev, lane1, to_lane(east_side[0:1, :], corner_lane, last_lane))
            wet_near = wet(near_lev)
            zonal = cross[ZONAL_ROW * sz.lev : (ZONAL_ROW + 1) * sz.lev, :]
            p = r * (sz.nf + 2)
            zonal_w = shift_west(zonal, lane16, to_lane(west_corner, p + sz.nf, 0))
            flow_e = keep(wet_near & wet(lev_at_e), zonal)
            flow_w = keep(wet_near & wet(lev_at_w), zonal_w)
            merid = cross[MERID_ROW * sz.lev : (MERID_ROW + 1) * sz.lev, :]
            if r == 0:
                merid_far = cross[MERID_ROW2 * sz.lev : (MERID_ROW2 + 1) * sz.lev, :]
                flow_n = keep(wet_near & wet(own_lev), merid)
                flow_s = keep(wet_near & wet(far_lev), merid_far)
            else:
                flow_n = keep(wet_near & wet(far_lev), merid)
                flow_s = keep(wet_near & wet(own_lev), level_rows(bulk, sz.slab, last_row, sz))
            weights = Weights(flow_e, flow_w, flow_n, flow_s, step)
            for f in range(sz.nf):
                at = 2 * f * sz.lev
                near, far = rows[at : at + sz.lev, :], rows[at + sz.lev : at + 2 * sz.lev, :]
                inside = level_rows(fields, f * sz.slab, edge, sz)
                at_w = shift_west(near, lane16, to_lane(west_corner, p + f, 0))
                at_e = shift_east(near, lane16, to_lane(east_corner, p + f, last_lane))
                up, down = (inside, far) if r == 0 else (far, inside)
                strip[f * sz.lev : (f + 1) * sz.lev, :] = weights.apply(near, at_e, at_w, up, down)

    def column_strips(step):
        tall = (sz.lev, sz.cols)
        lane16, depth16 = lane_ids(tall), row_ids(tall)
        depth = (lane % sz.lev).astype(jnp.float32)

        def column(value, at):
            return jnp.broadcast_to(value[:, at : at + 1], tile)

        def all_fields(value, first):
            value = jnp.where((lane >= first) & (lane < first + sz.lev), value, 0.0)
            width = sz.lev
            while width < sz.cols:
                value = value + turn(value, width, 1)
                width *= 2
            return value

        def corner_rows(message, r):
            items = message[3 * sz.rows : 3 * sz.rows + sz.lev, :]
            p = r * (sz.nf + 2)
            tracers = jnp.zeros(tall, jnp.float32)
            for f in range(sz.nf):
                spread = jnp.broadcast_to(items[:, p + f : p + f + 1], tall)
                tracers = jnp.where(lane16 == f * sz.lev + depth16, spread, tracers)
            spread = jnp.broadcast_to(items[:, p + sz.nf + 1 : p + sz.nf + 2], tall)
            velocity = jnp.where(lane16 % sz.lev == depth16, spread, 0.0)
            return jnp.sum(tracers, axis=0, keepdims=True), jnp.sum(velocity, axis=0, keepdims=True)

        for side in range(2):
            message, own_message = (from_west, own_west) if side == 0 else (from_east, own_east)
            edge = 0 if side == 0 else last_lane
            aside = west_side if side == 0 else east_side
            near, far = message[0 : sz.rows, :], message[sz.rows : 2 * sz.rows, :]
            inside = own_message[0 : sz.rows, :]
            low_tracers, low_merid = corner_rows(message, 0)
            high_tracers, _ = corner_rows(message, 1)
            near_lev, far_lev = column(aside, side_base), column(aside, side_base + 1)
            own_lev = column(lev, edge)
            lev_at_s = shift_south(near_lev, row, column(aside, side_base + 2))
            lev_at_n = shift_north(near_lev, row, column(aside, side_base + 3))
            wet_near = near_lev > depth
            zonal_first = sz.nf * sz.lev
            if side == 0:
                flow_e = keep(wet_near & (own_lev > depth), all_fields(near, zonal_first))
                flow_w = keep(wet_near & (far_lev > depth), all_fields(far, zonal_first))
            else:
                flow_e = keep(wet_near & (far_lev > depth), all_fields(near, zonal_first))
                flow_w = keep(wet_near & (own_lev > depth), all_fields(inside, zonal_first))
            merid = all_fields(near, zonal_first + sz.lev)
            merid_s = shift_south(merid, row, low_merid)
            flow_n = keep(wet_near & (lev_at_n > depth), merid)
            flow_s = keep(wet_near & (lev_at_s > depth), merid_s)
            at_s = shift_south(near, row, low_tracers)
            at_n = shift_north(near, row, high_tracers)
            east, west = (inside, far) if side == 0 else (far, inside)
            weights = Weights(flow_e, flow_w, flow_n, flow_s, step)
            side_strips[side * sz.rows : (side + 1) * sz.rows, :] = weights.apply(near, east, west, at_n, at_s)

    def transport(step):
        west_old, east_old = from_west[0 : sz.rows, :], from_east[0 : sz.rows, :]
        west_new, east_new = side_strips[0 : sz.rows, :], side_strips[sz.rows : 2 * sz.rows, :]
        zero = jnp.zeros(tile, jnp.float32)

        def faces(k):
            if k == sz.lev:
                return zero, zero
            at = k * sz.rows
            speed, mixing = vert[at : at + sz.rows, :], mix[at : at + sz.rows, :]
            return jnp.maximum(speed, 0.0) + mixing, jnp.minimum(speed, 0.0) - mixing

        previous = [None] * sz.nf
        last_ratio = None
        up, down = faces(0)
        for k in range(sz.lev):
            at = k * sz.rows
            wet, wet_e, wet_w, wet_n, wet_s = masks(k)
            zonal, merid = bulk[at : at + sz.rows, :], bulk[sz.slab + at : sz.slab + at + sz.rows, :]
            zonal_first = sz.nf * sz.lev
            zonal_west = shift_west(zonal, lane, to_lane(west_old, zonal_first + k, 0))
            beyond = MERID_ROW * sz.lev + k
            merid_south = shift_south(merid, row, cross_south[beyond : beyond + 1, :])
            weights = Weights(
                keep(wet_e, zonal), keep(wet_w, zonal_west), keep(wet_n, merid), keep(wet_s, merid_south), step
            )
            up_next, down_next = faces(k + 1)
            pivot = 1.0 + TIME_STEP * (up - down_next)
            lower = TIME_STEP * down
            if k > 0:
                pivot = pivot - lower * last_ratio
            inverse = 1.0 / pivot
            last_ratio = -TIME_STEP * up_next * inverse
            ratio[at : at + sz.rows, :] = last_ratio
            up, down = up_next, down_next
            for f in range(sz.nf):
                p = f * sz.lev + k
                value = fields[f * sz.slab + at : f * sz.slab + at + sz.rows, :]
                near = 2 * f * sz.lev + k
                for west, east, low, high in (
                    (west_old, east_old, south[near : near + 1, :], north[near : near + 1, :]),
                    (west_new, east_new, low_strip[p : p + 1, :], high_strip[p : p + 1, :]),
                ):
                    value = weights.apply(
                        value,
                        shift_east(value, lane, to_lane(east, p, last_lane)),
                        shift_west(value, lane, to_lane(west, p, 0)),
                        shift_north(value, row, high),
                        shift_south(value, row, low),
                    )
                if k > 0:
                    value = value - lower * previous[f]
                value = value * inverse
                previous[f] = value
                forward[f * sz.slab + at : f * sz.slab + at + sz.rows, :] = value
        for k in range(sz.lev - 1, -1, -1):
            at = k * sz.rows
            wet = lev > k
            for f in range(sz.nf):
                here = f * sz.slab + at
                if k < sz.lev - 1:
                    previous[f] = forward[here : here + sz.rows, :] - ratio[at : at + sz.rows, :] * previous[f]
                out[here : here + sz.rows, :] = keep(wet, previous[f])

    @pl.when(is_dynamics)
    def _():
        physics(True)

    @pl.when(jnp.logical_not(is_dynamics))
    def _():
        step = TIME_STEP / NSUB
        row_strips(step)
        column_strips(step)
        physics(False)
        transport(step)


def pair_of(index, count, odd):
    if not odd:
        return index ^ 1
    return (((index + 1) ^ 1) - 1) % count


def on_device(sizes_of, fields, levels):
    sz = Sizes(fields, levels)
    count_s, count_o, count_a = sizes_of
    flat = fields.reshape(sz.nf * sz.slab, sz.cols)
    axes = ("sect", "lon", "lat")

    def swap(value, odd):
        pairs = [(i, pair_of(i, count_a, odd)) for i in range(count_a)]
        return lax.ppermute(value, "lat", pairs)

    def from_dynamics(value, odd=None):
        mine = lax.axis_index("sect")
        got = None
        for hop in range(1, count_s):
            pairs = []
            for s in range(count_s):
                for o in range(count_o):
                    for a in range(count_a):
                        b = a if odd is None else pair_of(a, count_a, odd)
                        pairs.append(((s * count_o + o) * count_a + a, (((s + hop) % count_s) * count_o + o) * count_a + b))
            if odd is None:
                part = lax.ppermute(value, "sect", [(s, (s + hop) % count_s) for s in range(count_s)])
            else:
                part = lax.ppermute(value, axes, pairs)
            got = part if got is None else jnp.where(mine == hop, part, got)
        return got

    def around(value, step):
        return lax.ppermute(value, "lon", [(i, (i + step) % count_o) for i in range(count_o)])

    rows_shape = ((2 * sz.nf * sz.lev + 8), sz.cols)
    cross_shape = (5 * sz.lev, sz.cols)
    columns_shape = (3 * sz.rows + sz.lev, sz.cols)
    row_a, row_b, cross_a, cross_b, bulk = call_kernel(
        functools.partial(pack_rows, sz),
        [rows_shape, rows_shape, cross_shape, cross_shape, (2 * sz.slab + sz.rows, sz.cols)],
        [flat, levels],
    )
    bulk = from_dynamics(bulk)
    cross_b = from_dynamics(cross_b, True)
    row_b = swap(row_b, True)
    cross_a = from_dynamics(cross_a, False)
    row_a = swap(row_a, False)
    to_east, to_west, south, north, cross_south, cross_north, bulk_two = call_kernel(
        functools.partial(pack_columns, sz),
        [columns_shape] * 2 + [rows_shape] * 2 + [cross_shape] * 2 + [(3 * sz.slab, sz.cols)],
        [flat, levels, row_a, row_b, cross_a, cross_b, bulk],
    )
    bulk_two = from_dynamics(bulk_two)
    from_east = around(to_west, -1)
    from_west = around(to_east, 1)
    slab = (sz.slab, sz.cols)
    (out,) = call_kernel(
        functools.partial(finish, sz),
        [flat.shape],
        [flat, levels, south, north, cross_south, cross_north, bulk, bulk_two, to_east, to_west, from_west, from_east],
        [slab, slab, slab, (sz.nf * sz.lev, sz.cols), (sz.nf * sz.lev, sz.cols), (2 * sz.rows, sz.cols), slab, flat.shape],
    )
    return out.reshape(fields.shape)


def solution(mesh):
    sizes_of = (mesh.shape["sect"], mesh.shape["lon"], mesh.shape["lat"])
    return jax.shard_map(
        functools.partial(on_device, sizes_of),
        mesh=mesh,
        in_specs=(P("sect", None, None, "lat", "lon"), P("lat", "lon")),
        out_specs=P("sect", None, None, "lat", "lon"),
        check_vma=False,
    )
```

time: 114 us -> 25.8 us (0.23)
  the two profiles are of different devices: /device:TPU:0 before, /device:TPU:2 now
where the time goes in v1:
time: 25.8 us; the launch traced here: 25.6 us
  Pallas kernels  8.97 us (35%)
  starting transfers between devices  7.78 us (30%)
  waiting for transfers between devices  7.14 us (28%)
  local copies, waits for them, and re-layouts  1.68 us (7%)
    pallas_call x3, Pallas kernels, call_kernel(): pl.pallas_call(body, out_shape=[jax.ShapeDtypeStruct(shape, jnp.float32)...  8.97 us
    ppermute x2, waiting for transfers between devices, from_dynamics(): part = lax.ppermute(value, axes, pairs)  4.18 us
    ppermute x2, starting transfers between devices, around(): lax.ppermute(value, 'lon', [(i, (i + step) % count_o) for i in range(coun...  3.82 us
    ppermute x2, starting transfers between devices, swap(): return lax.ppermute(value, 'lat', pairs)  2.15 us
    ppermute x2, waiting for transfers between devices, around(): lax.ppermute(value, 'lon', [(i, (i + step) % count_o) for i in range(coun...  1.76 us
    unnamed x4, local copies, waits for them, and re-layouts  1.68 us
    ppermute x2, starting transfers between devices, from_dynamics(): part = lax.ppermute(value, axes, pairs)  1.25 us
    ppermute x2, waiting for transfers between devices, from_dynamics(): lax.ppermute(value, 'sect', [(s, (s + hop) % count_s) for s in range(coun...  1.2 us
  transfers between devices with their start and end apart: 8, of which 4 were waited for; matrix products, arithmetic and copies ran while one was open for 0% of the time, Pallas kernels for 0%

profile of v1, /device:TPU:2, one launch (start us, length us, event | category | flops | bytes accessed | tf_op | source)
XLA Modules:
  0.0 25.6 jit_solution(7678093093709293208)
XLA Ops:
  0.0 0.0 copy-start
  0.0 1.0 %copy-done = f32[1,6,16,8,128]{4,3,2,1,0:T(8,128)S(1)} copy-done((f32[1,6,16,8,128]{4,3,2,1,0:T(8,128)S(1)}, f32[1,6,16,8,128]{4,3,2,1,0:T(8,128)}, u32[]{:S(2)}) %copy-start) | copy-done | bytes 393240
  1.0 0.0 copy-start.1
  1.0 0.7 %copy-done.1 = s32[8,128]{1,0:T(8,128)S(1)} copy-done((s32[8,128]{1,0:T(8,128)S(1)}, s32[8,128]{1,0:T(8,128)}, u32[]{:S(2)}) %copy-start.1) | copy-done | bytes 4120
  1.7 0.2 shard_map.28
  1.9 0.0 collective-permute-start.4
  1.9 0.1 collective-permute-start
  2.0 2.1 %collective-permute-start.1 = (f32[200,128]{1,0:T(8,128)S(1)}, f32[200,128]{1,0:T(8,128)S(1)}, u32[]{:S(2)}, u32[]{:S(2)}) collective-permute-start(f32[200,128]{1,0:T(8,128)S(1)} %get-tuple-element.18), channel_id=1, source_target_pairs={{0,3},{1,2},{2,1},{3,0},{4,7},{5,6},{6,5},{7,4},{8,11},{9,10},{10,... | collective-permute-start | bytes 307208 | tf_op jit(solution)/shard_map/ppermute | solution.py:537
  4.1 1.1 %collective-permute-start.2 = (f32[80,128]{1,0:T(8,128)S(1)}, f32[80,128]{1,0:T(8,128)S(1)}, u32[]{:S(2)}, u32[]{:S(2)}) collective-permute-start(f32[80,128]{1,0:T(8,128)S(1)} %get-tuple-element.19), channel_id=1, source_target_pairs={{0,17},{1,16},{2,19},{3,18},{4,21},{5,20},{6,23},{7,22},{8,25},{9,... | collective-permute-start | bytes 122888 | tf_op jit(solution)/shard_map/ppermute | solution.py:552
  5.2 0.1 collective-permute-start.3
  5.3 2.7 %collective-permute-done.2.cross_a = f32[80,128]{1,0:T(8,128)S(1)} collective-permute-done((f32[80,128]{1,0:T(8,128)S(1)}, f32[80,128]{1,0:T(8,128)S(1)}, u32[]{:S(2)}, u32[]{:S(2)}) %collective-permute-start.2) | collective-permute-done | bytes 40992 | tf_op jit(solution)/shard_map/ppermute | solution.py:552
  8.0 1.5 %collective-permute-done.3.cross_b = f32[80,128]{1,0:T(8,128)S(1)} collective-permute-done((f32[80,128]{1,0:T(8,128)S(1)}, f32[80,128]{1,0:T(8,128)S(1)}, u32[]{:S(2)}, u32[]{:S(2)}) %collective-permute-start.3) | collective-permute-done | bytes 40992 | tf_op jit(solution)/shard_map/ppermute | solution.py:552
  9.5 0.0 collective-permute-done.row_a
  9.5 0.0 collective-permute-done.1.row_b
  9.5 0.0 collective-permute-done.4.bulk
  9.5 0.3 %shard_map.29 = (f32[40,128]{1,0:T(8,128)S(1)}, f32[40,128]{1,0:T(8,128)S(1)}, f32[200,128]{1,0:T(8,128)S(1)}, f32[200,128]{1,0:T(8,128)S(1)}, f32[80,128]{1,0:T...) custom-call(f32[768,128]{1,0:T(8,128)S(1)} %bitcast.3, s32[8,128]{1,0:T(8,128)S(1)} %copy-done.1, ...), custom_call_target="tpu_custom_call" | custom-call | tf_op jit(solution)/shard_map/pallas_call | solution.py:25
  9.8 0.6 %collective-permute-start.5 = (f32[384,128]{1,0:T(8,128)S(1)}, f32[384,128]{1,0:T(8,128)S(1)}, u32[]{:S(2)}, u32[]{:S(2)}) collective-permute-start(f32[384,128]{1,0:T(8,128)S(1)} %get-tuple-element.26), channel_id=1, source_target_pairs={{0,16},{16,0},{1,17},{17,1},{2,18},{18,2},{3,19},{19,3},{4,20},{20... | collective-permute-start | bytes 589832 | tf_op jit(solution)/shard_map/ppermute | solution.py:550
  10.4 1.6 %collective-permute-start.6 = (f32[40,128]{1,0:T(8,128)S(1)}, f32[40,128]{1,0:T(8,128)S(1)}, u32[]{:S(2)}, u32[]{:S(2)}) collective-permute-start(f32[40,128]{1,0:T(8,128)S(1)} %get-tuple-element.27.own_east), channel_id=1, source_target_pairs={{0,4},{4,8},{8,12},{12,0},{1,5},{5,9},{9,13},{13,1},{2,6},{6,10},{... | collective-permute-start | bytes 61448 | tf_op jit(solution)/shard_map/ppermute | solution.py:557
  11.9 2.2 %collective-permute-start.7 = (f32[40,128]{1,0:T(8,128)S(1)}, f32[40,128]{1,0:T(8,128)S(1)}, u32[]{:S(2)}, u32[]{:S(2)}) collective-permute-start(f32[40,128]{1,0:T(8,128)S(1)} %get-tuple-element.28.own_west), channel_id=1, source_target_pairs={{0,12},{4,0},{8,4},{12,8},{1,13},{5,1},{9,5},{13,9},{2,14},{6,2},{... | collective-permute-start | bytes 61448 | tf_op jit(solution)/shard_map/ppermute | solution.py:557
  14.2 1.8 %collective-permute-done.6.from_west = f32[40,128]{1,0:T(8,128)S(1)} collective-permute-done((f32[40,128]{1,0:T(8,128)S(1)}, f32[40,128]{1,0:T(8,128)S(1)}, u32[]{:S(2)}, u32[]{:S(2)}) %collective-permute-start.6) | collective-permute-done | bytes 20512 | tf_op jit(solution)/shard_map/ppermute | solution.py:557
  16.0 0.0 collective-permute-done.7.from_east
  16.0 1.2 %collective-permute-done.5.bulk_two = f32[384,128]{1,0:T(8,128)S(1)} collective-permute-done((f32[384,128]{1,0:T(8,128)S(1)}, f32[384,128]{1,0:T(8,128)S(1)}, u32[]{:S(2)}, u32[]{:S(2)}) %collective-permute-start.5) | collective-permute-done | bytes 196640 | tf_op jit(solution)/shard_map/ppermute | solution.py:550
  17.1 8.5 %shard_map.30 = f32[768,128]{1,0:T(8,128)} custom-call(f32[768,128]{1,0:T(8,128)S(1)} %bitcast.4, s32[8,128]{1,0:T(8,128)S(1)} %copy-done.1, f32[200,128]{1,0:T(8,128)S(1)} %get-tuple-element.22.south, f32[200,128]{1,0:T(8,128)S(1)} %get-tuple-element.23.north, f32[80,128]{1,0:T(8,128)S(1)} %get-tuple-element.24.cross_south, ...), custom_call_target="tpu_custom_call" | custom-call | tf_op jit(solution)/shard_map/pallas_call | solution.py:25
Async XLA Ops:
  0.0 1.0 %copy-start = (f32[1,6,16,8,128]{4,3,2,1,0:T(8,128)S(1)}, f32[1,6,16,8,128]{4,3,2,1,0:T(8,128)}, u32[]{:S(2)}) copy-start(f32[1,6,16,8,128]{4,3,2,1,0:T(8,128)} %param.2) | copy-start | bytes 1179652
  1.0 0.7 %copy-start.1 = (s32[8,128]{1,0:T(8,128)S(1)}, s32[8,128]{1,0:T(8,128)}, u32[]{:S(2)}) copy-start(s32[8,128]{1,0:T(8,128)} %levels.5) | copy-start | bytes 12292
  1.9 7.6 %collective-permute-start.4 = (f32[264,128]{1,0:T(8,128)S(1)}, f32[264,128]{1,0:T(8,128)S(1)}, u32[]{:S(2)}, u32[]{:S(2)}) collective-permute-start(f32[264,128]{1,0:T(8,128)S(1)} %get-tuple-element.21), channel_id=1, source_target_pairs={{0,16},{16,0},{1,17},{17,1},{2,18},{18,2},{3,19},{19,3},{4,20},{20... | collective-permute-start | bytes 405512 | tf_op jit(solution)/shard_map/ppermute | solution.py:550
  1.9 7.6 %collective-permute-start = (f32[200,128]{1,0:T(8,128)S(1)}, f32[200,128]{1,0:T(8,128)S(1)}, u32[]{:S(2)}, u32[]{:S(2)}) collective-permute-start(f32[200,128]{1,0:T(8,128)S(1)} %get-tuple-element.17), channel_id=1, source_target_pairs={{0,1},{1,0},{2,3},{3,2},{4,5},{5,4},{6,7},{7,6},{8,9},{9,8},{10,11... | collective-permute-start | bytes 307208 | tf_op jit(solution)/shard_map/ppermute | solution.py:537
  2.0 7.5 %collective-permute-start.1 = (f32[200,128]{1,0:T(8,128)S(1)}, f32[200,128]{1,0:T(8,128)S(1)}, u32[]{:S(2)}, u32[]{:S(2)}) collective-permute-start(f32[200,128]{1,0:T(8,128)S(1)} %get-tuple-element.18), channel_id=1, source_target_pairs={{0,3},{1,2},{2,1},{3,0},{4,7},{5,6},{6,5},{7,4},{8,11},{9,10},{10,... | collective-permute-start | bytes 307208 | tf_op jit(solution)/shard_map/ppermute | solution.py:537
  4.1 3.9 %collective-permute-start.2 = (f32[80,128]{1,0:T(8,128)S(1)}, f32[80,128]{1,0:T(8,128)S(1)}, u32[]{:S(2)}, u32[]{:S(2)}) collective-permute-start(f32[80,128]{1,0:T(8,128)S(1)} %get-tuple-element.19), channel_id=1, source_target_pairs={{0,17},{1,16},{2,19},{3,18},{4,21},{5,20},{6,23},{7,22},{8,25},{9,... | collective-permute-start | bytes 122888 | tf_op jit(solution)/shard_map/ppermute | solution.py:552
  5.2 4.3 %collective-permute-start.3 = (f32[80,128]{1,0:T(8,128)S(1)}, f32[80,128]{1,0:T(8,128)S(1)}, u32[]{:S(2)}, u32[]{:S(2)}) collective-permute-start(f32[80,128]{1,0:T(8,128)S(1)} %get-tuple-element.20), channel_id=1, source_target_pairs={{0,19},{1,18},{2,17},{3,16},{4,23},{5,22},{6,21},{7,20},{8,27},{9,... | collective-permute-start | bytes 122888 | tf_op jit(solution)/shard_map/ppermute | solution.py:552
  9.8 7.3 %collective-permute-start.5 = (f32[384,128]{1,0:T(8,128)S(1)}, f32[384,128]{1,0:T(8,128)S(1)}, u32[]{:S(2)}, u32[]{:S(2)}) collective-permute-start(f32[384,128]{1,0:T(8,128)S(1)} %get-tuple-element.26), channel_id=1, source_target_pairs={{0,16},{16,0},{1,17},{17,1},{2,18},{18,2},{3,19},{19,3},{4,20},{20... | collective-permute-start | bytes 589832 | tf_op jit(solution)/shard_map/ppermute | solution.py:550
  10.4 5.6 %collective-permute-start.6 = (f32[40,128]{1,0:T(8,128)S(1)}, f32[40,128]{1,0:T(8,128)S(1)}, u32[]{:S(2)}, u32[]{:S(2)}) collective-permute-start(f32[40,128]{1,0:T(8,128)S(1)} %get-tuple-element.27.own_east), channel_id=1, source_target_pairs={{0,4},{4,8},{8,12},{12,0},{1,5},{5,9},{9,13},{13,1},{2,6},{6,10},{... | collective-permute-start | bytes 61448 | tf_op jit(solution)/shard_map/ppermute | solution.py:557
  11.9 4.0 %collective-permute-start.7 = (f32[40,128]{1,0:T(8,128)S(1)}, f32[40,128]{1,0:T(8,128)S(1)}, u32[]{:S(2)}, u32[]{:S(2)}) collective-permute-start(f32[40,128]{1,0:T(8,128)S(1)} %get-tuple-element.28.own_west), channel_id=1, source_target_pairs={{0,12},{4,0},{8,4},{12,8},{1,13},{5,1},{9,5},{13,9},{2,14},{6,2},{... | collective-permute-start | bytes 61448 | tf_op jit(solution)/shard_map/ppermute | solution.py:557

commit v2 on v1

v2 whole, which is shorter than its diff:
```python
import functools
import jax
import jax.numpy as jnp
from jax import lax
from jax.experimental import pallas as pl
from jax.experimental.pallas import tpu as pltpu
from jax.sharding import PartitionSpec as P

NSUB = 2
TIME_STEP = 1.0
CORIOLIS = 0.3
THERMAL = 0.2
HALINE = 0.15
GRAVITY_SCALE = 0.05
MIX_BOOST = 4.0
RICHARDSON = 1.0

VMEM_LIMIT = 8 * 1024 * 1024

ZONAL_ROW, MERID_ROW, MERID_ROW2, TEMPER_ROW, VISC_ROW, LEVEL_ROW = range(6)


def call_kernel(body, outputs, inputs, scratch=()):
    in_vmem = pl.BlockSpec(memory_space=pltpu.VMEM)
    return pl.pallas_call(
        body,
        out_shape=[jax.ShapeDtypeStruct(shape, jnp.float32) for shape in outputs],
        in_specs=[in_vmem] * len(inputs),
        out_specs=[in_vmem] * len(outputs),
        scratch_shapes=[pltpu.VMEM(shape, jnp.float32) for shape in scratch],
        compiler_params=pltpu.CompilerParams(vmem_limit_bytes=VMEM_LIMIT),
    )(*inputs)


class Sizes:
    def __init__(self, fields, levels):
        self.nf, self.lev = fields.shape[1], fields.shape[2]
        self.rows, self.cols = levels.shape
        self.slab = self.lev * self.rows


def lane_ids(shape):
    return lax.broadcasted_iota(jnp.int32, shape, 1)


def row_ids(shape):
    return lax.broadcasted_iota(jnp.int32, shape, 0)


def turn(value, shift, axis):
    size = value.shape[axis]
    shift = shift % size
    return value if shift == 0 else pltpu.roll(value, shift, axis)


def to_lane(value, source, target):
    return turn(value, target - source, 1)


def level_rows(ref, first, row, sz):
    return ref[pl.ds(first + row, sz.lev, stride=sz.rows), :]


def send_north_first(sz, fill):
    even = lax.axis_index("lat") % 2 == 0
    top, second = sz.rows - 1, sz.rows - 2

    @pl.when(even)
    def _():
        fill(0, top, second)
        fill(1, 0, 1)

    @pl.when(jnp.logical_not(even))
    def _():
        fill(0, 0, 1)
        fill(1, top, second)


def pack_edges(sz, fields, row_a, row_b, side):
    def fill(which, near, far):
        message = (row_a, row_b)[which]
        for f in range(sz.nf):
            for r, row in enumerate((near, far)):
                at = (2 * f + r) * sz.lev
                message[at : at + sz.lev, :] = level_rows(fields, f * sz.slab, row, sz)

    send_north_first(sz, fill)
    for place, column in enumerate(edge_columns(sz, fields, sz.nf, 0)):
        side[place * sz.rows : (place + 1) * sz.rows, :] = column


def pack_cross(sz, fields, levels, cross_a, cross_b):
    lev = levels[...].astype(jnp.float32)

    def fill(which, near, far):
        cross = (cross_a, cross_b)[which]
        for at, (f, row) in enumerate(((0, near), (1, near), (1, far), (2, near), (4, near))):
            cross[at * sz.lev : (at + 1) * sz.lev, :] = level_rows(fields, f * sz.slab, row, sz)
        at = LEVEL_ROW * sz.lev
        cross[at : at + 1, :] = lev[near : near + 1, :]
        cross[at + 1 : at + 2, :] = lev[far : far + 1, :]
        cross[at + 2 : at + 8, :] = jnp.zeros((6, sz.cols), jnp.float32)

    send_north_first(sz, fill)


def edge_columns(sz, ref, count, first):
    tile = (sz.rows, sz.cols)
    lane = lane_ids(tile)
    zero = jnp.zeros(tile, jnp.float32)
    last = sz.cols - 1
    east_one, west_one, east_two, west_two = zero, zero, zero, zero
    for f in range(count):
        for k in range(sz.lev):
            at = f * sz.slab + k * sz.rows
            p = (first + f) * sz.lev + k
            moved = to_lane(ref[at : at + sz.rows, :], last, p)
            east_one = jnp.where(lane == p, moved, east_one)
            west_one = jnp.where(lane == (p + 1) % sz.cols, moved, west_one)
            west_two = jnp.where(lane == (p + 2) % sz.cols, moved, west_two)
            east_two = jnp.where(lane == (p - 1) % sz.cols, moved, east_two)
    return east_one, turn(west_one, -1, 1), turn(east_two, 1, 1), turn(west_two, -2, 1)


def pack_columns(
    sz, fields, levels, row_a, row_b, cross_a, cross_b, own_side, side,
    to_east, to_west, south, north, cross_south, cross_north, bulk,
):
    position = lax.axis_index("lat")
    even = position % 2 == 0
    has_south = position > 0
    has_north = position < lax.axis_size("lat") - 1
    for low, high, from_a, from_b in ((south, north, row_a, row_b), (cross_south, cross_north, cross_a, cross_b)):
        first, other = from_a[...], from_b[...]
        low[...] = jnp.where(has_south, jnp.where(even, other, first), 0.0)
        high[...] = jnp.where(has_north, jnp.where(even, first, other), 0.0)

    tile = (sz.rows, sz.cols)
    lane = lane_ids(tile)
    last = sz.cols - 1
    bulk[0 : 2 * sz.slab, :] = fields[0 : 2 * sz.slab, :]
    tracer_lanes = lane < sz.nf * sz.lev
    for place, (message, at) in enumerate(((to_east, 0), (to_west, 0), (to_east, sz.rows), (to_west, sz.rows))):
        own = own_side[place * sz.rows : (place + 1) * sz.rows, :]
        dynamics = side[place * sz.rows : (place + 1) * sz.rows, :]
        message[at : at + sz.rows, :] = jnp.where(tracer_lanes, own, turn(dynamics, sz.nf * sz.lev, 1))

    lev = levels[...].astype(jnp.float32)
    level_row = LEVEL_ROW * sz.lev
    south_lev = cross_south[level_row : level_row + 1, :]
    north_lev = cross_north[level_row : level_row + 1, :]
    base = 2 * sz.lev
    for place, (message, near, far) in enumerate(((to_east, last, last - 1), (to_west, 0, 1))):
        part = side[place * sz.rows : (place + 1) * sz.rows, :]
        part = jnp.where(lane < sz.lev, turn(part, -2 * sz.lev, 1), turn(part, -3 * sz.lev, 1))
        part = jnp.where(lane == base, to_lane(lev, near, base), part)
        part = jnp.where(lane == base + 1, to_lane(lev, far, base + 1), part)
        low = jnp.broadcast_to(to_lane(south_lev, near, base + 2), tile)
        high = jnp.broadcast_to(to_lane(north_lev, near, base + 3), tile)
        part = jnp.where(lane == base + 2, low, part)
        part = jnp.where(lane == base + 3, high, part)
        message[2 * sz.rows : 3 * sz.rows, :] = part

    tall = (sz.lev, sz.cols)
    tall_lane = lane_ids(tall)
    east_corner = jnp.zeros(tall, jnp.float32)
    west_corner = east_corner
    for r, (rows, cross) in enumerate(((south, cross_south), (north, cross_north))):
        for f in range(sz.nf + 2):
            if f < sz.nf:
                values = rows[2 * f * sz.lev : (2 * f + 1) * sz.lev, :]
            else:
                at = (ZONAL_ROW, MERID_ROW)[f - sz.nf] * sz.lev
                values = cross[at : at + sz.lev, :]
            p = r * (sz.nf + 2) + f
            moved = to_lane(values, last, p)
            east_corner = jnp.where(tall_lane == p, moved, east_corner)
            west_corner = jnp.where(tall_lane == p + 1, moved, west_corner)
    to_east[3 * sz.rows : 3 * sz.rows + sz.lev, :] = east_corner
    to_west[3 * sz.rows : 3 * sz.rows + sz.lev, :] = turn(west_corner, -1, 1)

    @pl.when(lax.axis_index("sect") == 0)
    def _():
        row = row_ids(tile)
        lev_e, lev_w = turn(lev, -1, 1), turn(lev, 1, 1)
        lev_n, lev_s = shift_north(lev, row, north_lev), shift_south(lev, row, south_lev)
        warm_above = None
        for k in range(sz.lev):
            at = k * sz.rows

            def around(f):
                value = fields[f * sz.slab + at : f * sz.slab + at + sz.rows, :]
                beyond = 2 * f * sz.lev + k
                return (
                    value, turn(value, -1, 1), turn(value, 1, 1),
                    shift_north(value, row, north[beyond : beyond + 1, :]),
                    shift_south(value, row, south[beyond : beyond + 1, :]),
                )

            wet = lev > k
            masks = wet, wet & (lev_e > k), wet & (lev_w > k), wet & (lev_n > k), wet & (lev_s > k)
            warm = diffused(around(2), around(4), masks)
            background = fields[5 * sz.slab + at : 5 * sz.slab + at + sz.rows, :]
            mixing = jnp.zeros(tile, jnp.float32) if k == 0 else mixed(warm_above, warm, background, wet)
            warm_above = warm
            bulk[2 * sz.slab + at : 2 * sz.slab + at + sz.rows, :] = mixing


def keep(mask, value):
    return jnp.where(mask, value, 0.0)


def diffused(quantity, viscosity, masks):
    mid, e, w, n, s = quantity
    visc, visc_e, visc_w, visc_n, visc_s = viscosity
    _, wet_e, wet_w, wet_n, wet_s = masks
    change = (
        keep(wet_e, 0.5 * (visc + visc_e)) * (e - mid)
        - keep(wet_w, 0.5 * (visc_w + visc)) * (mid - w)
        + keep(wet_n, 0.5 * (visc + visc_n)) * (n - mid)
        - keep(wet_s, 0.5 * (visc_s + visc)) * (mid - s)
    )
    return mid + TIME_STEP * change


def mixed(warm_above, warm, background, wet):
    jump = THERMAL * (warm_above - warm)
    return keep(wet, background * (1.0 + MIX_BOOST / (1.0 + RICHARDSON * jump * jump)))


def shift_west(value, lane, edge):
    return jnp.where(lane == 0, edge, turn(value, 1, 1))


def shift_east(value, lane, edge):
    return jnp.where(lane == value.shape[1] - 1, edge, turn(value, -1, 1))


def shift_south(value, row, edge):
    return jnp.where(row == 0, edge, turn(value, 1, 0))


def shift_north(value, row, edge):
    return jnp.where(row == value.shape[0] - 1, edge, turn(value, -1, 0))


class Weights:
    def __init__(self, east, west, north, south, step):
        self.own = 1.0 - step * (
            jnp.maximum(east, 0.0) - jnp.minimum(west, 0.0) + (jnp.maximum(north, 0.0) - jnp.minimum(south, 0.0))
        )
        self.east = -step * jnp.minimum(east, 0.0)
        self.west = step * jnp.maximum(west, 0.0)
        self.north = -step * jnp.minimum(north, 0.0)
        self.south = step * jnp.maximum(south, 0.0)

    def parts(self):
        return self.own, self.east, self.west, self.north, self.south

    @classmethod
    def of(cls, own, east, west, north, south):
        weights = cls.__new__(cls)
        weights.own, weights.east, weights.west, weights.north, weights.south = own, east, west, north, south
        return weights

    def apply(self, own, east, west, north, south):
        return self.own * own + self.east * east + self.west * west + (self.north * north + self.south * south)


def finish(
    sz, fields, levels, south, north, cross_south, cross_north, bulk,
    own_east, own_west, side, from_west, from_east,
    out, div, mix, vert, low_strip, high_strip, side_strips, ratio, forward, inv_ref, wref, pull, moved,
):
    tile = (sz.rows, sz.cols)
    lane, row = lane_ids(tile), row_ids(tile)
    last_lane, last_row = sz.cols - 1, sz.rows - 1
    lev = levels[...].astype(jnp.float32)
    level_row = LEVEL_ROW * sz.lev
    side_base = 2 * sz.lev
    west_side = from_west[2 * sz.rows : 3 * sz.rows, :]
    east_side = from_east[2 * sz.rows : 3 * sz.rows, :]
    lev_w = shift_west(lev, lane, to_lane(west_side, side_base, 0))
    lev_e = shift_east(lev, lane, to_lane(east_side, side_base, last_lane))
    south_lev, north_lev = cross_south[level_row : level_row + 1, :], cross_north[level_row : level_row + 1, :]
    lev_s = shift_south(lev, row, south_lev)
    lev_n = shift_north(lev, row, north_lev)

    def masks(k):
        wet = lev > k
        return wet, wet & (lev_e > k), wet & (lev_w > k), wet & (lev_n > k), wet & (lev_s > k)

    is_dynamics = lax.axis_index("sect") == 0

    def physics():
        def around(f, k):
            at = f * sz.slab + k * sz.rows
            value = fields[at : at + sz.rows, :]
            lane_at, beyond = f * sz.lev + k, 2 * f * sz.lev + k
            return (
                value,
                shift_east(value, lane, to_lane(from_east[0 : sz.rows, :], lane_at, last_lane)),
                shift_west(value, lane, to_lane(from_west[0 : sz.rows, :], lane_at, 0)),
                shift_north(value, row, north[beyond : beyond + 1, :]),
                shift_south(value, row, south[beyond : beyond + 1, :]),
            )

        press = jnp.zeros(tile, jnp.float32)
        press_e, press_n, warm_above = press, press, press
        for k in range(sz.lev):
            at = k * sz.rows
            mask = masks(k)
            wet, wet_e, wet_w, wet_n, wet_s = mask
            zonal, merid, temper, saline, visc = (around(f, k) for f in range(5))
            flow_east, flow_west = keep(wet_e, zonal[0]), keep(wet_w, zonal[2])
            flow_north, flow_south = keep(wet_n, merid[0]), keep(wet_s, merid[4])
            div[at : at + sz.rows, :] = flow_east - flow_west + (flow_north - flow_south)
            warm = diffused(temper, visc, mask)
            mixing = jnp.zeros(tile, jnp.float32)
            if k > 0:
                background = fields[5 * sz.slab + at : 5 * sz.slab + at + sz.rows, :]
                mixing = mixed(warm_above, warm, background, wet)
            warm_above = warm

            def weight(place, wet_there):
                return keep(wet_there, HALINE * saline[place] - THERMAL * temper[place])

            press = press + GRAVITY_SCALE * weight(0, wet)
            press_e = press_e + GRAVITY_SCALE * weight(1, lev_e > k)
            press_n = press_n + GRAVITY_SCALE * weight(3, lev_n > k)
            zonal_new = diffused(zonal, visc, mask) + TIME_STEP * (CORIOLIS * merid[0] - (press_e - press))
            merid_new = diffused(merid, visc, mask) - TIME_STEP * (CORIOLIS * zonal[0] + (press_n - press))
            saline_new = diffused(saline, visc, mask)
            parts = (keep(wet_e, zonal_new), keep(wet_n, merid_new), warm, saline_new, None, mixing)
            for f, part in enumerate(parts):
                if part is not None:
                    out[f * sz.slab + at : f * sz.slab + at + sz.rows, :] = part
        total = jnp.zeros(tile, jnp.float32)
        for k in range(sz.lev - 1, -1, -1):
            at = k * sz.rows
            total = total + div[at : at + sz.rows, :]
            out[4 * sz.slab + at : 4 * sz.slab + at + sz.rows, :] = -total if k > 0 else jnp.zeros(tile, jnp.float32)

    def column(value, at):
        return jnp.broadcast_to(value[:, at : at + 1], value.shape)

    def both(west, east):
        return jnp.concatenate([west, east], axis=0)

    tall = (sz.lev, sz.cols)
    pair_row = row_ids((2 * sz.rows, sz.cols)) % sz.rows
    pair_lane = lane_ids((2 * sz.rows, sz.cols))

    def pair_south(value, edge):
        return jnp.where(pair_row == 0, edge, turn(value, 1, 0))

    def pair_north(value, edge):
        return jnp.where(pair_row == last_row, edge, turn(value, -1, 0))

    def edge_mixing():
        diagonal = lane_ids(tall) == row_ids(tall)

        def levels_in_lanes(rows, at):
            return jnp.broadcast_to(jnp.sum(keep(diagonal, column(rows, at)), axis=0, keepdims=True), tile)

        def place(index):
            return side[index * sz.rows : (index + 1) * sz.rows, :]

        own_pair, inner_w, inner_e = both(place(1), place(0)), place(3), place(2)

        def around(f, message_lane, cross_row):
            shift = -f * sz.lev
            outer_w, outer_e = turn(west_side, -message_lane, 1), turn(east_side, -message_lane, 1)
            own = turn(own_pair, shift, 1)
            low, high = (
                cross[cross_row * sz.lev : (cross_row + 1) * sz.lev, :] for cross in (cross_south, cross_north)
            )
            return (
                own,
                both(turn(inner_w, shift, 1), outer_e),
                both(outer_w, turn(inner_e, shift, 1)),
                pair_north(own, both(levels_in_lanes(high, 0), levels_in_lanes(high, last_lane))),
                pair_south(own, both(levels_in_lanes(low, 0), levels_in_lanes(low, last_lane))),
            )

        depth = pair_lane.astype(jnp.float32)

        def wet(value):
            return both(column(value, 0), column(value, last_lane)) > depth

        mid = wet(lev)
        mask = mid, mid & wet(lev_e), mid & wet(lev_w), mid & wet(lev_n), mid & wet(lev_s)
        warm = diffused(around(2, 0, TEMPER_ROW), around(4, sz.lev, VISC_ROW), mask)
        background = turn(own_pair, -5 * sz.lev, 1)
        return jnp.where(pair_lane == 0, 0.0, mixed(turn(warm, 1, 1), warm, background, mid))

    def row_strips(step):
        lane16, depth = lane_ids(tall), row_ids(tall).astype(jnp.float32)

        def wet(levels_row):
            return levels_row > depth

        west_corner = from_west[3 * sz.rows : 3 * sz.rows + sz.lev, :]
        east_corner = from_east[3 * sz.rows : 3 * sz.rows + sz.lev, :]
        lane1 = lane_ids((1, sz.cols))
        for r in range(2):
            rows, cross = (south, cross_south) if r == 0 else (north, cross_north)
            strip = low_strip if r == 0 else high_strip
            edge = 0 if r == 0 else last_row
            near_lev = cross[level_row : level_row + 1, :]
            far_lev = cross[level_row + 1 : level_row + 2, :]
            own_lev = lev[edge : edge + 1, :]
            corner_lane = side_base + 2 + r
            lev_at_w = shift_west(near_lev, lane1, to_lane(west_side[0:1, :], corner_lane, 0))
            lev_at_e = shift_east(near_lev, lane1, to_lane(east_side[0:1, :], corner_lane, last_lane))
            wet_near = wet(near_lev)
            zonal = cross[ZONAL_ROW * sz.lev : (ZONAL_ROW + 1) * sz.lev, :]
            p = r * (sz.nf + 2)
            zonal_w = shift_west(zonal, lane16, to_lane(west_corner, p + sz.nf, 0))
            flow_e = keep(wet_near & wet(lev_at_e), zonal)
            flow_w = keep(wet_near & wet(lev_at_w), zonal_w)
            merid = cross[MERID_ROW * sz.lev : (MERID_ROW + 1) * sz.lev, :]
            if r == 0:
                merid_far = cross[MERID_ROW2 * sz.lev : (MERID_ROW2 + 1) * sz.lev, :]
                flow_n = keep(wet_near & wet(own_lev), merid)
                flow_s = keep(wet_near & wet(far_lev), merid_far)
            else:
                flow_n = keep(wet_near & wet(far_lev), merid)
                flow_s = keep(wet_near & wet(own_lev), level_rows(bulk, sz.slab, last_row, sz))
            weights = Weights(flow_e, flow_w, flow_n, flow_s, step)
            for f in range(sz.nf):
                at = 2 * f * sz.lev
                near, far = rows[at : at + sz.lev, :], rows[at + sz.lev : at + 2 * sz.lev, :]
                inside = level_rows(fields, f * sz.slab, edge, sz)
                at_w = shift_west(near, lane16, to_lane(west_corner, p + f, 0))
                at_e = shift_east(near, lane16, to_lane(east_corner, p + f, last_lane))
                up, down = (inside, far) if r == 0 else (far, inside)
                strip[f * sz.lev : (f + 1) * sz.lev, :] = weights.apply(near, at_e, at_w, up, down)

    def column_strips(step):
        lane16, depth16 = lane_ids(tall), row_ids(tall)

        def all_fields(value, first):
            at = lane_ids(value.shape)
            value = jnp.where((at >= first) & (at < first + sz.lev), value, 0.0)
            width = sz.lev
            while width < sz.cols:
                value = value + turn(value, width, 1)
                width *= 2
            return value

        def corner_rows(message, r):
            items = message[3 * sz.rows : 3 * sz.rows + sz.lev, :]
            p = r * (sz.nf + 2)
            tracers = jnp.zeros(tall, jnp.float32)
            for f in range(sz.nf):
                spread = jnp.broadcast_to(items[:, p + f : p + f + 1], tall)
                tracers = jnp.where(lane16 == f * sz.lev + depth16, spread, tracers)
            spread = jnp.broadcast_to(items[:, p + sz.nf + 1 : p + sz.nf + 2], tall)
            velocity = jnp.where(lane16 % sz.lev == depth16, spread, 0.0)
            return jnp.sum(tracers, axis=0, keepdims=True), jnp.sum(velocity, axis=0, keepdims=True)

        inside_w, inside_e = own_west[0 : sz.rows, :], own_east[0 : sz.rows, :]
        near = both(from_west[0 : sz.rows, :], from_east[0 : sz.rows, :])
        far_w, far_e = from_west[sz.rows : 2 * sz.rows, :], from_east[sz.rows : 2 * sz.rows, :]
        corners = [corner_rows(message, r) for message in (from_west, from_east) for r in range(2)]
        low_tracers, high_tracers, low_merid = (
            both(jnp.broadcast_to(corners[i][part], tile), jnp.broadcast_to(corners[i + 2][part], tile))
            for i, part in ((0, 0), (1, 0), (0, 1))
        )

        def side_levels(at):
            return column(west_side, at), column(east_side, at)

        near_lev = both(*side_levels(side_base))
        far_lev_w, far_lev_e = side_levels(side_base + 1)
        own_lev_w, own_lev_e = column(lev, 0), column(lev, last_lane)
        lev_at_s = pair_south(near_lev, both(*side_levels(side_base + 2)))
        lev_at_n = pair_north(near_lev, both(*side_levels(side_base + 3)))
        depth = (lane_ids(near.shape) % sz.lev).astype(jnp.float32)
        wet_near = near_lev > depth
        zonal_first = sz.nf * sz.lev
        west, east = both(far_w, inside_e), both(inside_w, far_e)
        flow_e = keep(wet_near & (both(own_lev_w, far_lev_e) > depth), all_fields(near, zonal_first))
        flow_w = keep(wet_near & (both(far_lev_w, own_lev_e) > depth), all_fields(west, zonal_first))
        merid = all_fields(near, zonal_first + sz.lev)
        flow_n = keep(wet_near & (lev_at_n > depth), merid)
        flow_s = keep(wet_near & (lev_at_s > depth), pair_south(merid, low_merid))
        weights = Weights(flow_e, flow_w, flow_n, flow_s, step)
        side_strips[...] = weights.apply(near, east, west, pair_north(near, high_tracers), pair_south(near, low_tracers))

    def transport(step):
        west_old, east_old = from_west[0 : sz.rows, :], from_east[0 : sz.rows, :]
        zero = jnp.zeros(tile, jnp.float32)

        def faces(k):
            if k == sz.lev:
                return zero, zero
            at = k * sz.rows
            speed, mixing = vert[at : at + sz.rows, :], mix[at : at + sz.rows, :]
            return jnp.maximum(speed, 0.0) + mixing, jnp.minimum(speed, 0.0) - mixing

        every = range(sz.nf)

        def stored_weights(k):
            at = k * sz.rows
            return Weights.of(*(wref[i * sz.slab + at : i * sz.slab + at + sz.rows, :] for i in range(5)))

        def substep(weights, values, k, west, east, lows, highs):
            to_e = [turn(value, -1, 1) for value in values]
            to_w = [turn(value, 1, 1) for value in values]
            edge_e = [to_lane(east, f * sz.lev + k, last_lane) for f in every]
            edge_w = [to_lane(west, f * sz.lev + k, 0) for f in every]
            return [
                weights.apply(
                    values[f],
                    jnp.where(lane == last_lane, edge_e[f], to_e[f]),
                    jnp.where(lane == 0, edge_w[f], to_w[f]),
                    shift_north(values[f], row, highs[f]),
                    shift_south(values[f], row, lows[f]),
                )
                for f in every
            ]

        for k in range(sz.lev):
            at = k * sz.rows
            wet, wet_e, wet_w, wet_n, wet_s = masks(k)
            zonal, merid = bulk[at : at + sz.rows, :], bulk[sz.slab + at : sz.slab + at + sz.rows, :]
            zonal_first = sz.nf * sz.lev
            zonal_west = shift_west(zonal, lane, to_lane(west_old, zonal_first + k, 0))
            beyond = MERID_ROW * sz.lev + k
            merid_south = shift_south(merid, row, cross_south[beyond : beyond + 1, :])
            flow_e, flow_w, flow_n, flow_s = (
                keep(wet_e, zonal), keep(wet_w, zonal_west), keep(wet_n, merid), keep(wet_s, merid_south)
            )
            div[at : at + sz.rows, :] = flow_e - flow_w + (flow_n - flow_s)
            weights = Weights(flow_e, flow_w, flow_n, flow_s, step)
            for i, part in enumerate(weights.parts()):
                wref[i * sz.slab + at : i * sz.slab + at + sz.rows, :] = part
        column_strips(step)
        row_strips(step)
        west_new, east_new = side_strips[0 : sz.rows, :], side_strips[sz.rows : 2 * sz.rows, :]
        for k in range(sz.lev):
            at = k * sz.rows
            weights = stored_weights(k)
            values = [fields[f * sz.slab + at : f * sz.slab + at + sz.rows, :] for f in every]
            lows = [south[2 * f * sz.lev + k : 2 * f * sz.lev + k + 1, :] for f in every]
            highs = [north[2 * f * sz.lev + k : 2 * f * sz.lev + k + 1, :] for f in every]
            values = substep(weights, values, k, west_old, east_old, lows, highs)
            for f in every:
                forward[f * sz.slab + at : f * sz.slab + at + sz.rows, :] = values[f]
        edges = edge_mixing()
        edge_w, edge_e = edges[0 : sz.rows, :], edges[sz.rows : 2 * sz.rows, :]
        total = zero
        for k in range(sz.lev - 1, -1, -1):
            at = k * sz.rows
            total = total + div[at : at + sz.rows, :]
            vert[at : at + sz.rows, :] = -total if k > 0 else zero
            mixing = bulk[2 * sz.slab + at : 2 * sz.slab + at + sz.rows, :]
            mixing = jnp.where(lane == 0, to_lane(edge_w, k, 0), mixing)
            mix[at : at + sz.rows, :] = jnp.where(lane == last_lane, to_lane(edge_e, k, last_lane), mixing)
        last_ratio = None
        up, down = faces(0)
        lower, inverse = [], []
        for k in range(sz.lev):
            at = k * sz.rows
            up_next, down_next = faces(k + 1)
            pivot = 1.0 + TIME_STEP * (up - down_next)
            lower.append(TIME_STEP * down)
            if k > 0:
                pivot = pivot - lower[k] * last_ratio
            inverse.append(1.0 / pivot)
            last_ratio = -TIME_STEP * up_next * inverse[k]
            ratio[at : at + sz.rows, :] = last_ratio
            inv_ref[at : at + sz.rows, :] = inverse[k]
            pull[at : at + sz.rows, :] = lower[k] * inverse[k]
            up, down = up_next, down_next
        previous = [None] * sz.nf
        for k in range(sz.lev):
            at = k * sz.rows
            weights = stored_weights(k)
            values = [forward[f * sz.slab + at : f * sz.slab + at + sz.rows, :] for f in every]
            lows = [low_strip[f * sz.lev + k : f * sz.lev + k + 1, :] for f in every]
            highs = [high_strip[f * sz.lev + k : f * sz.lev + k + 1, :] for f in every]
            values = substep(weights, values, k, west_new, east_new, lows, highs)
            for f in every:
                moved[f * sz.slab + at : f * sz.slab + at + sz.rows, :] = values[f] * inv_ref[at : at + sz.rows, :]
        for k in range(sz.lev):
            at = k * sz.rows
            for f in every:
                here = f * sz.slab + at
                value = moved[here : here + sz.rows, :]
                if k > 0:
                    value = value - pull[at : at + sz.rows, :] * previous[f]
                forward[here : here + sz.rows, :] = value
                previous[f] = value
        for k in range(sz.lev - 1, -1, -1):
            at = k * sz.rows
            wet = lev > k
            for f in range(sz.nf):
                here = f * sz.slab + at
                if k < sz.lev - 1:
                    previous[f] = forward[here : here + sz.rows, :] - ratio[at : at + sz.rows, :] * previous[f]
                out[here : here + sz.rows, :] = keep(wet, previous[f])

    @pl.when(is_dynamics)
    def _():
        physics()

    @pl.when(jnp.logical_not(is_dynamics))
    def _():
        transport(TIME_STEP / NSUB)


def pair_of(index, count, odd):
    if not odd:
        return index ^ 1
    return (((index + 1) ^ 1) - 1) % count


def on_device(sizes_of, fields, levels):
    sz = Sizes(fields, levels)
    count_s, count_o, count_a = sizes_of
    flat = fields.reshape(sz.nf * sz.slab, sz.cols)
    axes = ("sect", "lon", "lat")

    def swap(value, odd):
        pairs = [(i, pair_of(i, count_a, odd)) for i in range(count_a)]
        return lax.ppermute(value, "lat", pairs)

    def from_dynamics(value, odd=None):
        mine = lax.axis_index("sect")
        got = None
        for hop in range(1, count_s):
            pairs = []
            for s in range(count_s):
                for o in range(count_o):
                    for a in range(count_a):
                        b = a if odd is None else pair_of(a, count_a, odd)
                        pairs.append(((s * count_o + o) * count_a + a, (((s + hop) % count_s) * count_o + o) * count_a + b))
            if odd is None:
                part = lax.ppermute(value, "sect", [(s, (s + hop) % count_s) for s in range(count_s)])
            else:
                part = lax.ppermute(value, axes, pairs)
            got = part if got is None else jnp.where(mine == hop, part, got)
        return got

    def around(value, step):
        return lax.ppermute(value, "lon", [(i, (i + step) % count_o) for i in range(count_o)])

    rows_shape = (2 * sz.nf * sz.lev, sz.cols)
    cross_shape = (LEVEL_ROW * sz.lev + 8, sz.cols)
    columns_shape = (3 * sz.rows + sz.lev, sz.cols)
    side_shape = (4 * sz.rows, sz.cols)
    row_a, row_b, own_side = call_kernel(functools.partial(pack_edges, sz), [rows_shape, rows_shape, side_shape], [flat])
    cross_a, cross_b = call_kernel(functools.partial(pack_cross, sz), [cross_shape, cross_shape], [flat, levels])
    side = from_dynamics(own_side)
    cross_b = from_dynamics(cross_b, True)
    row_b = swap(row_b, True)
    cross_a = from_dynamics(cross_a, False)
    row_a = swap(row_a, False)
    to_east, to_west, south, north, cross_south, cross_north, bulk = call_kernel(
        functools.partial(pack_columns, sz),
        [columns_shape] * 2 + [rows_shape] * 2 + [cross_shape] * 2 + [(3 * sz.slab, sz.cols)],
        [flat, levels, row_a, row_b, cross_a, cross_b, own_side, side],
    )
    bulk = from_dynamics(bulk)
    from_east = around(to_west, -1)
    from_west = around(to_east, 1)
    slab = (sz.slab, sz.cols)
    (out,) = call_kernel(
        functools.partial(finish, sz),
        [flat.shape],
        [flat, levels, south, north, cross_south, cross_north, bulk, to_east, to_west, side, from_west, from_east],
        [slab, slab, slab, (sz.nf * sz.lev, sz.cols), (sz.nf * sz.lev, sz.cols), (2 * sz.rows, sz.cols), slab, flat.shape, slab, (5 * sz.slab, sz.cols), slab, flat.shape],
    )
    return out.reshape(fields.shape)


def solution(mesh):
    sizes_of = (mesh.shape["sect"], mesh.shape["lon"], mesh.shape["lat"])
    return jax.shard_map(
        functools.partial(on_device, sizes_of),
        mesh=mesh,
        in_specs=(P("sect", None, None, "lat", "lon"), P("lat", "lon")),
        out_specs=P("sect", None, None, "lat", "lon"),
        check_vma=False,
    )
```

time: 25.8 us -> 19.1 us (0.74)
  the two profiles are of different devices: /device:TPU:2 before, /device:TPU:0 now
where the time goes in v2:
time: 19.1 us; the launch traced here: 19 us
  starting transfers between devices  11.4 us (60%)
  waiting for transfers between devices  4.6 us (24%)
  Pallas kernels  1.88 us (10%)
  local copies, waits for them, and re-layouts  1 us (5%)
    ppermute x2, starting transfers between devices, around(): lax.ppermute(value, 'lon', [(i, (i + step) % count_o) for i in range(coun...  3.82 us
    ppermute x2, starting transfers between devices, swap(): return lax.ppermute(value, 'lat', pairs)  3.1 us
    ppermute x2, starting transfers between devices, from_dynamics(): lax.ppermute(value, 'sect', [(s, (s + hop) % count_s) for s in range(coun...  3 us
    ppermute x2, waiting for transfers between devices, from_dynamics(): lax.ppermute(value, 'sect', [(s, (s + hop) % count_s) for s in range(coun...  2.61 us
    pallas_call x4, Pallas kernels, call_kernel(): pl.pallas_call(body, out_shape=[jax.ShapeDtypeStruct(shape, jnp.float32)...  1.88 us
    ppermute x2, waiting for transfers between devices, around(): lax.ppermute(value, 'lon', [(i, (i + step) % count_o) for i in range(coun...  1.87 us
    ppermute x2, starting transfers between devices, from_dynamics(): part = lax.ppermute(value, axes, pairs)  1.52 us
    unnamed x4, local copies, waits for them, and re-layouts  1 us
  transfers between devices with their start and end apart: 8, of which 4 were waited for; matrix products, arithmetic and copies ran while one was open for 0% of the time, Pallas kernels for 0%

profile of v2, /device:TPU:0, one launch (start us, length us, event | category | flops | bytes accessed | tf_op | source)
XLA Modules:
  0.0 19.0 jit_solution(1019838161499349461)
XLA Ops:
  0.0 0.0 copy-start
  0.0 1.0 %copy-done = f32[1,6,16,8,128]{4,3,2,1,0:T(8,128)S(1)} copy-done((f32[1,6,16,8,128]{4,3,2,1,0:T(8,128)S(1)}, f32[1,6,16,8,128]{4,3,2,1,0:T(8,128)}, u32[]{:S(2)}) %copy-start) | copy-done | bytes 393240
  1.0 0.0 copy-start.1
  1.0 0.3 %shard_map.28 = (f32[192,128]{1,0:T(8,128)S(1)}, f32[192,128]{1,0:T(8,128)S(1)}, f32[32,128]{1,0:T(8,128)S(1)}) custom-call(f32[768,128]{1,0:T(8,128)S(1)} %bitcast.2), custom_call_target="tpu_custom_call" | custom-call | tf_op jit(solution)/shard_map/pallas_call | solution.py:25
  1.3 0.5 %collective-permute-start = (f32[192,128]{1,0:T(8,128)S(1)}, f32[192,128]{1,0:T(8,128)S(1)}, u32[]{:S(2)}, u32[]{:S(2)}) collective-permute-start(f32[192,128]{1,0:T(8,128)S(1)} %get-tuple-element.17), channel_id=1, source_target_pairs={{0,1},{1,0},{2,3},{3,2},{4,5},{5,4},{6,7},{7,6},{8,9},{9,8},{10,11... | collective-permute-start | bytes 294920 | tf_op jit(solution)/shard_map/ppermute | solution.py:629
  1.7 2.6 %collective-permute-start.1 = (f32[192,128]{1,0:T(8,128)S(1)}, f32[192,128]{1,0:T(8,128)S(1)}, u32[]{:S(2)}, u32[]{:S(2)}) collective-permute-start(f32[192,128]{1,0:T(8,128)S(1)} %get-tuple-element.18), channel_id=1, source_target_pairs={{0,3},{1,2},{2,1},{3,0},{4,7},{5,6},{6,5},{7,4},{8,11},{9,10},{10,... | collective-permute-start | bytes 294920 | tf_op jit(solution)/shard_map/ppermute | solution.py:629
  4.4 0.0 copy-done.1
  4.4 1.2 %collective-permute-start.2 = (f32[88,128]{1,0:T(8,128)S(1)}, f32[88,128]{1,0:T(8,128)S(1)}, u32[]{:S(2)}, u32[]{:S(2)}) collective-permute-start(f32[88,128]{1,0:T(8,128)S(1)} %get-tuple-element.19), channel_id=1, source_target_pairs={{0,17},{1,16},{2,19},{3,18},{4,21},{5,20},{6,23},{7,22},{8,25},{9,... | collective-permute-start | bytes 135176 | tf_op jit(solution)/shard_map/ppermute | solution.py:644
  5.6 0.3 %collective-permute-start.3 = (f32[88,128]{1,0:T(8,128)S(1)}, f32[88,128]{1,0:T(8,128)S(1)}, u32[]{:S(2)}, u32[]{:S(2)}) collective-permute-start(f32[88,128]{1,0:T(8,128)S(1)} %get-tuple-element.20), channel_id=1, source_target_pairs={{0,19},{1,18},{2,17},{3,16},{4,23},{5,22},{6,21},{7,20},{8,27},{9,... | collective-permute-start | bytes 135176 | tf_op jit(solution)/shard_map/ppermute | solution.py:644
  5.9 1.7 %collective-permute-start.4 = (f32[32,128]{1,0:T(8,128)S(1)}, f32[32,128]{1,0:T(8,128)S(1)}, u32[]{:S(2)}, u32[]{:S(2)}) collective-permute-start(f32[32,128]{1,0:T(8,128)S(1)} %get-tuple-element.21.own_side), channel_id=1, source_target_pairs={{0,16},{16,0},{1,17},{17,1},{2,18},{18,2},{3,19},{19,3},{4,20},{20... | collective-permute-start | bytes 49160 | tf_op jit(solution)/shard_map/ppermute | solution.py:642
  7.7 2.2 %collective-permute-done.4.side = f32[32,128]{1,0:T(8,128)S(1)} collective-permute-done((f32[32,128]{1,0:T(8,128)S(1)}, f32[32,128]{1,0:T(8,128)S(1)}, u32[]{:S(2)}, u32[]{:S(2)}) %collective-permute-start.4) | collective-permute-done | bytes 16416 | tf_op jit(solution)/shard_map/ppermute | solution.py:642
  9.9 0.0 collective-permute-done.2.cross_a
  9.9 0.1 collective-permute-done.3.cross_b
  10.0 0.0 collective-permute-done.row_a
  10.0 0.0 collective-permute-done.1.row_b
  10.0 0.3 %shard_map.30 = (f32[40,128]{1,0:T(8,128)S(1)}, f32[40,128]{1,0:T(8,128)S(1)}, f32[192,128]{1,0:T(8,128)S(1)}, f32[192,128]{1,0:T(8,128)S(1)}, f32[88,128]{1,0:T...) custom-call(f32[768,128]{1,0:T(8,128)S(1)} %bitcast.4, s32[8,128]{1,0:T(8,128)S(1)} %copy-done.1, ...), custom_call_target="tpu_custom_call" | custom-call | tf_op jit(solution)/shard_map/pallas_call | solution.py:25
  10.4 1.3 %collective-permute-start.5 = (f32[384,128]{1,0:T(8,128)S(1)}, f32[384,128]{1,0:T(8,128)S(1)}, u32[]{:S(2)}, u32[]{:S(2)}) collective-permute-start(f32[384,128]{1,0:T(8,128)S(1)} %get-tuple-element.26), channel_id=1, source_target_pairs={{0,16},{16,0},{1,17},{17,1},{2,18},{18,2},{3,19},{19,3},{4,20},{20... | collective-permute-start | bytes 589832 | tf_op jit(solution)/shard_map/ppermute | solution.py:642
  11.6 1.6 %collective-permute-start.6 = (f32[40,128]{1,0:T(8,128)S(1)}, f32[40,128]{1,0:T(8,128)S(1)}, u32[]{:S(2)}, u32[]{:S(2)}) collective-permute-start(f32[40,128]{1,0:T(8,128)S(1)} %get-tuple-element.27.own_east), channel_id=1, source_target_pairs={{0,4},{4,8},{8,12},{12,0},{1,5},{5,9},{9,13},{13,1},{2,6},{6,10},{... | collective-permute-start | bytes 61448 | tf_op jit(solution)/shard_map/ppermute | solution.py:649
  13.2 2.2 %collective-permute-start.7 = (f32[40,128]{1,0:T(8,128)S(1)}, f32[40,128]{1,0:T(8,128)S(1)}, u32[]{:S(2)}, u32[]{:S(2)}) collective-permute-start(f32[40,128]{1,0:T(8,128)S(1)} %get-tuple-element.28.own_west), channel_id=1, source_target_pairs={{0,12},{4,0},{8,4},{12,8},{1,13},{5,1},{9,5},{13,9},{2,14},{6,2},{... | collective-permute-start | bytes 61448 | tf_op jit(solution)/shard_map/ppermute | solution.py:649
  15.5 1.9 %collective-permute-done.6.from_west = f32[40,128]{1,0:T(8,128)S(1)} collective-permute-done((f32[40,128]{1,0:T(8,128)S(1)}, f32[40,128]{1,0:T(8,128)S(1)}, u32[]{:S(2)}, u32[]{:S(2)}) %collective-permute-start.6) | collective-permute-done | bytes 20512 | tf_op jit(solution)/shard_map/ppermute | solution.py:649
  17.3 0.0 collective-permute-done.7.from_east
  17.3 0.4 %collective-permute-done.5.bulk = f32[384,128]{1,0:T(8,128)S(1)} collective-permute-done((f32[384,128]{1,0:T(8,128)S(1)}, f32[384,128]{1,0:T(8,128)S(1)}, u32[]{:S(2)}, u32[]{:S(2)}) %collective-permute-start.5) | collective-permute-done | bytes 196640 | tf_op jit(solution)/shard_map/ppermute | solution.py:642
  17.7 1.2 %shard_map.31 = f32[768,128]{1,0:T(8,128)} custom-call(f32[768,128]{1,0:T(8,128)S(1)} %bitcast.5, s32[8,128]{1,0:T(8,128)S(1)} %copy-done.1, f32[192,128]{1,0:T(8,128)S(1)} %get-tuple-element.22.south, f32[192,128]{1,0:T(8,128)S(1)} %get-tuple-element.23.north, f32[88,128]{1,0:T(8,128)S(1)} %get-tuple-element.24.cross_south, ...), custom_call_target="tpu_custom_call" | custom-call | tf_op jit(solution)/shard_map/pallas_call | solution.py:25
  (1 shorter events, 0.0 us)
Async XLA Ops:
  0.0 1.0 %copy-start = (f32[1,6,16,8,128]{4,3,2,1,0:T(8,128)S(1)}, f32[1,6,16,8,128]{4,3,2,1,0:T(8,128)}, u32[]{:S(2)}) copy-start(f32[1,6,16,8,128]{4,3,2,1,0:T(8,128)} %param.2) | copy-start | bytes 1179652
  1.0 3.4 %copy-start.1 = (s32[8,128]{1,0:T(8,128)S(1)}, s32[8,128]{1,0:T(8,128)}, u32[]{:S(2)}) copy-start(s32[8,128]{1,0:T(8,128)} %levels.5) | copy-start | bytes 12292
  1.3 8.7 %collective-permute-start = (f32[192,128]{1,0:T(8,128)S(1)}, f32[192,128]{1,0:T(8,128)S(1)}, u32[]{:S(2)}, u32[]{:S(2)}) collective-permute-start(f32[192,128]{1,0:T(8,128)S(1)} %get-tuple-element.17), channel_id=1, source_target_pairs={{0,1},{1,0},{2,3},{3,2},{4,5},{5,4},{6,7},{7,6},{8,9},{9,8},{10,11... | collective-permute-start | bytes 294920 | tf_op jit(solution)/shard_map/ppermute | solution.py:629
  1.7 8.3 %collective-permute-start.1 = (f32[192,128]{1,0:T(8,128)S(1)}, f32[192,128]{1,0:T(8,128)S(1)}, u32[]{:S(2)}, u32[]{:S(2)}) collective-permute-start(f32[192,128]{1,0:T(8,128)S(1)} %get-tuple-element.18), channel_id=1, source_target_pairs={{0,3},{1,2},{2,1},{3,0},{4,7},{5,6},{6,5},{7,4},{8,11},{9,10},{10,... | collective-permute-start | bytes 294920 | tf_op jit(solution)/shard_map/ppermute | solution.py:629
  4.4 5.5 %collective-permute-start.2 = (f32[88,128]{1,0:T(8,128)S(1)}, f32[88,128]{1,0:T(8,128)S(1)}, u32[]{:S(2)}, u32[]{:S(2)}) collective-permute-start(f32[88,128]{1,0:T(8,128)S(1)} %get-tuple-element.19), channel_id=1, source_target_pairs={{0,17},{1,16},{2,19},{3,18},{4,21},{5,20},{6,23},{7,22},{8,25},{9,... | collective-permute-start | bytes 135176 | tf_op jit(solution)/shard_map/ppermute | solution.py:644
  5.6 4.4 %collective-permute-start.3 = (f32[88,128]{1,0:T(8,128)S(1)}, f32[88,128]{1,0:T(8,128)S(1)}, u32[]{:S(2)}, u32[]{:S(2)}) collective-permute-start(f32[88,128]{1,0:T(8,128)S(1)} %get-tuple-element.20), channel_id=1, source_target_pairs={{0,19},{1,18},{2,17},{3,16},{4,23},{5,22},{6,21},{7,20},{8,27},{9,... | collective-permute-start | bytes 135176 | tf_op jit(solution)/shard_map/ppermute | solution.py:644
  5.9 3.9 %collective-permute-start.4 = (f32[32,128]{1,0:T(8,128)S(1)}, f32[32,128]{1,0:T(8,128)S(1)}, u32[]{:S(2)}, u32[]{:S(2)}) collective-permute-start(f32[32,128]{1,0:T(8,128)S(1)} %get-tuple-element.21.own_side), channel_id=1, source_target_pairs={{0,16},{16,0},{1,17},{17,1},{2,18},{18,2},{3,19},{19,3},{4,20},{20... | collective-permute-start | bytes 49160 | tf_op jit(solution)/shard_map/ppermute | solution.py:642
  10.4 7.4 %collective-permute-start.5 = (f32[384,128]{1,0:T(8,128)S(1)}, f32[384,128]{1,0:T(8,128)S(1)}, u32[]{:S(2)}, u32[]{:S(2)}) collective-permute-start(f32[384,128]{1,0:T(8,128)S(1)} %get-tuple-element.26), channel_id=1, source_target_pairs={{0,16},{16,0},{1,17},{17,1},{2,18},{18,2},{3,19},{19,3},{4,20},{20... | collective-permute-start | bytes 589832 | tf_op jit(solution)/shard_map/ppermute | solution.py:642
  11.6 5.7 %collective-permute-start.6 = (f32[40,128]{1,0:T(8,128)S(1)}, f32[40,128]{1,0:T(8,128)S(1)}, u32[]{:S(2)}, u32[]{:S(2)}) collective-permute-start(f32[40,128]{1,0:T(8,128)S(1)} %get-tuple-element.27.own_east), channel_id=1, source_target_pairs={{0,4},{4,8},{8,12},{12,0},{1,5},{5,9},{9,13},{13,1},{2,6},{6,10},{... | collective-permute-start | bytes 61448 | tf_op jit(solution)/shard_map/ppermute | solution.py:649
  13.2 4.1 %collective-permute-start.7 = (f32[40,128]{1,0:T(8,128)S(1)}, f32[40,128]{1,0:T(8,128)S(1)}, u32[]{:S(2)}, u32[]{:S(2)}) collective-permute-start(f32[40,128]{1,0:T(8,128)S(1)} %get-tuple-element.28.own_west), channel_id=1, source_target_pairs={{0,12},{4,0},{8,4},{12,8},{1,13},{5,1},{9,5},{13,9},{2,14},{6,2},{... | collective-permute-start | bytes 61448 | tf_op jit(solution)/shard_map/ppermute | solution.py:649

commit v3 on v2

--- a/solution.py
+++ b/solution.py
@@ -89,11 +89,12 @@
         side[place * sz.rows : (place + 1) * sz.rows, :] = column
 
 
-def pack_cross(sz, fields, levels, cross_a, cross_b):
+def pack_cross(sz, fields, levels, cross):
     lev = levels[...].astype(jnp.float32)
 
     def fill(which, near, far):
-        cross = (cross_a, cross_b)[which]
+        if which == 0:
+            return
         for at, (f, row) in enumerate(((0, near), (1, near), (1, far), (2, near), (4, near))):
             cross[at * sz.lev : (at + 1) * sz.lev, :] = level_rows(fields, f * sz.slab, row, sz)
         at = LEVEL_ROW * sz.lev
@@ -102,6 +103,23 @@
         cross[at + 2 : at + 8, :] = jnp.zeros((6, sz.cols), jnp.float32)
 
     send_north_first(sz, fill)
+
+
+def pack_twin(sz, fields, own_side, row_a, twin):
+    base = 4 * sz.rows
+    twin[0:base, :] = own_side[...]
+    for at, (f, r) in enumerate(((0, 0), (1, 0), (1, 1), (2, 0), (4, 0))):
+        first = (2 * f + r) * sz.lev
+        twin[base + at * sz.lev : base + (at + 1) * sz.lev, :] = row_a[first : first + sz.lev, :]
+    twin[zonal_place(sz) : zonal_place(sz) + early(sz), :] = fields[0 : early(sz), :]
+
+
+def early(sz):
+    return sz.lev // 2 * sz.rows
+
+
+def zonal_place(sz):
+    return 4 * sz.rows + LEVEL_ROW * sz.lev
 
 
 def edge_columns(sz, ref, count, first):
@@ -123,22 +141,38 @@
 
 
 def pack_columns(
-    sz, fields, levels, row_a, row_b, cross_a, cross_b, own_side, side,
+    sz, fields, levels, levels_a, row_a, row_b, twin, cross_b, own_side,
     to_east, to_west, south, north, cross_south, cross_north, bulk,
 ):
     position = lax.axis_index("lat")
     even = position % 2 == 0
     has_south = position > 0
     has_north = position < lax.axis_size("lat") - 1
-    for low, high, from_a, from_b in ((south, north, row_a, row_b), (cross_south, cross_north, cross_a, cross_b)):
-        first, other = from_a[...], from_b[...]
-        low[...] = jnp.where(has_south, jnp.where(even, other, first), 0.0)
-        high[...] = jnp.where(has_north, jnp.where(even, first, other), 0.0)
-
     tile = (sz.rows, sz.cols)
     lane = lane_ids(tile)
     last = sz.cols - 1
-    bulk[0 : 2 * sz.slab, :] = fields[0 : 2 * sz.slab, :]
+    side = twin
+    level_row = LEVEL_ROW * sz.lev
+    near_a = levels_a[...].astype(jnp.float32)
+    top, second = sz.rows - 1, sz.rows - 2
+    near_a, far_a = (
+        jnp.where(even, near_a[low : low + 1, :], near_a[high : high + 1, :]) for low, high in ((0, top), (1, second))
+    )
+    near_b, far_b = (cross_b[level_row + i : level_row + i + 1, :] for i in range(2))
+    pairs = (
+        (south, north, slice(None), row_a[...], row_b[...]),
+        (cross_south, cross_north, slice(0, level_row), twin[4 * sz.rows : 4 * sz.rows + level_row, :], cross_b[0:level_row, :]),
+        (cross_south, cross_north, slice(level_row, level_row + 1), near_a, near_b),
+        (cross_south, cross_north, slice(level_row + 1, level_row + 2), far_a, far_b),
+    )
+    for low, high, at, first, other in pairs:
+        low[at, :] = jnp.where(has_south, jnp.where(even, other, first), 0.0)
+        high[at, :] = jnp.where(has_north, jnp.where(even, first, other), 0.0)
+    for ref in (cross_south, cross_north):
+        ref[level_row + 2 : level_row + 8, :] = jnp.zeros((6, sz.cols), jnp.float32)
+
+    bulk[0 : sz.slab, :] = fields[sz.slab : 2 * sz.slab, :]
+    bulk[2 * sz.slab : 3 * sz.slab - early(sz), :] = fields[early(sz) : sz.slab, :]
     tracer_lanes = lane < sz.nf * sz.lev
     for place, (message, at) in enumerate(((to_east, 0), (to_west, 0), (to_east, sz.rows), (to_west, sz.rows))):
         own = own_side[place * sz.rows : (place + 1) * sz.rows, :]
@@ -146,7 +180,6 @@
         message[at : at + sz.rows, :] = jnp.where(tracer_lanes, own, turn(dynamics, sz.nf * sz.lev, 1))
 
     lev = levels[...].astype(jnp.float32)
-    level_row = LEVEL_ROW * sz.lev
     south_lev = cross_south[level_row : level_row + 1, :]
     north_lev = cross_north[level_row : level_row + 1, :]
     base = 2 * sz.lev
@@ -203,7 +236,7 @@
             background = fields[5 * sz.slab + at : 5 * sz.slab + at + sz.rows, :]
             mixing = jnp.zeros(tile, jnp.float32) if k == 0 else mixed(warm_above, warm, background, wet)
             warm_above = warm
-            bulk[2 * sz.slab + at : 2 * sz.slab + at + sz.rows, :] = mixing
+            bulk[sz.slab + at : sz.slab + at + sz.rows, :] = mixing
 
 
 def keep(mask, value):
@@ -426,7 +459,7 @@
                 flow_s = keep(wet_near & wet(far_lev), merid_far)
             else:
                 flow_n = keep(wet_near & wet(far_lev), merid)
-                flow_s = keep(wet_near & wet(own_lev), level_rows(bulk, sz.slab, last_row, sz))
+                flow_s = keep(wet_near & wet(own_lev), level_rows(bulk, 0, last_row, sz))
             weights = Weights(flow_e, flow_w, flow_n, flow_s, step)
             for f in range(sz.nf):
                 at = 2 * f * sz.lev
@@ -525,7 +558,9 @@
         for k in range(sz.lev):
             at = k * sz.rows
             wet, wet_e, wet_w, wet_n, wet_s = masks(k)
-            zonal, merid = bulk[at : at + sz.rows, :], bulk[sz.slab + at : sz.slab + at + sz.rows, :]
+            zonal_at = zonal_place(sz) + at if at < early(sz) else 2 * sz.slab + at - early(sz)
+            zonal = (side if at < early(sz) else bulk)[zonal_at : zonal_at + sz.rows, :]
+            merid = bulk[at : at + sz.rows, :]
             zonal_first = sz.nf * sz.lev
             zonal_west = shift_west(zonal, lane, to_lane(west_old, zonal_first + k, 0))
             beyond = MERID_ROW * sz.lev + k
@@ -556,7 +591,7 @@
             at = k * sz.rows
             total = total + div[at : at + sz.rows, :]
             vert[at : at + sz.rows, :] = -total if k > 0 else zero
-            mixing = bulk[2 * sz.slab + at : 2 * sz.slab + at + sz.rows, :]
+            mixing = bulk[sz.slab + at : sz.slab + at + sz.rows, :]
             mixing = jnp.where(lane == 0, to_lane(edge_w, k, 0), mixing)
             mix[at : at + sz.rows, :] = jnp.where(lane == last_lane, to_lane(edge_e, k, last_lane), mixing)
         last_ratio = None
@@ -622,26 +657,33 @@
     sz = Sizes(fields, levels)
     count_s, count_o, count_a = sizes_of
     flat = fields.reshape(sz.nf * sz.slab, sz.cols)
-    axes = ("sect", "lon", "lat")
-
-    def swap(value, odd):
-        pairs = [(i, pair_of(i, count_a, odd)) for i in range(count_a)]
-        return lax.ppermute(value, "lat", pairs)
+
+    def place(s, o, a):
+        return (s * count_o + o) * count_a + a
+
+    def partner(s, o, a, odd, hop):
+        b = pair_of(a, count_a, odd)
+        if abs(a - b) > 1 and count_o % 2 == 0:
+            return place(s, o ^ 1, a)
+        return place((s + hop) % count_s, o, b)
+
+    def swap(value, odd, hop=0):
+        pairs = [
+            (place(s, o, a), partner(s, o, a, odd, hop))
+            for s in range(count_s)
+            for o in range(count_o)
+            for a in range(count_a)
+        ]
+        return lax.ppermute(value, ("sect", "lon", "lat"), pairs)
 
     def from_dynamics(value, odd=None):
         mine = lax.axis_index("sect")
         got = None
         for hop in range(1, count_s):
-            pairs = []
-            for s in range(count_s):
-                for o in range(count_o):
-                    for a in range(count_a):
-                        b = a if odd is None else pair_of(a, count_a, odd)
-                        pairs.append(((s * count_o + o) * count_a + a, (((s + hop) % count_s) * count_o + o) * count_a + b))
             if odd is None:
                 part = lax.ppermute(value, "sect", [(s, (s + hop) % count_s) for s in range(count_s)])
             else:
-                part = lax.ppermute(value, axes, pairs)
+                part = swap(value, odd, hop)
             got = part if got is None else jnp.where(mine == hop, part, got)
         return got
 
@@ -653,16 +695,19 @@
     columns_shape = (3 * sz.rows + sz.lev, sz.cols)
     side_shape = (4 * sz.rows, sz.cols)
     row_a, row_b, own_side = call_kernel(functools.partial(pack_edges, sz), [rows_shape, rows_shape, side_shape], [flat])
-    cross_a, cross_b = call_kernel(functools.partial(pack_cross, sz), [cross_shape, cross_shape], [flat, levels])
-    side = from_dynamics(own_side)
+    (cross_b,) = call_kernel(functools.partial(pack_cross, sz), [cross_shape], [flat, levels])
+    row_a = swap(row_a, False)
+    levels_a = swap(levels, False)
+    row_b = swap(row_b, True)
+    (twin,) = call_kernel(
+        functools.partial(pack_twin, sz), [(zonal_place(sz) + early(sz), sz.cols)], [flat, own_side, row_a]
+    )
+    twin = from_dynamics(twin)
     cross_b = from_dynamics(cross_b, True)
-    row_b = swap(row_b, True)
-    cross_a = from_dynamics(cross_a, False)
-    row_a = swap(row_a, False)
     to_east, to_west, south, north, cross_south, cross_north, bulk = call_kernel(
         functools.partial(pack_columns, sz),
-        [columns_shape] * 2 + [rows_shape] * 2 + [cross_shape] * 2 + [(3 * sz.slab, sz.cols)],
-        [flat, levels, row_a, row_b, cross_a, cross_b, own_side, side],
+        [columns_shape] * 2 + [rows_shape] * 2 + [cross_shape] * 2 + [(3 * sz.slab - early(sz), sz.cols)],
+        [flat, levels, levels_a, row_a, row_b, twin, cross_b, own_side],
     )
     bulk = from_dynamics(bulk)
     from_east = around(to_west, -1)
@@ -671,7 +716,7 @@
     (out,) = call_kernel(
         functools.partial(finish, sz),
         [flat.shape],
-        [flat, levels, south, north, cross_south, cross_north, bulk, to_east, to_west, side, from_west, from_east],
+        [flat, levels, south, north, cross_south, cross_north, bulk, to_east, to_west, twin, from_west, from_east],
         [slab, slab, slab, (sz.nf * sz.lev, sz.cols), (sz.nf * sz.lev, sz.cols), (2 * sz.rows, sz.cols), slab, flat.shape, slab, (5 * sz.slab, sz.cols), slab, flat.shape],
     )
     return out.reshape(fields.shape)

time: 19.1 us -> 18.3 us (0.958)
  starting transfers between devices: 11.4 us -> 10.5 us
    ppermute x4, waiting for transfers between devices: 0.13 us -> 2.73 us  [swap(): return lax.ppermute(value, ('sect', 'lon', 'lat'), pairs)]
    ppermute x2, waiting for transfers between devices: 2.61 us -> 0.07 us  [from_dynamics(): lax.ppermute(value, 'sect', [(s, (s + hop) % count_s) for s in range(coun...]
    ppermute x2, starting transfers between devices: 3 us -> 2.19 us  [from_dynamics(): lax.ppermute(value, 'sect', [(s, (s + hop) % count_s) for s in range(coun...]
    pallas_call x4 -> x5, Pallas kernels: 1.88 us -> 1.88 us  [call_kernel(): pl.pallas_call(body, out_shape=[jax.ShapeDtypeStruct(shape, jnp.float32)...]
  transfers between devices with their start and end apart: 8 -> 8, of which waited for: 4 -> 5; matrix products, arithmetic and copies ran while one was open for 0% -> 0% of each run, Pallas kernels for 0% -> 0%
where the time goes in v3:
time: 18.3 us; the launch traced here: 18.2 us
  starting transfers between devices  10.5 us (57%)
  waiting for transfers between devices  4.75 us (26%)
  Pallas kernels  1.88 us (10%)
  local copies, waits for them, and re-layouts  1 us (5%)
    ppermute x4, starting transfers between devices, swap(): return lax.ppermute(value, ('sect', 'lon', 'lat'), pairs)  4.49 us
    ppermute x2, starting transfers between devices, around(): lax.ppermute(value, 'lon', [(i, (i + step) % count_o) for i in range(coun...  3.82 us
    ppermute x4, waiting for transfers between devices, swap(): return lax.ppermute(value, ('sect', 'lon', 'lat'), pairs)  2.73 us
    ppermute x2, starting transfers between devices, from_dynamics(): lax.ppermute(value, 'sect', [(s, (s + hop) % count_s) for s in range(coun...  2.19 us
    ppermute x2, waiting for transfers between devices, around(): lax.ppermute(value, 'lon', [(i, (i + step) % count_o) for i in range(coun...  1.95 us
    pallas_call x5, Pallas kernels, call_kernel(): pl.pallas_call(body, out_shape=[jax.ShapeDtypeStruct(shape, jnp.float32)...  1.88 us
    unnamed x4, local copies, waits for them, and re-layouts  1 us
  transfers between devices with their start and end apart: 8, of which 5 were waited for; matrix products, arithmetic and copies ran while one was open for 0% of the time, Pallas kernels for 0%

profile of v3, /device:TPU:0, one launch (start us, length us, event | category | flops | bytes accessed | tf_op | source)
XLA Modules:
  0.0 18.2 jit_solution(15426257609931249305)
XLA Ops:
  0.0 0.0 copy-start
  0.0 1.0 %copy-done = f32[1,6,16,8,128]{4,3,2,1,0:T(8,128)S(1)} copy-done((f32[1,6,16,8,128]{4,3,2,1,0:T(8,128)S(1)}, f32[1,6,16,8,128]{4,3,2,1,0:T(8,128)}, u32[]{:S(2)}) %copy-start) | copy-done | bytes 393240
  1.0 0.3 %shard_map.28 = (f32[192,128]{1,0:T(8,128)S(1)}, f32[192,128]{1,0:T(8,128)S(1)}, f32[32,128]{1,0:T(8,128)S(1)}) custom-call(f32[768,128]{1,0:T(8,128)S(1)} %bitcast.2), custom_call_target="tpu_custom_call" | custom-call | tf_op jit(solution)/shard_map/pallas_call | solution.py:25
  1.3 0.5 %collective-permute-start.1 = (f32[192,128]{1,0:T(8,128)S(1)}, f32[192,128]{1,0:T(8,128)S(1)}, u32[]{:S(2)}, u32[]{:S(2)}) collective-permute-start(f32[192,128]{1,0:T(8,128)S(1)} %get-tuple-element.15), channel_id=1, source_target_pairs={{0,1},{1,0},{2,3},{3,2},{4,5},{5,4},{6,7},{7,6},{8,9},{9,8},{10,11... | collective-permute-start | bytes 294920 | tf_op jit(solution)/shard_map/ppermute | solution.py:677
  1.7 2.6 %collective-permute-start.2 = (f32[192,128]{1,0:T(8,128)S(1)}, f32[192,128]{1,0:T(8,128)S(1)}, u32[]{:S(2)}, u32[]{:S(2)}) collective-permute-start(f32[192,128]{1,0:T(8,128)S(1)} %get-tuple-element.16), channel_id=1, source_target_pairs={{0,4},{1,2},{2,1},{3,7},{4,0},{5,6},{6,5},{7,3},{8,12},{9,10},{10,... | collective-permute-start | bytes 294920 | tf_op jit(solution)/shard_map/ppermute | solution.py:677
  4.4 0.0 collective-permute-done.1.row_a
  4.4 0.0 copy-start.1
  4.4 1.6 %collective-permute-start.3 = (f32[176,128]{1,0:T(8,128)S(1)}, f32[176,128]{1,0:T(8,128)S(1)}, u32[]{:S(2)}, u32[]{:S(2)}) collective-permute-start(f32[176,128]{1,0:T(8,128)S(1)} %shard_map.29), channel_id=1, source_target_pairs={{0,16},{16,0},{1,17},{17,1},{2,18},{18,2},{3,19},{19,3},{4,20},{20... | collective-permute-start | bytes 270344 | tf_op jit(solution)/shard_map/ppermute | solution.py:684
  5.9 0.0 copy-done.1
  6.0 1.3 %collective-permute-start.4 = (f32[88,128]{1,0:T(8,128)S(1)}, f32[88,128]{1,0:T(8,128)S(1)}, u32[]{:S(2)}, u32[]{:S(2)}) collective-permute-start(f32[88,128]{1,0:T(8,128)S(1)} %shard_map.30), channel_id=1, source_target_pairs={{0,4},{1,18},{2,17},{3,7},{4,0},{5,22},{6,21},{7,3},{8,12},{9,26},... | collective-permute-start | bytes 135176 | tf_op jit(solution)/shard_map/ppermute | solution.py:677
  7.3 0.1 collective-permute-start
  7.4 1.1 %collective-permute-done.levels_a = s32[8,128]{1,0:T(8,128)S(1)} collective-permute-done((s32[8,128]{1,0:T(8,128)S(1)}, s32[8,128]{1,0:T(8,128)S(1)}, u32[]{:S(2)}, u32[]{:S(2)}) %collective-permute-start) | collective-permute-done | bytes 4128 | tf_op jit(solution)/shard_map/ppermute | solution.py:677
  8.4 1.7 %collective-permute-done.4.cross_b = f32[88,128]{1,0:T(8,128)S(1)} collective-permute-done((f32[88,128]{1,0:T(8,128)S(1)}, f32[88,128]{1,0:T(8,128)S(1)}, u32[]{:S(2)}, u32[]{:S(2)}) %collective-permute-start.4) | collective-permute-done | bytes 45088 | tf_op jit(solution)/shard_map/ppermute | solution.py:677
  10.1 0.0 collective-permute-done.2.row_b
  10.1 0.0 collective-permute-done.3.twin.side
  10.1 0.4 %shard_map.31 = (f32[40,128]{1,0:T(8,128)S(1)}, f32[40,128]{1,0:T(8,128)S(1)}, f32[192,128]{1,0:T(8,128)S(1)}, f32[192,128]{1,0:T(8,128)S(1)}, f32[88,128]{1,0:T...) custom-call(f32[768,128]{1,0:T(8,128)S(1)} %bitcast.5, s32[8,128]{1,0:T(8,128)S(1)} %copy-done.1, ...), custom_call_target="tpu_custom_call" | custom-call | tf_op jit(solution)/shard_map/pallas_call | solution.py:25
  10.4 0.6 %collective-permute-start.5 = (f32[320,128]{1,0:T(8,128)S(1)}, f32[320,128]{1,0:T(8,128)S(1)}, u32[]{:S(2)}, u32[]{:S(2)}) collective-permute-start(f32[320,128]{1,0:T(8,128)S(1)} %get-tuple-element.22), channel_id=1, source_target_pairs={{0,16},{16,0},{1,17},{17,1},{2,18},{18,2},{3,19},{19,3},{4,20},{20... | collective-permute-start | bytes 491528 | tf_op jit(solution)/shard_map/ppermute | solution.py:684
  11.1 1.6 %collective-permute-start.6 = (f32[40,128]{1,0:T(8,128)S(1)}, f32[40,128]{1,0:T(8,128)S(1)}, u32[]{:S(2)}, u32[]{:S(2)}) collective-permute-start(f32[40,128]{1,0:T(8,128)S(1)} %get-tuple-element.23.own_east), channel_id=1, source_target_pairs={{0,4},{4,8},{8,12},{12,0},{1,5},{5,9},{9,13},{13,1},{2,6},{6,10},{... | collective-permute-start | bytes 61448 | tf_op jit(solution)/shard_map/ppermute | solution.py:691
  12.6 2.3 %collective-permute-start.7 = (f32[40,128]{1,0:T(8,128)S(1)}, f32[40,128]{1,0:T(8,128)S(1)}, u32[]{:S(2)}, u32[]{:S(2)}) collective-permute-start(f32[40,128]{1,0:T(8,128)S(1)} %get-tuple-element.24.own_west), channel_id=1, source_target_pairs={{0,12},{4,0},{8,4},{12,8},{1,13},{5,1},{9,5},{13,9},{2,14},{6,2},{... | collective-permute-start | bytes 61448 | tf_op jit(solution)/shard_map/ppermute | solution.py:691
  14.9 1.9 %collective-permute-done.6.from_west = f32[40,128]{1,0:T(8,128)S(1)} collective-permute-done((f32[40,128]{1,0:T(8,128)S(1)}, f32[40,128]{1,0:T(8,128)S(1)}, u32[]{:S(2)}, u32[]{:S(2)}) %collective-permute-start.6) | collective-permute-done | bytes 20512 | tf_op jit(solution)/shard_map/ppermute | solution.py:691
  16.8 0.1 collective-permute-done.7.from_east
  16.9 0.1 collective-permute-done.5.bulk
  16.9 1.2 %shard_map.32 = f32[768,128]{1,0:T(8,128)} custom-call(f32[768,128]{1,0:T(8,128)S(1)} %bitcast.6, s32[8,128]{1,0:T(8,128)S(1)} %copy-done.1, f32[192,128]{1,0:T(8,128)S(1)} %get-tuple-element.18.south, f32[192,128]{1,0:T(8,128)S(1)} %get-tuple-element.19.north, f32[88,128]{1,0:T(8,128)S(1)} %get-tuple-element.20.cross_south, ...), custom_call_target="tpu_custom_call" | custom-call | tf_op jit(solution)/shard_map/pallas_call | solution.py:25
  (2 shorter events, 0.0 us)
Async XLA Ops:
  0.0 1.0 %copy-start = (f32[1,6,16,8,128]{4,3,2,1,0:T(8,128)S(1)}, f32[1,6,16,8,128]{4,3,2,1,0:T(8,128)}, u32[]{:S(2)}) copy-start(f32[1,6,16,8,128]{4,3,2,1,0:T(8,128)} %param.2) | copy-start | bytes 1179652
  1.3 3.1 %collective-permute-start.1 = (f32[192,128]{1,0:T(8,128)S(1)}, f32[192,128]{1,0:T(8,128)S(1)}, u32[]{:S(2)}, u32[]{:S(2)}) collective-permute-start(f32[192,128]{1,0:T(8,128)S(1)} %get-tuple-element.15), channel_id=1, source_target_pairs={{0,1},{1,0},{2,3},{3,2},{4,5},{5,4},{6,7},{7,6},{8,9},{9,8},{10,11... | collective-permute-start | bytes 294920 | tf_op jit(solution)/shard_map/ppermute | solution.py:677
  1.7 8.4 %collective-permute-start.2 = (f32[192,128]{1,0:T(8,128)S(1)}, f32[192,128]{1,0:T(8,128)S(1)}, u32[]{:S(2)}, u32[]{:S(2)}) collective-permute-start(f32[192,128]{1,0:T(8,128)S(1)} %get-tuple-element.16), channel_id=1, source_target_pairs={{0,4},{1,2},{2,1},{3,7},{4,0},{5,6},{6,5},{7,3},{8,12},{9,10},{10,... | collective-permute-start | bytes 294920 | tf_op jit(solution)/shard_map/ppermute | solution.py:677
  4.4 1.6 %copy-start.1 = (s32[8,128]{1,0:T(8,128)S(1)}, s32[8,128]{1,0:T(8,128)}, u32[]{:S(2)}) copy-start(s32[8,128]{1,0:T(8,128)} %levels.5) | copy-start | bytes 12292
  4.4 5.7 %collective-permute-start.3 = (f32[176,128]{1,0:T(8,128)S(1)}, f32[176,128]{1,0:T(8,128)S(1)}, u32[]{:S(2)}, u32[]{:S(2)}) collective-permute-start(f32[176,128]{1,0:T(8,128)S(1)} %shard_map.29), channel_id=1, source_target_pairs={{0,16},{16,0},{1,17},{17,1},{2,18},{18,2},{3,19},{19,3},{4,20},{20... | collective-permute-start | bytes 270344 | tf_op jit(solution)/shard_map/ppermute | solution.py:684
  6.0 4.1 %collective-permute-start.4 = (f32[88,128]{1,0:T(8,128)S(1)}, f32[88,128]{1,0:T(8,128)S(1)}, u32[]{:S(2)}, u32[]{:S(2)}) collective-permute-start(f32[88,128]{1,0:T(8,128)S(1)} %shard_map.30), channel_id=1, source_target_pairs={{0,4},{1,18},{2,17},{3,7},{4,0},{5,22},{6,21},{7,3},{8,12},{9,26},... | collective-permute-start | bytes 135176 | tf_op jit(solution)/shard_map/ppermute | solution.py:677
  7.3 1.2 %collective-permute-start = (s32[8,128]{1,0:T(8,128)S(1)}, s32[8,128]{1,0:T(8,128)S(1)}, u32[]{:S(2)}, u32[]{:S(2)}) collective-permute-start(s32[8,128]{1,0:T(8,128)S(1)} %copy-done.1), channel_id=1, source_target_pairs={{0,1},{1,0},{2,3},{3,2},{4,5},{5,4},{6,7},{7,6},{8,9},{9,8},{10,11... | collective-permute-start | bytes 12296 | tf_op jit(solution)/shard_map/ppermute | solution.py:677
  10.4 6.5 %collective-permute-start.5 = (f32[320,128]{1,0:T(8,128)S(1)}, f32[320,128]{1,0:T(8,128)S(1)}, u32[]{:S(2)}, u32[]{:S(2)}) collective-permute-start(f32[320,128]{1,0:T(8,128)S(1)} %get-tuple-element.22), channel_id=1, source_target_pairs={{0,16},{16,0},{1,17},{17,1},{2,18},{18,2},{3,19},{19,3},{4,20},{20... | collective-permute-start | bytes 491528 | tf_op jit(solution)/shard_map/ppermute | solution.py:684
  11.1 5.7 %collective-permute-start.6 = (f32[40,128]{1,0:T(8,128)S(1)}, f32[40,128]{1,0:T(8,128)S(1)}, u32[]{:S(2)}, u32[]{:S(2)}) collective-permute-start(f32[40,128]{1,0:T(8,128)S(1)} %get-tuple-element.23.own_east), channel_id=1, source_target_pairs={{0,4},{4,8},{8,12},{12,0},{1,5},{5,9},{9,13},{13,1},{2,6},{6,10},{... | collective-permute-start | bytes 61448 | tf_op jit(solution)/shard_map/ppermute | solution.py:691
  12.6 4.2 %collective-permute-start.7 = (f32[40,128]{1,0:T(8,128)S(1)}, f32[40,128]{1,0:T(8,128)S(1)}, u32[]{:S(2)}, u32[]{:S(2)}) collective-permute-start(f32[40,128]{1,0:T(8,128)S(1)} %get-tuple-element.24.own_west), channel_id=1, source_target_pairs={{0,12},{4,0},{8,4},{12,8},{1,13},{5,1},{9,5},{13,9},{2,14},{6,2},{... | collective-permute-start | bytes 61448 | tf_op jit(solution)/shard_map/ppermute | solution.py:691

commit v4 on v3

--- a/solution.py
+++ b/solution.py
@@ -16,18 +16,23 @@
 RICHARDSON = 1.0
 
 VMEM_LIMIT = 8 * 1024 * 1024
+CHUNKS = 4
+EARLY_LEVELS = 0
 
 ZONAL_ROW, MERID_ROW, MERID_ROW2, TEMPER_ROW, VISC_ROW, LEVEL_ROW = range(6)
 
 
-def call_kernel(body, outputs, inputs, scratch=()):
+def call_kernel(body, outputs, inputs, scratch=(), copies=0):
     in_vmem = pl.BlockSpec(memory_space=pltpu.VMEM)
+    scratch = [pltpu.VMEM(shape, jnp.float32) for shape in scratch]
+    if copies:
+        scratch.append(pltpu.SemaphoreType.DMA((copies,)))
     return pl.pallas_call(
         body,
         out_shape=[jax.ShapeDtypeStruct(shape, jnp.float32) for shape in outputs],
         in_specs=[in_vmem] * len(inputs),
-        out_specs=[in_vmem] * len(outputs),
-        scratch_shapes=[pltpu.VMEM(shape, jnp.float32) for shape in scratch],
+        out_specs=[pl.BlockSpec(memory_space=pl.ANY) if copies else in_vmem] * len(outputs),
+        scratch_shapes=scratch,
         compiler_params=pltpu.CompilerParams(vmem_limit_bytes=VMEM_LIMIT),
     )(*inputs)
 
@@ -100,7 +105,7 @@
         at = LEVEL_ROW * sz.lev
         cross[at : at + 1, :] = lev[near : near + 1, :]
         cross[at + 1 : at + 2, :] = lev[far : far + 1, :]
-        cross[at + 2 : at + 8, :] = jnp.zeros((6, sz.cols), jnp.float32)
+        cross[at + 2 :, :] = jnp.zeros((cross.shape[0] - at - 2, sz.cols), jnp.float32)
 
     send_north_first(sz, fill)
 
@@ -111,11 +116,12 @@
     for at, (f, r) in enumerate(((0, 0), (1, 0), (1, 1), (2, 0), (4, 0))):
         first = (2 * f + r) * sz.lev
         twin[base + at * sz.lev : base + (at + 1) * sz.lev, :] = row_a[first : first + sz.lev, :]
-    twin[zonal_place(sz) : zonal_place(sz) + early(sz), :] = fields[0 : early(sz), :]
+    if early(sz):
+        twin[zonal_place(sz) : zonal_place(sz) + early(sz), :] = fields[0 : early(sz), :]
 
 
 def early(sz):
-    return sz.lev // 2 * sz.rows
+    return EARLY_LEVELS * sz.rows
 
 
 def zonal_place(sz):
@@ -140,9 +146,33 @@
     return east_one, turn(west_one, -1, 1), turn(east_two, 1, 1), turn(west_two, -2, 1)
 
 
+def place_rows(sz, row_a, row_b, south, north, corners):
+    position = lax.axis_index("lat")
+    even = position % 2 == 0
+    first, other = row_a[...], row_b[...]
+    tall = (sz.lev, sz.cols)
+    lane, depth = lane_ids(tall), row_ids(tall)
+    low = jnp.where(position > 0, jnp.where(even, other, first), 0.0)
+    high = jnp.where(position < lax.axis_size("lat") - 1, jnp.where(even, first, other), 0.0)
+    south[...] = low
+    north[...] = high
+    ends = []
+    for column in (sz.cols - 1, 0):
+        for rows in (low, high):
+            total = jnp.zeros(tall, jnp.float32)
+            for f in range(sz.nf):
+                near = rows[2 * f * sz.lev : (2 * f + 1) * sz.lev, :]
+                spread = jnp.broadcast_to(near[:, column : column + 1], tall)
+                total = jnp.where(lane == f * sz.lev + depth, spread, total)
+            ends.append(jnp.sum(total, axis=0, keepdims=True))
+    for i, end in enumerate(ends):
+        corners[i : i + 1, :] = end
+    corners[len(ends) :, :] = jnp.zeros((sz.rows - len(ends), sz.cols), jnp.float32)
+
+
 def pack_columns(
-    sz, fields, levels, levels_a, row_a, row_b, twin, cross_b, own_side,
-    to_east, to_west, south, north, cross_south, cross_north, bulk,
+    sz, fields, levels, levels_a, south, north, corners, twin, cross_b, own_side,
+    to_east, to_west, cross_south, cross_north, bulk,
 ):
     position = lax.axis_index("lat")
     even = position % 2 == 0
@@ -160,7 +190,6 @@
     )
     near_b, far_b = (cross_b[level_row + i : level_row + i + 1, :] for i in range(2))
     pairs = (
-        (south, north, slice(None), row_a[...], row_b[...]),
         (cross_south, cross_north, slice(0, level_row), twin[4 * sz.rows : 4 * sz.rows + level_row, :], cross_b[0:level_row, :]),
         (cross_south, cross_north, slice(level_row, level_row + 1), near_a, near_b),
         (cross_south, cross_north, slice(level_row + 1, level_row + 2), far_a, far_b),
@@ -211,6 +240,9 @@
             west_corner = jnp.where(tall_lane == p + 1, moved, west_corner)
     to_east[3 * sz.rows : 3 * sz.rows + sz.lev, :] = east_corner
     to_west[3 * sz.rows : 3 * sz.rows + sz.lev, :] = turn(west_corner, -1, 1)
+    ends = corners[...]
+    to_east[3 * sz.rows + sz.lev :, :] = ends
+    to_west[3 * sz.rows + sz.lev :, :] = turn(ends, -2, 0)
 
     @pl.when(lax.axis_index("sect") == 0)
     def _():
@@ -300,10 +332,24 @@
         return self.own * own + self.east * east + self.west * west + (self.north * north + self.south * south)
 
 
-def finish(
-    sz, fields, levels, south, north, cross_south, cross_north, bulk,
-    own_east, own_west, side, from_west, from_east,
-    out, div, mix, vert, low_strip, high_strip, side_strips, ratio, forward, inv_ref, wref, pull, moved,
+def shift_fields(sz, fields, south, north, kept, moved_e, moved_w, moved_n, moved_s):
+    kept[...] = fields[...]
+    row = row_ids((sz.rows, sz.cols))
+    for f in range(sz.nf):
+        for k in range(sz.lev):
+            at = f * sz.slab + k * sz.rows
+            here = slice(at, at + sz.rows)
+            value = fields[here, :]
+            beyond = 2 * f * sz.lev + k
+            moved_e[here, :] = turn(value, -1, 1)
+            moved_w[here, :] = turn(value, 1, 1)
+            moved_n[here, :] = shift_north(value, row, north[beyond : beyond + 1, :])
+            moved_s[here, :] = shift_south(value, row, south[beyond : beyond + 1, :])
+
+
+def column_edges(
+    sz, levels, cross_south, cross_north, own_east, own_west, side, from_west, from_east, moved_e, moved_w,
+    around_e, around_w, second, edge_mix,
 ):
     tile = (sz.rows, sz.cols)
     lane, row = lane_ids(tile), row_ids(tile)
@@ -323,57 +369,6 @@
         wet = lev > k
         return wet, wet & (lev_e > k), wet & (lev_w > k), wet & (lev_n > k), wet & (lev_s > k)
 
-    is_dynamics = lax.axis_index("sect") == 0
-
-    def physics():
-        def around(f, k):
-            at = f * sz.slab + k * sz.rows
-            value = fields[at : at + sz.rows, :]
-            lane_at, beyond = f * sz.lev + k, 2 * f * sz.lev + k
-            return (
-                value,
-                shift_east(value, lane, to_lane(from_east[0 : sz.rows, :], lane_at, last_lane)),
-                shift_west(value, lane, to_lane(from_west[0 : sz.rows, :], lane_at, 0)),
-                shift_north(value, row, north[beyond : beyond + 1, :]),
-                shift_south(value, row, south[beyond : beyond + 1, :]),
-            )
-
-        press = jnp.zeros(tile, jnp.float32)
-        press_e, press_n, warm_above = press, press, press
-        for k in range(sz.lev):
-            at = k * sz.rows
-            mask = masks(k)
-            wet, wet_e, wet_w, wet_n, wet_s = mask
-            zonal, merid, temper, saline, visc = (around(f, k) for f in range(5))
-            flow_east, flow_west = keep(wet_e, zonal[0]), keep(wet_w, zonal[2])
-            flow_north, flow_south = keep(wet_n, merid[0]), keep(wet_s, merid[4])
-            div[at : at + sz.rows, :] = flow_east - flow_west + (flow_north - flow_south)
-            warm = diffused(temper, visc, mask)
-            mixing = jnp.zeros(tile, jnp.float32)
-            if k > 0:
-                background = fields[5 * sz.slab + at : 5 * sz.slab + at + sz.rows, :]
-                mixing = mixed(warm_above, warm, background, wet)
-            warm_above = warm
-
-            def weight(place, wet_there):
-                return keep(wet_there, HALINE * saline[place] - THERMAL * temper[place])
-
-            press = press + GRAVITY_SCALE * weight(0, wet)
-            press_e = press_e + GRAVITY_SCALE * weight(1, lev_e > k)
-            press_n = press_n + GRAVITY_SCALE * weight(3, lev_n > k)
-            zonal_new = diffused(zonal, visc, mask) + TIME_STEP * (CORIOLIS * merid[0] - (press_e - press))
-            merid_new = diffused(merid, visc, mask) - TIME_STEP * (CORIOLIS * zonal[0] + (press_n - press))
-            saline_new = diffused(saline, visc, mask)
-            parts = (keep(wet_e, zonal_new), keep(wet_n, merid_new), warm, saline_new, None, mixing)
-            for f, part in enumerate(parts):
-                if part is not None:
-                    out[f * sz.slab + at : f * sz.slab + at + sz.rows, :] = part
-        total = jnp.zeros(tile, jnp.float32)
-        for k in range(sz.lev - 1, -1, -1):
-            at = k * sz.rows
-            total = total + div[at : at + sz.rows, :]
-            out[4 * sz.slab + at : 4 * sz.slab + at + sz.rows, :] = -total if k > 0 else jnp.zeros(tile, jnp.float32)
-
     def column(value, at):
         return jnp.broadcast_to(value[:, at : at + 1], value.shape)
 
@@ -426,6 +421,175 @@
         warm = diffused(around(2, 0, TEMPER_ROW), around(4, sz.lev, VISC_ROW), mask)
         background = turn(own_pair, -5 * sz.lev, 1)
         return jnp.where(pair_lane == 0, 0.0, mixed(turn(warm, 1, 1), warm, background, mid))
+
+    def column_strips(step):
+        lane16, depth16 = lane_ids(tall), row_ids(tall)
+
+        def all_fields(value, first):
+            at = lane_ids(value.shape)
+            value = jnp.where((at >= first) & (at < first + sz.lev), value, 0.0)
+            width = sz.lev
+            while width < sz.cols:
+                value = value + turn(value, width, 1)
+                width *= 2
+            return value
+
+        def corner_rows(message, r):
+            items = message[3 * sz.rows : 3 * sz.rows + sz.lev, :]
+            p = r * (sz.nf + 2)
+            ends = 3 * sz.rows + sz.lev + r
+            tracers = message[ends : ends + 1, :]
+            spread = jnp.broadcast_to(items[:, p + sz.nf + 1 : p + sz.nf + 2], tall)
+            velocity = jnp.where(lane16 % sz.lev == depth16, spread, 0.0)
+            return tracers, jnp.sum(velocity, axis=0, keepdims=True)
+
+        inside_w, inside_e = own_west[0 : sz.rows, :], own_east[0 : sz.rows, :]
+        near = both(from_west[0 : sz.rows, :], from_east[0 : sz.rows, :])
+        far_w, far_e = from_west[sz.rows : 2 * sz.rows, :], from_east[sz.rows : 2 * sz.rows, :]
+        corners = [corner_rows(message, r) for message in (from_west, from_east) for r in range(2)]
+        low_tracers, high_tracers, low_merid = (
+            both(jnp.broadcast_to(corners[i][part], tile), jnp.broadcast_to(corners[i + 2][part], tile))
+            for i, part in ((0, 0), (1, 0), (0, 1))
+        )
+
+        def side_levels(at):
+            return column(west_side, at), column(east_side, at)
+
+        near_lev = both(*side_levels(side_base))
+        far_lev_w, far_lev_e = side_levels(side_base + 1)
+        own_lev_w, own_lev_e = column(lev, 0), column(lev, last_lane)
+        lev_at_s = pair_south(near_lev, both(*side_levels(side_base + 2)))
+        lev_at_n = pair_north(near_lev, both(*side_levels(side_base + 3)))
+        depth = (lane_ids(near.shape) % sz.lev).astype(jnp.float32)
+        wet_near = near_lev > depth
+        zonal_first = sz.nf * sz.lev
+        west, east = both(far_w, inside_e), both(inside_w, far_e)
+        flow_e = keep(wet_near & (both(own_lev_w, far_lev_e) > depth), all_fields(near, zonal_first))
+        flow_w = keep(wet_near & (both(far_lev_w, own_lev_e) > depth), all_fields(west, zonal_first))
+        merid = all_fields(near, zonal_first + sz.lev)
+        flow_n = keep(wet_near & (lev_at_n > depth), merid)
+        flow_s = keep(wet_near & (lev_at_s > depth), pair_south(merid, low_merid))
+        weights = Weights(flow_e, flow_w, flow_n, flow_s, step)
+        return weights.apply(near, east, west, pair_north(near, high_tracers), pair_south(near, low_tracers))
+
+    @pl.when(lax.axis_index("sect") > 0)
+    def _():
+        west_old, east_old = from_west[0 : sz.rows, :], from_east[0 : sz.rows, :]
+        strips = column_strips(TIME_STEP / NSUB)
+        west_new, east_new = strips[0 : sz.rows, :], strips[sz.rows : 2 * sz.rows, :]
+        edges = edge_mixing()
+        edge_w, edge_e = edges[0 : sz.rows, :], edges[sz.rows : 2 * sz.rows, :]
+        first, last = lane == 0, lane == last_lane
+        for k in range(sz.lev):
+            at = k * sz.rows
+            edge_mix[at : at + sz.rows, :] = jnp.where(first, to_lane(edge_w, k, 0), to_lane(edge_e, k, last_lane))
+            for f in range(sz.nf):
+                here = slice(f * sz.slab + at, f * sz.slab + at + sz.rows)
+                p = f * sz.lev + k
+                around_e[here, :] = jnp.where(last, to_lane(east_old, p, last_lane), moved_e[here, :])
+                around_w[here, :] = jnp.where(first, to_lane(west_old, p, 0), moved_w[here, :])
+        for k in range(sz.lev):
+            for f in range(sz.nf):
+                here = slice(f * sz.slab + k * sz.rows, f * sz.slab + (k + 1) * sz.rows)
+                p = f * sz.lev + k
+                second[here, :] = jnp.where(first, to_lane(west_new, p, 0), to_lane(east_new, p, last_lane))
+
+
+def finish(
+    sz, fields, levels, south, north, cross_south, cross_north, bulk,
+    side, from_west, from_east, moved_e, moved_w, around_e, around_w, around_n, around_s, second, edge_mix,
+    result, out, div, mix, vert, low_strip, high_strip, ratio, forward, inv_ref, wref, pull, moved, sent,
+):
+    tile = (sz.rows, sz.cols)
+    lane, row = lane_ids(tile), row_ids(tile)
+    last_lane, last_row = sz.cols - 1, sz.rows - 1
+    lev = levels[...].astype(jnp.float32)
+    level_row = LEVEL_ROW * sz.lev
+    side_base = 2 * sz.lev
+    west_side = from_west[2 * sz.rows : 3 * sz.rows, :]
+    east_side = from_east[2 * sz.rows : 3 * sz.rows, :]
+    lev_w = shift_west(lev, lane, to_lane(west_side, side_base, 0))
+    lev_e = shift_east(lev, lane, to_lane(east_side, side_base, last_lane))
+    south_lev, north_lev = cross_south[level_row : level_row + 1, :], cross_north[level_row : level_row + 1, :]
+    lev_s = shift_south(lev, row, south_lev)
+    lev_n = shift_north(lev, row, north_lev)
+
+    def masks(k):
+        wet = lev > k
+        return wet, wet & (lev_e > k), wet & (lev_w > k), wet & (lev_n > k), wet & (lev_s > k)
+
+    is_dynamics = lax.axis_index("sect") == 0
+    chunk = sz.lev // CHUNKS
+    copies = []
+
+    def send(first, last, part):
+        at = pl.ds(part * chunk * sz.rows, chunk * sz.rows)
+        copy = pltpu.make_async_copy(
+            out.at[pl.ds(first, last - first), at, :], result.at[pl.ds(first, last - first), at, :], sent.at[len(copies)]
+        )
+        copy.start()
+        copies.append(copy)
+
+    def finish_copies():
+        for copy in copies:
+            copy.wait()
+        copies.clear()
+
+    def physics():
+        def around(f, k):
+            at = f * sz.slab + k * sz.rows
+            here = slice(at, at + sz.rows)
+            lane_at = f * sz.lev + k
+            return (
+                fields[here, :],
+                jnp.where(lane == last_lane, to_lane(from_east[0 : sz.rows, :], lane_at, last_lane), moved_e[here, :]),
+                jnp.where(lane == 0, to_lane(from_west[0 : sz.rows, :], lane_at, 0), moved_w[here, :]),
+                around_n[here, :],
+                around_s[here, :],
+            )
+
+        press = jnp.zeros(tile, jnp.float32)
+        press_e, press_n, warm_above = press, press, press
+        for k in range(sz.lev):
+            at = k * sz.rows
+            mask = masks(k)
+            wet, wet_e, wet_w, wet_n, wet_s = mask
+            zonal, merid, temper, saline, visc = (around(f, k) for f in range(5))
+            flow_east, flow_west = keep(wet_e, zonal[0]), keep(wet_w, zonal[2])
+            flow_north, flow_south = keep(wet_n, merid[0]), keep(wet_s, merid[4])
+            div[at : at + sz.rows, :] = flow_east - flow_west + (flow_north - flow_south)
+            warm = diffused(temper, visc, mask)
+            mixing = jnp.zeros(tile, jnp.float32)
+            if k > 0:
+                background = fields[5 * sz.slab + at : 5 * sz.slab + at + sz.rows, :]
+                mixing = mixed(warm_above, warm, background, wet)
+            warm_above = warm
+
+            def weight(place, wet_there):
+                return keep(wet_there, HALINE * saline[place] - THERMAL * temper[place])
+
+            press = press + GRAVITY_SCALE * weight(0, wet)
+            press_e = press_e + GRAVITY_SCALE * weight(1, lev_e > k)
+            press_n = press_n + GRAVITY_SCALE * weight(3, lev_n > k)
+            zonal_new = diffused(zonal, visc, mask) + TIME_STEP * (CORIOLIS * merid[0] - (press_e - press))
+            merid_new = diffused(merid, visc, mask) - TIME_STEP * (CORIOLIS * zonal[0] + (press_n - press))
+            saline_new = diffused(saline, visc, mask)
+            parts = (keep(wet_e, zonal_new), keep(wet_n, merid_new), warm, saline_new, None, mixing)
+            for f, part in enumerate(parts):
+                if part is not None:
+                    out[f, at : at + sz.rows, :] = part
+            if k % chunk == chunk - 1:
+                send(0, 4, k // chunk)
+                send(5, 6, k // chunk)
+        total = jnp.zeros(tile, jnp.float32)
+        for k in range(sz.lev - 1, -1, -1):
+            at = k * sz.rows
+            total = total + div[at : at + sz.rows, :]
+            out[4, at : at + sz.rows, :] = -total if k > 0 else jnp.zeros(tile, jnp.float32)
+            if k % chunk == 0:
+                send(4, 5, k // chunk)
+
+    tall = (sz.lev, sz.cols)
 
     def row_strips(step):
         lane16, depth = lane_ids(tall), row_ids(tall).astype(jnp.float32)
@@ -470,60 +634,8 @@
                 up, down = (inside, far) if r == 0 else (far, inside)
                 strip[f * sz.lev : (f + 1) * sz.lev, :] = weights.apply(near, at_e, at_w, up, down)
 
-    def column_strips(step):
-        lane16, depth16 = lane_ids(tall), row_ids(tall)
-
-        def all_fields(value, first):
-            at = lane_ids(value.shape)
-            value = jnp.where((at >= first) & (at < first + sz.lev), value, 0.0)
-            width = sz.lev
-            while width < sz.cols:
-                value = value + turn(value, width, 1)
-                width *= 2
-            return value
-
-        def corner_rows(message, r):
-            items = message[3 * sz.rows : 3 * sz.rows + sz.lev, :]
-            p = r * (sz.nf + 2)
-            tracers = jnp.zeros(tall, jnp.float32)
-            for f in range(sz.nf):
-                spread = jnp.broadcast_to(items[:, p + f : p + f + 1], tall)
-                tracers = jnp.where(lane16 == f * sz.lev + depth16, spread, tracers)
-            spread = jnp.broadcast_to(items[:, p + sz.nf + 1 : p + sz.nf + 2], tall)
-            velocity = jnp.where(lane16 % sz.lev == depth16, spread, 0.0)
-            return jnp.sum(tracers, axis=0, keepdims=True), jnp.sum(velocity, axis=0, keepdims=True)
-
-        inside_w, inside_e = own_west[0 : sz.rows, :], own_east[0 : sz.rows, :]
-        near = both(from_west[0 : sz.rows, :], from_east[0 : sz.rows, :])
-        far_w, far_e = from_west[sz.rows : 2 * sz.rows, :], from_east[sz.rows : 2 * sz.rows, :]
-        corners = [corner_rows(message, r) for message in (from_west, from_east) for r in range(2)]
-        low_tracers, high_tracers, low_merid = (
-            both(jnp.broadcast_to(corners[i][part], tile), jnp.broadcast_to(corners[i + 2][part], tile))
-            for i, part in ((0, 0), (1, 0), (0, 1))
-        )
-
-        def side_levels(at):
-            return column(west_side, at), column(east_side, at)
-
-        near_lev = both(*side_levels(side_base))
-        far_lev_w, far_lev_e = side_levels(side_base + 1)
-        own_lev_w, own_lev_e = column(lev, 0), column(lev, last_lane)
-        lev_at_s = pair_south(near_lev, both(*side_levels(side_base + 2)))
-        lev_at_n = pair_north(near_lev, both(*side_levels(side_base + 3)))
-        depth = (lane_ids(near.shape) % sz.lev).astype(jnp.float32)
-        wet_near = near_lev > depth
-        zonal_first = sz.nf * sz.lev
-        west, east = both(far_w, inside_e), both(inside_w, far_e)
-        flow_e = keep(wet_near & (both(own_lev_w, far_lev_e) > depth), all_fields(near, zonal_first))
-        flow_w = keep(wet_near & (both(far_lev_w, own_lev_e) > depth), all_fields(west, zonal_first))
-        merid = all_fields(near, zonal_first + sz.lev)
-        flow_n = keep(wet_near & (lev_at_n > depth), merid)
-        flow_s = keep(wet_near & (lev_at_s > depth), pair_south(merid, low_merid))
-        weights = Weights(flow_e, flow_w, flow_n, flow_s, step)
-        side_strips[...] = weights.apply(near, east, west, pair_north(near, high_tracers), pair_south(near, low_tracers))
-
     def transport(step):
-        west_old, east_old = from_west[0 : sz.rows, :], from_east[0 : sz.rows, :]
+        west_old = from_west[0 : sz.rows, :]
         zero = jnp.zeros(tile, jnp.float32)
 
         def faces(k):
@@ -538,22 +650,6 @@
         def stored_weights(k):
             at = k * sz.rows
             return Weights.of(*(wref[i * sz.slab + at : i * sz.slab + at + sz.rows, :] for i in range(5)))
-
-        def substep(weights, values, k, west, east, lows, highs):
-            to_e = [turn(value, -1, 1) for value in values]
-            to_w = [turn(value, 1, 1) for value in values]
-            edge_e = [to_lane(east, f * sz.lev + k, last_lane) for f in every]
-            edge_w = [to_lane(west, f * sz.lev + k, 0) for f in every]
-            return [
-                weights.apply(
-                    values[f],
-                    jnp.where(lane == last_lane, edge_e[f], to_e[f]),
-                    jnp.where(lane == 0, edge_w[f], to_w[f]),
-                    shift_north(values[f], row, highs[f]),
-                    shift_south(values[f], row, lows[f]),
-                )
-                for f in every
-            ]
 
         for k in range(sz.lev):
             at = k * sz.rows
@@ -572,28 +668,21 @@
             weights = Weights(flow_e, flow_w, flow_n, flow_s, step)
             for i, part in enumerate(weights.parts()):
                 wref[i * sz.slab + at : i * sz.slab + at + sz.rows, :] = part
-        column_strips(step)
         row_strips(step)
-        west_new, east_new = side_strips[0 : sz.rows, :], side_strips[sz.rows : 2 * sz.rows, :]
         for k in range(sz.lev):
             at = k * sz.rows
             weights = stored_weights(k)
-            values = [fields[f * sz.slab + at : f * sz.slab + at + sz.rows, :] for f in every]
-            lows = [south[2 * f * sz.lev + k : 2 * f * sz.lev + k + 1, :] for f in every]
-            highs = [north[2 * f * sz.lev + k : 2 * f * sz.lev + k + 1, :] for f in every]
-            values = substep(weights, values, k, west_old, east_old, lows, highs)
             for f in every:
-                forward[f * sz.slab + at : f * sz.slab + at + sz.rows, :] = values[f]
-        edges = edge_mixing()
-        edge_w, edge_e = edges[0 : sz.rows, :], edges[sz.rows : 2 * sz.rows, :]
+                here = slice(f * sz.slab + at, f * sz.slab + at + sz.rows)
+                forward[here, :] = weights.apply(*(ref[here, :] for ref in (fields, around_e, around_w, around_n, around_s)))
+        at_edge = (lane == 0) | (lane == last_lane)
         total = zero
         for k in range(sz.lev - 1, -1, -1):
             at = k * sz.rows
             total = total + div[at : at + sz.rows, :]
             vert[at : at + sz.rows, :] = -total if k > 0 else zero
             mixing = bulk[sz.slab + at : sz.slab + at + sz.rows, :]
-            mixing = jnp.where(lane == 0, to_lane(edge_w, k, 0), mixing)
-            mix[at : at + sz.rows, :] = jnp.where(lane == last_lane, to_lane(edge_e, k, last_lane), mixing)
+            mix[at : at + sz.rows, :] = jnp.where(at_edge, edge_mix[at : at + sz.rows, :], mixing)
         last_ratio = None
         up, down = faces(0)
         lower, inverse = [], []
@@ -615,11 +704,19 @@
             at = k * sz.rows
             weights = stored_weights(k)
             values = [forward[f * sz.slab + at : f * sz.slab + at + sz.rows, :] for f in every]
-            lows = [low_strip[f * sz.lev + k : f * sz.lev + k + 1, :] for f in every]
-            highs = [high_strip[f * sz.lev + k : f * sz.lev + k + 1, :] for f in every]
-            values = substep(weights, values, k, west_new, east_new, lows, highs)
+            to_e, to_w = [turn(value, -1, 1) for value in values], [turn(value, 1, 1) for value in values]
             for f in every:
-                moved[f * sz.slab + at : f * sz.slab + at + sz.rows, :] = values[f] * inv_ref[at : at + sz.rows, :]
+                here = slice(f * sz.slab + at, f * sz.slab + at + sz.rows)
+                beyond = slice(f * sz.lev + k, f * sz.lev + k + 1)
+                edge = second[here, :]
+                value = weights.apply(
+                    values[f],
+                    jnp.where(lane == last_lane, edge, to_e[f]),
+                    jnp.where(lane == 0, edge, to_w[f]),
+                    shift_north(values[f], row, high_strip[beyond, :]),
+                    shift_south(values[f], row, low_strip[beyond, :]),
+                )
+                moved[here, :] = value * inv_ref[at : at + sz.rows, :]
         for k in range(sz.lev):
             at = k * sz.rows
             for f in every:
@@ -636,15 +733,19 @@
                 here = f * sz.slab + at
                 if k < sz.lev - 1:
                     previous[f] = forward[here : here + sz.rows, :] - ratio[at : at + sz.rows, :] * previous[f]
-                out[here : here + sz.rows, :] = keep(wet, previous[f])
+                out[f, at : at + sz.rows, :] = keep(wet, previous[f])
+            if k % chunk == 0:
+                send(0, sz.nf, k // chunk)
 
     @pl.when(is_dynamics)
     def _():
         physics()
+        finish_copies()
 
     @pl.when(jnp.logical_not(is_dynamics))
     def _():
         transport(TIME_STEP / NSUB)
+        finish_copies()
 
 
 def pair_of(index, count, odd):
@@ -692,32 +793,51 @@
 
     rows_shape = (2 * sz.nf * sz.lev, sz.cols)
     cross_shape = (LEVEL_ROW * sz.lev + 8, sz.cols)
-    columns_shape = (3 * sz.rows + sz.lev, sz.cols)
+    columns_shape = (4 * sz.rows + sz.lev, sz.cols)
     side_shape = (4 * sz.rows, sz.cols)
     row_a, row_b, own_side = call_kernel(functools.partial(pack_edges, sz), [rows_shape, rows_shape, side_shape], [flat])
-    (cross_b,) = call_kernel(functools.partial(pack_cross, sz), [cross_shape], [flat, levels])
+    twin_shape = (zonal_place(sz) + early(sz), sz.cols)
+    wide_shape = (max(cross_shape[0], twin_shape[0] + 8), sz.cols)
+    (cross_b,) = call_kernel(functools.partial(pack_cross, sz), [wide_shape], [flat, levels])
     row_a = swap(row_a, False)
     levels_a = swap(levels, False)
     row_b = swap(row_b, True)
     (twin,) = call_kernel(
-        functools.partial(pack_twin, sz), [(zonal_place(sz) + early(sz), sz.cols)], [flat, own_side, row_a]
+        functools.partial(pack_twin, sz), [twin_shape], [flat, own_side, row_a]
     )
     twin = from_dynamics(twin)
     cross_b = from_dynamics(cross_b, True)
-    to_east, to_west, south, north, cross_south, cross_north, bulk = call_kernel(
+    south, north, corners = call_kernel(
+        functools.partial(place_rows, sz), [rows_shape, rows_shape, (sz.rows, sz.cols)], [row_a, row_b]
+    )
+    to_east, to_west, cross_south, cross_north, bulk = call_kernel(
         functools.partial(pack_columns, sz),
-        [columns_shape] * 2 + [rows_shape] * 2 + [cross_shape] * 2 + [(3 * sz.slab - early(sz), sz.cols)],
-        [flat, levels, levels_a, row_a, row_b, twin, cross_b, own_side],
+        [columns_shape] * 2 + [cross_shape] * 2 + [(3 * sz.slab - early(sz), sz.cols)],
+        [flat, levels, levels_a, south, north, corners, twin, cross_b, own_side],
     )
     bulk = from_dynamics(bulk)
     from_east = around(to_west, -1)
     from_west = around(to_east, 1)
+    kept, moved_e, moved_w, around_n, around_s = call_kernel(
+        functools.partial(shift_fields, sz), [flat.shape] * 5, [flat, south, north]
+    )
     slab = (sz.slab, sz.cols)
+    around_e, around_w, second, edge_mix = call_kernel(
+        functools.partial(column_edges, sz),
+        [flat.shape] * 3 + [slab],
+        [levels, cross_south, cross_north, to_east, to_west, twin, from_west, from_east, moved_e, moved_w],
+    )
+    out_shape = (sz.nf, sz.slab, sz.cols)
+    strip = (sz.nf * sz.lev, sz.cols)
     (out,) = call_kernel(
         functools.partial(finish, sz),
-        [flat.shape],
-        [flat, levels, south, north, cross_south, cross_north, bulk, to_east, to_west, twin, from_west, from_east],
-        [slab, slab, slab, (sz.nf * sz.lev, sz.cols), (sz.nf * sz.lev, sz.cols), (2 * sz.rows, sz.cols), slab, flat.shape, slab, (5 * sz.slab, sz.cols), slab, flat.shape],
+        [out_shape],
+        [
+            kept, levels, south, north, cross_south, cross_north, bulk, twin, from_west, from_east,
+            moved_e, moved_w, around_e, around_w, around_n, around_s, second, edge_mix,
+        ],
+        [out_shape, slab, slab, slab, strip, strip, slab, flat.shape, slab, (5 * sz.slab, sz.cols), slab, flat.shape],
+        copies=3 * CHUNKS,
     )
     return out.reshape(fields.shape)
 

time: 18.3 us -> 18.1 us (0.989)
  Pallas kernels: 1.88 us -> 2.25 us
  waiting for transfers between devices: 4.75 us -> 4.43 us
  starting transfers between devices: 10.5 us -> 10.2 us
    ppermute x4, starting transfers between devices: 4.49 us -> 3.5 us  [swap(): return lax.ppermute(value, ('sect', 'lon', 'lat'), pairs)]
    ppermute x2, waiting for transfers between devices: 0.07 us -> 0.8 us  [from_dynamics(): lax.ppermute(value, 'sect', [(s, (s + hop) % count_s) for s in range(coun...]
    ppermute x2, starting transfers between devices: 2.19 us -> 2.86 us  [from_dynamics(): lax.ppermute(value, 'sect', [(s, (s + hop) % count_s) for s in range(coun...]
    ppermute x4, waiting for transfers between devices: 2.73 us -> 2.07 us  [swap(): return lax.ppermute(value, ('sect', 'lon', 'lat'), pairs)]
    ppermute x2, waiting for transfers between devices: 1.95 us -> 1.56 us  [around(): lax.ppermute(value, 'lon', [(i, (i + step) % count_o) for i in range(coun...]
    pallas_call x5 -> x8, Pallas kernels: 1.88 us -> 2.25 us  [call_kernel(): pl.pallas_call(body, out_shape=[jax.ShapeDtypeStruct(shape, jnp.float32)...]
    unnamed x4 -> x6, local copies, waits for them, and re-layouts: 1 us -> 1.01 us
  transfers between devices with their start and end apart: 8 -> 8, of which waited for: 5 -> 6; matrix products, arithmetic and copies ran while one was open for 0% -> 0% of each run, Pallas kernels for 0% -> 3%
where the time goes in v4:
time: 18.1 us; the launch traced here: 17.9 us
  starting transfers between devices  10.2 us (56%)
  waiting for transfers between devices  4.43 us (24%)
  Pallas kernels  2.25 us (12%)
  local copies, waits for them, and re-layouts  1.01 us (6%)
    ppermute x2, starting transfers between devices, around(): lax.ppermute(value, 'lon', [(i, (i + step) % count_o) for i in range(coun...  3.82 us
    ppermute x4, starting transfers between devices, swap(): return lax.ppermute(value, ('sect', 'lon', 'lat'), pairs)  3.5 us
    ppermute x2, starting transfers between devices, from_dynamics(): lax.ppermute(value, 'sect', [(s, (s + hop) % count_s) for s in range(coun...  2.86 us
    pallas_call x8, Pallas kernels, call_kernel(): pl.pallas_call(body, out_shape=[jax.ShapeDtypeStruct(shape, jnp.float32)...  2.25 us
    ppermute x4, waiting for transfers between devices, swap(): return lax.ppermute(value, ('sect', 'lon', 'lat'), pairs)  2.07 us
    ppermute x2, waiting for transfers between devices, around(): lax.ppermute(value, 'lon', [(i, (i + step) % count_o) for i in range(coun...  1.56 us
    unnamed x6, local copies, waits for them, and re-layouts  1.01 us
    ppermute x2, waiting for transfers between devices, from_dynamics(): lax.ppermute(value, 'sect', [(s, (s + hop) % count_s) for s in range(coun...  0.8 us
  transfers between devices with their start and end apart: 8, of which 6 were waited for; matrix products, arithmetic and copies ran while one was open for 0% of the time, Pallas kernels for 3%

profile of v4, /device:TPU:0, one launch (start us, length us, event | category | flops | bytes accessed | tf_op | source)
XLA Modules:
  0.0 17.9 jit_solution(2656906146022524834)
XLA Ops:
  0.0 0.0 copy-start
  0.0 1.0 %copy-done = f32[1,6,16,8,128]{4,3,2,1,0:T(8,128)S(1)} copy-done((f32[1,6,16,8,128]{4,3,2,1,0:T(8,128)S(1)}, f32[1,6,16,8,128]{4,3,2,1,0:T(8,128)}, u32[]{:S(2)}) %copy-start) | copy-done | bytes 393240
  1.0 0.0 copy-start.2
  1.0 0.3 %shard_map.28 = (f32[192,128]{1,0:T(8,128)S(1)}, f32[192,128]{1,0:T(8,128)S(1)}, f32[32,128]{1,0:T(8,128)S(1)}) custom-call(f32[768,128]{1,0:T(8,128)S(1)} %bitcast.2), custom_call_target="tpu_custom_call" | custom-call | tf_op jit(solution)/shard_map/pallas_call | solution.py:30
  1.3 0.5 %collective-permute-start = (f32[192,128]{1,0:T(8,128)S(1)}, f32[192,128]{1,0:T(8,128)S(1)}, u32[]{:S(2)}, u32[]{:S(2)}) collective-permute-start(f32[192,128]{1,0:T(8,128)S(1)} %get-tuple-element.25), channel_id=1, source_target_pairs={{0,1},{1,0},{2,3},{3,2},{4,5},{5,4},{6,7},{7,6},{8,9},{9,8},{10,11... | collective-permute-start | bytes 294920 | tf_op jit(solution)/shard_map/ppermute | solution.py:778
  1.7 2.6 %collective-permute-start.1 = (f32[192,128]{1,0:T(8,128)S(1)}, f32[192,128]{1,0:T(8,128)S(1)}, u32[]{:S(2)}, u32[]{:S(2)}) collective-permute-start(f32[192,128]{1,0:T(8,128)S(1)} %get-tuple-element.26), channel_id=1, source_target_pairs={{0,4},{1,2},{2,1},{3,7},{4,0},{5,6},{6,5},{7,3},{8,12},{9,10},{10,... | collective-permute-start | bytes 294920 | tf_op jit(solution)/shard_map/ppermute | solution.py:778
  4.4 0.0 copy-done.2
  4.4 0.0 copy-start.1
  4.4 0.4 %collective-permute-start.4 = (f32[120,128]{1,0:T(8,128)S(1)}, f32[120,128]{1,0:T(8,128)S(1)}, u32[]{:S(2)}, u32[]{:S(2)}) collective-permute-start(f32[120,128]{1,0:T(8,128)S(1)} %shard_map.32), channel_id=1, source_target_pairs={{0,4},{1,18},{2,17},{3,7},{4,0},{5,22},{6,21},{7,3},{8,12},{9,26},... | collective-permute-start | bytes 184328 | tf_op jit(solution)/shard_map/ppermute | solution.py:778
  4.8 0.0 collective-permute-done.row_a
  4.8 1.7 %collective-permute-start.3 = (f32[112,128]{1,0:T(8,128)S(1)}, f32[112,128]{1,0:T(8,128)S(1)}, u32[]{:S(2)}, u32[]{:S(2)}) collective-permute-start(f32[112,128]{1,0:T(8,128)S(1)} %shard_map.31), channel_id=1, source_target_pairs={{0,16},{16,0},{1,17},{17,1},{2,18},{18,2},{3,19},{19,3},{4,20},{20... | collective-permute-start | bytes 172040 | tf_op jit(solution)/shard_map/ppermute | solution.py:785
  6.5 0.0 collective-permute-start.2
  6.5 0.5 %collective-permute-done.1.row_b = f32[192,128]{1,0:T(8,128)S(1)} collective-permute-done((f32[192,128]{1,0:T(8,128)S(1)}, f32[192,128]{1,0:T(8,128)S(1)}, u32[]{:S(2)}, u32[]{:S(2)}) %collective-permute-start.1) | collective-permute-done | bytes 98336 | tf_op jit(solution)/shard_map/ppermute | solution.py:778
  7.0 0.1 shard_map.29
  7.1 0.6 %collective-permute-done.2.levels_a = s32[8,128]{1,0:T(8,128)S(1)} collective-permute-done((s32[8,128]{1,0:T(8,128)S(1)}, s32[8,128]{1,0:T(8,128)S(1)}, u32[]{:S(2)}, u32[]{:S(2)}) %collective-permute-start.2) | collective-permute-done | bytes 4128 | tf_op jit(solution)/shard_map/ppermute | solution.py:778
  7.7 1.0 %collective-permute-done.4.cross_b = f32[120,128]{1,0:T(8,128)S(1)} collective-permute-done((f32[120,128]{1,0:T(8,128)S(1)}, f32[120,128]{1,0:T(8,128)S(1)}, u32[]{:S(2)}, u32[]{:S(2)}) %collective-permute-start.4) | collective-permute-done | bytes 61472 | tf_op jit(solution)/shard_map/ppermute | solution.py:778
  8.7 0.7 %collective-permute-done.3.twin.side = f32[112,128]{1,0:T(8,128)S(1)} collective-permute-done((f32[112,128]{1,0:T(8,128)S(1)}, f32[112,128]{1,0:T(8,128)S(1)}, u32[]{:S(2)}, u32[]{:S(2)}) %collective-permute-start.3) | collective-permute-done | bytes 57376 | tf_op jit(solution)/shard_map/ppermute | solution.py:785
  9.4 0.0 copy-done.1
  9.4 0.3 %shard_map.33 = (f32[48,128]{1,0:T(8,128)S(1)}, f32[48,128]{1,0:T(8,128)S(1)}, f32[88,128]{1,0:T(8,128)S(1)}, f32[88,128]{1,0:T(8,128)S(1)}, f32[384,128]{1,0:T(8,128)S(1)}) custom-call(f32[768,128]{1,0:T(8,128)S(1)} %bitcast.5, s32[8,128]{1,0:T(8,128)S(1)} %copy-done.2, s32[8,128]{1,0:T(8,128)S(1)} %collective-permute-done.2.levels_a, ...), custom_call_target="tpu_custom_call" | custom-call | tf_op jit(solution)/shard_map/pallas_call | solution.py:30
  9.8 1.2 %collective-permute-start.5 = (f32[384,128]{1,0:T(8,128)S(1)}, f32[384,128]{1,0:T(8,128)S(1)}, u32[]{:S(2)}, u32[]{:S(2)}) collective-permute-start(f32[384,128]{1,0:T(8,128)S(1)} %get-tuple-element.34), channel_id=1, source_target_pairs={{0,16},{16,0},{1,17},{17,1},{2,18},{18,2},{3,19},{19,3},{4,20},{20... | collective-permute-start | bytes 589832 | tf_op jit(solution)/shard_map/ppermute | solution.py:785
  11.0 1.6 %collective-permute-start.6 = (f32[48,128]{1,0:T(8,128)S(1)}, f32[48,128]{1,0:T(8,128)S(1)}, u32[]{:S(2)}, u32[]{:S(2)}) collective-permute-start(f32[48,128]{1,0:T(8,128)S(1)} %get-tuple-element.35.own_east), channel_id=1, source_target_pairs={{0,4},{4,8},{8,12},{12,0},{1,5},{5,9},{9,13},{13,1},{2,6},{6,10},{... | collective-permute-start | bytes 73736 | tf_op jit(solution)/shard_map/ppermute | solution.py:792
  12.5 2.2 %collective-permute-start.7 = (f32[48,128]{1,0:T(8,128)S(1)}, f32[48,128]{1,0:T(8,128)S(1)}, u32[]{:S(2)}, u32[]{:S(2)}) collective-permute-start(f32[48,128]{1,0:T(8,128)S(1)} %get-tuple-element.36.own_west), channel_id=1, source_target_pairs={{0,12},{4,0},{8,4},{12,8},{1,13},{5,1},{9,5},{13,9},{2,14},{6,2},{... | collective-permute-start | bytes 73736 | tf_op jit(solution)/shard_map/ppermute | solution.py:792
  14.8 0.3 %shard_map.30 = (f32[768,128]{1,0:T(8,128)S(1)}, f32[768,128]{1,0:T(8,128)S(1)}, f32[768,128]{1,0:T(8,128)S(1)}, f32[768,128]{1,0:T(8,128)S(1)}, f32[768,128]{1,0:T(8,128)S(1)}) custom-call(f32[768,128]{1,0:T(8,128)S(1)} %bitcast.6, f32[192,128]{1,0:T(8,128)S(1)} %get-tuple-element.27.south, f32[192,128]{1,0:T(8,128)S(1)} %get-tuple-element.28.north), custom_call_target="tpu_custom_call" | custom-call | tf_op jit(solution)/shard_map/pallas_call | solution.py:30
  15.1 1.6 %collective-permute-done.6.from_west = f32[48,128]{1,0:T(8,128)S(1)} collective-permute-done((f32[48,128]{1,0:T(8,128)S(1)}, f32[48,128]{1,0:T(8,128)S(1)}, u32[]{:S(2)}, u32[]{:S(2)}) %collective-permute-start.6) | collective-permute-done | bytes 24608 | tf_op jit(solution)/shard_map/ppermute | solution.py:792
  16.6 0.0 collective-permute-done.7.from_east
  16.6 0.1 shard_map.34
  16.7 0.1 collective-permute-done.5.bulk
  16.8 1.2 %shard_map.35 = f32[6,128,128]{2,1,0:T(8,128)} custom-call(f32[768,128]{1,0:T(8,128)S(1)} %get-tuple-element.29.fields, s32[8,128]{1,0:T(8,128)S(1)} %copy-done.2, f32[192,128]{1,0:T(8,128)S(1)} %get-tuple-element.27.south, f32[192,128]{1,0:T(8,128)S(1)} %get-tuple-element.28.north, f32[88,128]{1,0:T(8,128)S(1)} %get-tuple-element.32.cross_south, ...), custom_call_target="tpu_custom_call" | custom-call | tf_op jit(solution)/shard_map/pallas_call | solution.py:30
  (2 shorter events, 0.0 us)
Async XLA Ops:
  0.0 1.0 %copy-start = (f32[1,6,16,8,128]{4,3,2,1,0:T(8,128)S(1)}, f32[1,6,16,8,128]{4,3,2,1,0:T(8,128)}, u32[]{:S(2)}) copy-start(f32[1,6,16,8,128]{4,3,2,1,0:T(8,128)} %param.2) | copy-start | bytes 1179652
  1.0 3.4 %copy-start.2 = (s32[8,128]{1,0:T(8,128)S(1)}, s32[8,128]{1,0:T(8,128)}, u32[]{:S(2)}) copy-start(s32[8,128]{1,0:T(8,128)} %levels.7) | copy-start | bytes 12292
  1.3 3.5 %collective-permute-start = (f32[192,128]{1,0:T(8,128)S(1)}, f32[192,128]{1,0:T(8,128)S(1)}, u32[]{:S(2)}, u32[]{:S(2)}) collective-permute-start(f32[192,128]{1,0:T(8,128)S(1)} %get-tuple-element.25), channel_id=1, source_target_pairs={{0,1},{1,0},{2,3},{3,2},{4,5},{5,4},{6,7},{7,6},{8,9},{9,8},{10,11... | collective-permute-start | bytes 294920 | tf_op jit(solution)/shard_map/ppermute | solution.py:778
  1.7 5.2 %collective-permute-start.1 = (f32[192,128]{1,0:T(8,128)S(1)}, f32[192,128]{1,0:T(8,128)S(1)}, u32[]{:S(2)}, u32[]{:S(2)}) collective-permute-start(f32[192,128]{1,0:T(8,128)S(1)} %get-tuple-element.26), channel_id=1, source_target_pairs={{0,4},{1,2},{2,1},{3,7},{4,0},{5,6},{6,5},{7,3},{8,12},{9,10},{10,... | collective-permute-start | bytes 294920 | tf_op jit(solution)/shard_map/ppermute | solution.py:778
  4.4 5.0 %copy-start.1 = (f32[1,6,16,8,128]{4,3,2,1,0:T(8,128)S(1)}, f32[1,6,16,8,128]{4,3,2,1,0:T(8,128)}, u32[]{:S(2)}) copy-start(f32[1,6,16,8,128]{4,3,2,1,0:T(8,128)} %param.2) | copy-start | bytes 1179652
  4.4 4.3 %collective-permute-start.4 = (f32[120,128]{1,0:T(8,128)S(1)}, f32[120,128]{1,0:T(8,128)S(1)}, u32[]{:S(2)}, u32[]{:S(2)}) collective-permute-start(f32[120,128]{1,0:T(8,128)S(1)} %shard_map.32), channel_id=1, source_target_pairs={{0,4},{1,18},{2,17},{3,7},{4,0},{5,22},{6,21},{7,3},{8,12},{9,26},... | collective-permute-start | bytes 184328 | tf_op jit(solution)/shard_map/ppermute | solution.py:778
  4.8 4.6 %collective-permute-start.3 = (f32[112,128]{1,0:T(8,128)S(1)}, f32[112,128]{1,0:T(8,128)S(1)}, u32[]{:S(2)}, u32[]{:S(2)}) collective-permute-start(f32[112,128]{1,0:T(8,128)S(1)} %shard_map.31), channel_id=1, source_target_pairs={{0,16},{16,0},{1,17},{17,1},{2,18},{18,2},{3,19},{19,3},{4,20},{20... | collective-permute-start | bytes 172040 | tf_op jit(solution)/shard_map/ppermute | solution.py:785
  6.5 1.2 %collective-permute-start.2 = (s32[8,128]{1,0:T(8,128)S(1)}, s32[8,128]{1,0:T(8,128)S(1)}, u32[]{:S(2)}, u32[]{:S(2)}) collective-permute-start(s32[8,128]{1,0:T(8,128)S(1)} %copy-done.2), channel_id=1, source_target_pairs={{0,1},{1,0},{2,3},{3,2},{4,5},{5,4},{6,7},{7,6},{8,9},{9,8},{10,11... | collective-permute-start | bytes 12296 | tf_op jit(solution)/shard_map/ppermute | solution.py:778
  9.8 7.0 %collective-permute-start.5 = (f32[384,128]{1,0:T(8,128)S(1)}, f32[384,128]{1,0:T(8,128)S(1)}, u32[]{:S(2)}, u32[]{:S(2)}) collective-permute-start(f32[384,128]{1,0:T(8,128)S(1)} %get-tuple-element.34), channel_id=1, source_target_pairs={{0,16},{16,0},{1,17},{17,1},{2,18},{18,2},{3,19},{19,3},{4,20},{20... | collective-permute-start | bytes 589832 | tf_op jit(solution)/shard_map/ppermute | solution.py:785
  11.0 5.7 %collective-permute-start.6 = (f32[48,128]{1,0:T(8,128)S(1)}, f32[48,128]{1,0:T(8,128)S(1)}, u32[]{:S(2)}, u32[]{:S(2)}) collective-permute-start(f32[48,128]{1,0:T(8,128)S(1)} %get-tuple-element.35.own_east), channel_id=1, source_target_pairs={{0,4},{4,8},{8,12},{12,0},{1,5},{5,9},{9,13},{13,1},{2,6},{6,10},{... | collective-permute-start | bytes 73736 | tf_op jit(solution)/shard_map/ppermute | solution.py:792
  12.5 4.1 %collective-permute-start.7 = (f32[48,128]{1,0:T(8,128)S(1)}, f32[48,128]{1,0:T(8,128)S(1)}, u32[]{:S(2)}, u32[]{:S(2)}) collective-permute-start(f32[48,128]{1,0:T(8,128)S(1)} %get-tuple-element.36.own_west), channel_id=1, source_target_pairs={{0,12},{4,0},{8,4},{12,8},{1,13},{5,1},{9,5},{13,9},{2,14},{6,2},{... | collective-permute-start | bytes 73736 | tf_op jit(solution)/shard_map/ppermute | solution.py:792

commit v5 on v4

--- a/solution.py
+++ b/solution.py
@@ -19,7 +19,8 @@
 CHUNKS = 4
 EARLY_LEVELS = 0
 
-ZONAL_ROW, MERID_ROW, MERID_ROW2, TEMPER_ROW, VISC_ROW, LEVEL_ROW = range(6)
+ZONAL_ROW, MERID_ROW, MERID_ROW2, END_ROW, LEVEL_ROW = range(5)
+TEMPER_END, VISC_END = 0, 2
 
 
 def call_kernel(body, outputs, inputs, scratch=(), copies=0):
@@ -81,7 +82,10 @@
         fill(1, top, second)
 
 
-def pack_edges(sz, fields, row_a, row_b, side):
+def pack_edges(sz, fields, row_a, row_b, side, zonal, merid):
+    zonal[...] = fields[0 : sz.slab, :]
+    merid[...] = fields[sz.slab : 2 * sz.slab, :]
+
     def fill(which, near, far):
         message = (row_a, row_b)[which]
         for f in range(sz.nf):
@@ -100,8 +104,11 @@
     def fill(which, near, far):
         if which == 0:
             return
-        for at, (f, row) in enumerate(((0, near), (1, near), (1, far), (2, near), (4, near))):
+        for at, (f, row) in enumerate(((0, near), (1, near), (1, far))):
             cross[at * sz.lev : (at + 1) * sz.lev, :] = level_rows(fields, f * sz.slab, row, sz)
+        cross[END_ROW * sz.lev : (END_ROW + 1) * sz.lev, :] = row_ends(
+            level_rows(fields, 2 * sz.slab, near, sz), level_rows(fields, 4 * sz.slab, near, sz)
+        )
         at = LEVEL_ROW * sz.lev
         cross[at : at + 1, :] = lev[near : near + 1, :]
         cross[at + 1 : at + 2, :] = lev[far : far + 1, :]
@@ -110,12 +117,23 @@
     send_north_first(sz, fill)
 
 
+def row_ends(temper, visc):
+    lane = lane_ids(temper.shape)
+    ends = jnp.where(lane == TEMPER_END, temper, turn(temper, TEMPER_END + 2, 1))
+    ends = jnp.where(lane == VISC_END, turn(visc, VISC_END, 1), ends)
+    return jnp.where(lane == VISC_END + 1, turn(visc, VISC_END + 2, 1), ends)
+
+
 def pack_twin(sz, fields, own_side, row_a, twin):
     base = 4 * sz.rows
     twin[0:base, :] = own_side[...]
-    for at, (f, r) in enumerate(((0, 0), (1, 0), (1, 1), (2, 0), (4, 0))):
+    def row_of(f, r):
         first = (2 * f + r) * sz.lev
-        twin[base + at * sz.lev : base + (at + 1) * sz.lev, :] = row_a[first : first + sz.lev, :]
+        return row_a[first : first + sz.lev, :]
+
+    parts = (row_of(0, 0), row_of(1, 0), row_of(1, 1), row_ends(row_of(2, 0), row_of(4, 0)))
+    for at, part in enumerate(parts):
+        twin[base + at * sz.lev : base + (at + 1) * sz.lev, :] = part
     if early(sz):
         twin[zonal_place(sz) : zonal_place(sz) + early(sz), :] = fields[0 : early(sz), :]
 
@@ -170,9 +188,57 @@
     corners[len(ends) :, :] = jnp.zeros((sz.rows - len(ends), sz.cols), jnp.float32)
 
 
+def beside_levels(sz, levels_a, cross_b):
+    even = lax.axis_index("lat") % 2 == 0
+    partner = levels_a[...].astype(jnp.float32)
+    level_row = LEVEL_ROW * sz.lev
+
+    def row_at(low, high):
+        return jnp.where(even, partner[low : low + 1, :], partner[high : high + 1, :])
+
+    near_b, far_b = (cross_b[level_row + i : level_row + i + 1, :] for i in range(2))
+    return row_at(0, sz.rows - 1), row_at(1, sz.rows - 2), near_b, far_b
+
+
+def pack_mixing(sz, fields, levels, levels_a, cross_b, south, north, mixing_out):
+    position = lax.axis_index("lat")
+    even = position % 2 == 0
+    near_a, _, near_b, _ = beside_levels(sz, levels_a, cross_b)
+    south_lev = jnp.where(position > 0, jnp.where(even, near_b, near_a), 0.0)
+    north_lev = jnp.where(position < lax.axis_size("lat") - 1, jnp.where(even, near_a, near_b), 0.0)
+    tile = (sz.rows, sz.cols)
+    lev = levels[...].astype(jnp.float32)
+
+    @pl.when(lax.axis_index("sect") == 0)
+    def _():
+        row = row_ids(tile)
+        lev_e, lev_w = turn(lev, -1, 1), turn(lev, 1, 1)
+        lev_n, lev_s = shift_north(lev, row, north_lev), shift_south(lev, row, south_lev)
+        warm_above = None
+        for k in range(sz.lev):
+            at = k * sz.rows
+
+            def around(f):
+                value = fields[f * sz.slab + at : f * sz.slab + at + sz.rows, :]
+                beyond = 2 * f * sz.lev + k
+                return (
+                    value, turn(value, -1, 1), turn(value, 1, 1),
+                    shift_north(value, row, north[beyond : beyond + 1, :]),
+                    shift_south(value, row, south[beyond : beyond + 1, :]),
+                )
+
+            wet = lev > k
+            masks = wet, wet & (lev_e > k), wet & (lev_w > k), wet & (lev_n > k), wet & (lev_s > k)
+            warm = diffused(around(2), around(4), masks)
+            background = fields[5 * sz.slab + at : 5 * sz.slab + at + sz.rows, :]
+            mixing = jnp.zeros(tile, jnp.float32) if k == 0 else mixed(warm_above, warm, background, wet)
+            warm_above = warm
+            mixing_out[at : at + sz.rows, :] = mixing
+
+
 def pack_columns(
-    sz, fields, levels, levels_a, south, north, corners, twin, cross_b, own_side,
-    to_east, to_west, cross_south, cross_north, bulk,
+    sz, levels, levels_a, south, north, corners, twin, cross_b, own_side,
+    to_east, to_west, cross_south, cross_north,
 ):
     position = lax.axis_index("lat")
     even = position % 2 == 0
@@ -183,12 +249,7 @@
     last = sz.cols - 1
     side = twin
     level_row = LEVEL_ROW * sz.lev
-    near_a = levels_a[...].astype(jnp.float32)
-    top, second = sz.rows - 1, sz.rows - 2
-    near_a, far_a = (
-        jnp.where(even, near_a[low : low + 1, :], near_a[high : high + 1, :]) for low, high in ((0, top), (1, second))
-    )
-    near_b, far_b = (cross_b[level_row + i : level_row + i + 1, :] for i in range(2))
+    near_a, far_a, near_b, far_b = beside_levels(sz, levels_a, cross_b)
     pairs = (
         (cross_south, cross_north, slice(0, level_row), twin[4 * sz.rows : 4 * sz.rows + level_row, :], cross_b[0:level_row, :]),
         (cross_south, cross_north, slice(level_row, level_row + 1), near_a, near_b),
@@ -200,8 +261,6 @@
     for ref in (cross_south, cross_north):
         ref[level_row + 2 : level_row + 8, :] = jnp.zeros((6, sz.cols), jnp.float32)
 
-    bulk[0 : sz.slab, :] = fields[sz.slab : 2 * sz.slab, :]
-    bulk[2 * sz.slab : 3 * sz.slab - early(sz), :] = fields[early(sz) : sz.slab, :]
     tracer_lanes = lane < sz.nf * sz.lev
     for place, (message, at) in enumerate(((to_east, 0), (to_west, 0), (to_east, sz.rows), (to_west, sz.rows))):
         own = own_side[place * sz.rows : (place + 1) * sz.rows, :]
@@ -244,32 +303,6 @@
     to_east[3 * sz.rows + sz.lev :, :] = ends
     to_west[3 * sz.rows + sz.lev :, :] = turn(ends, -2, 0)
 
-    @pl.when(lax.axis_index("sect") == 0)
-    def _():
-        row = row_ids(tile)
-        lev_e, lev_w = turn(lev, -1, 1), turn(lev, 1, 1)
-        lev_n, lev_s = shift_north(lev, row, north_lev), shift_south(lev, row, south_lev)
-        warm_above = None
-        for k in range(sz.lev):
-            at = k * sz.rows
-
-            def around(f):
-                value = fields[f * sz.slab + at : f * sz.slab + at + sz.rows, :]
-                beyond = 2 * f * sz.lev + k
-                return (
-                    value, turn(value, -1, 1), turn(value, 1, 1),
-                    shift_north(value, row, north[beyond : beyond + 1, :]),
-                    shift_south(value, row, south[beyond : beyond + 1, :]),
-                )
-
-            wet = lev > k
-            masks = wet, wet & (lev_e > k), wet & (lev_w > k), wet & (lev_n > k), wet & (lev_s > k)
-            warm = diffused(around(2), around(4), masks)
-            background = fields[5 * sz.slab + at : 5 * sz.slab + at + sz.rows, :]
-            mixing = jnp.zeros(tile, jnp.float32) if k == 0 else mixed(warm_above, warm, background, wet)
-            warm_above = warm
-            bulk[sz.slab + at : sz.slab + at + sz.rows, :] = mixing
-
 
 def keep(mask, value):
     return jnp.where(mask, value, 0.0)
@@ -332,19 +365,65 @@
         return self.own * own + self.east * east + self.west * west + (self.north * north + self.south * south)
 
 
-def shift_fields(sz, fields, south, north, kept, moved_e, moved_w, moved_n, moved_s):
+def shift_fields(
+    sz, fields, levels, south, north, cross_south, cross_north, kept, moved_e, moved_w, around_n, around_s
+):
     kept[...] = fields[...]
-    row = row_ids((sz.rows, sz.cols))
-    for f in range(sz.nf):
-        for k in range(sz.lev):
-            at = f * sz.slab + k * sz.rows
-            here = slice(at, at + sz.rows)
-            value = fields[here, :]
-            beyond = 2 * f * sz.lev + k
-            moved_e[here, :] = turn(value, -1, 1)
-            moved_w[here, :] = turn(value, 1, 1)
-            moved_n[here, :] = shift_north(value, row, north[beyond : beyond + 1, :])
-            moved_s[here, :] = shift_south(value, row, south[beyond : beyond + 1, :])
+    tile = (sz.rows, sz.cols)
+    row = row_ids(tile)
+    for at in range(0, sz.nf * sz.slab, sz.rows):
+        here = slice(at, at + sz.rows)
+        value = fields[here, :]
+        moved_e[here, :] = turn(value, -1, 1)
+        moved_w[here, :] = turn(value, 1, 1)
+
+    def along_lat(f, k):
+        value = fields[f * sz.slab + k * sz.rows : f * sz.slab + (k + 1) * sz.rows, :]
+        beyond = slice(2 * f * sz.lev + k, 2 * f * sz.lev + k + 1)
+        return value, shift_north(value, row, north[beyond, :]), shift_south(value, row, south[beyond, :])
+
+    is_dynamics = lax.axis_index("sect") == 0
+
+    @pl.when(jnp.logical_not(is_dynamics))
+    def _():
+        for f in range(sz.nf):
+            for k in range(sz.lev):
+                here = slice(f * sz.slab + k * sz.rows, f * sz.slab + (k + 1) * sz.rows)
+                _, around_n[here, :], around_s[here, :] = along_lat(f, k)
+
+    @pl.when(is_dynamics)
+    def _():
+        lev = levels[...].astype(jnp.float32)
+        level_row = LEVEL_ROW * sz.lev
+        lev_n = shift_north(lev, row, cross_north[level_row : level_row + 1, :])
+        lev_s = shift_south(lev, row, cross_south[level_row : level_row + 1, :])
+        press = jnp.zeros(tile, jnp.float32)
+        press_n = press
+        for k in range(sz.lev):
+            wet, wet_n, wet_s = lev > k, lev_n > k, lev_s > k
+            zonal, merid, temper, saline, visc = (along_lat(f, k) for f in range(5))
+            coef_n = keep(wet & wet_n, 0.5 * (visc[0] + visc[1]))
+            coef_s = keep(wet & wet_s, 0.5 * (visc[2] + visc[0]))
+
+            def advanced(quantity):
+                mid, n, s = quantity
+                return mid + TIME_STEP * (coef_n * (n - mid) - coef_s * (mid - s))
+
+            def weight(place, wet_there):
+                return keep(wet_there, HALINE * saline[place] - THERMAL * temper[place])
+
+            press = press + GRAVITY_SCALE * weight(0, wet)
+            press_n = press_n + GRAVITY_SCALE * weight(1, wet_n)
+            parts = (
+                advanced(zonal) + TIME_STEP * CORIOLIS * merid[0],
+                advanced(merid) - TIME_STEP * (CORIOLIS * zonal[0] + (press_n - press)),
+                advanced(temper),
+                advanced(saline),
+                press,
+                keep(wet & wet_n, merid[0]) - keep(wet & wet_s, merid[2]),
+            )
+            for f, part in enumerate(parts):
+                around_n[f * sz.slab + k * sz.rows : f * sz.slab + (k + 1) * sz.rows, :] = part
 
 
 def column_edges(
@@ -396,19 +475,17 @@
 
         own_pair, inner_w, inner_e = both(place(1), place(0)), place(3), place(2)
 
-        def around(f, message_lane, cross_row):
+        def around(f, message_lane, end):
             shift = -f * sz.lev
             outer_w, outer_e = turn(west_side, -message_lane, 1), turn(east_side, -message_lane, 1)
             own = turn(own_pair, shift, 1)
-            low, high = (
-                cross[cross_row * sz.lev : (cross_row + 1) * sz.lev, :] for cross in (cross_south, cross_north)
-            )
+            low, high = (cross[END_ROW * sz.lev : (END_ROW + 1) * sz.lev, :] for cross in (cross_south, cross_north))
             return (
                 own,
                 both(turn(inner_w, shift, 1), outer_e),
                 both(outer_w, turn(inner_e, shift, 1)),
-                pair_north(own, both(levels_in_lanes(high, 0), levels_in_lanes(high, last_lane))),
-                pair_south(own, both(levels_in_lanes(low, 0), levels_in_lanes(low, last_lane))),
+                pair_north(own, both(levels_in_lanes(high, end), levels_in_lanes(high, end + 1))),
+                pair_south(own, both(levels_in_lanes(low, end), levels_in_lanes(low, end + 1))),
             )
 
         depth = pair_lane.astype(jnp.float32)
@@ -418,7 +495,7 @@
 
         mid = wet(lev)
         mask = mid, mid & wet(lev_e), mid & wet(lev_w), mid & wet(lev_n), mid & wet(lev_s)
-        warm = diffused(around(2, 0, TEMPER_ROW), around(4, sz.lev, VISC_ROW), mask)
+        warm = diffused(around(2, 0, TEMPER_END), around(4, sz.lev, VISC_END), mask)
         background = turn(own_pair, -5 * sz.lev, 1)
         return jnp.where(pair_lane == 0, 0.0, mixed(turn(warm, 1, 1), warm, background, mid))
 
@@ -496,7 +573,7 @@
 
 
 def finish(
-    sz, fields, levels, south, north, cross_south, cross_north, bulk,
+    sz, fields, levels, south, north, cross_south, cross_north, zonal_in, merid_in, mixing_in,
     side, from_west, from_east, moved_e, moved_w, around_e, around_w, around_n, around_s, second, edge_mix,
     result, out, div, mix, vert, low_strip, high_strip, ratio, forward, inv_ref, wref, pull, moved, sent,
 ):
@@ -537,43 +614,40 @@
 
     def physics():
         def around(f, k):
-            at = f * sz.slab + k * sz.rows
-            here = slice(at, at + sz.rows)
+            here = slice(f * sz.slab + k * sz.rows, f * sz.slab + (k + 1) * sz.rows)
             lane_at = f * sz.lev + k
             return (
                 fields[here, :],
                 jnp.where(lane == last_lane, to_lane(from_east[0 : sz.rows, :], lane_at, last_lane), moved_e[here, :]),
                 jnp.where(lane == 0, to_lane(from_west[0 : sz.rows, :], lane_at, 0), moved_w[here, :]),
-                around_n[here, :],
-                around_s[here, :],
             )
 
-        press = jnp.zeros(tile, jnp.float32)
-        press_e, press_n, warm_above = press, press, press
-        for k in range(sz.lev):
-            at = k * sz.rows
-            mask = masks(k)
-            wet, wet_e, wet_w, wet_n, wet_s = mask
+        press_e, warm_above = jnp.zeros(tile, jnp.float32), None
+        for k in range(sz.lev):
+            at = k * sz.rows
+            wet, wet_e, wet_w, wet_n, _ = masks(k)
             zonal, merid, temper, saline, visc = (around(f, k) for f in range(5))
-            flow_east, flow_west = keep(wet_e, zonal[0]), keep(wet_w, zonal[2])
-            flow_north, flow_south = keep(wet_n, merid[0]), keep(wet_s, merid[4])
-            div[at : at + sz.rows, :] = flow_east - flow_west + (flow_north - flow_south)
-            warm = diffused(temper, visc, mask)
+            zonal_far, merid_far, temper_far, saline_far, press, div_far = (
+                around_n[f * sz.slab + at : f * sz.slab + at + sz.rows, :] for f in range(6)
+            )
+            div[at : at + sz.rows, :] = keep(wet_e, zonal[0]) - keep(wet_w, zonal[2]) + div_far
+            coef_e = keep(wet_e, 0.5 * (visc[0] + visc[1]))
+            coef_w = keep(wet_w, 0.5 * (visc[2] + visc[0]))
+
+            def along_lon(quantity):
+                mid, e, w = quantity
+                return TIME_STEP * (coef_e * (e - mid) - coef_w * (mid - w))
+
+            warm = temper_far + along_lon(temper)
             mixing = jnp.zeros(tile, jnp.float32)
             if k > 0:
                 background = fields[5 * sz.slab + at : 5 * sz.slab + at + sz.rows, :]
                 mixing = mixed(warm_above, warm, background, wet)
             warm_above = warm
-
-            def weight(place, wet_there):
-                return keep(wet_there, HALINE * saline[place] - THERMAL * temper[place])
-
-            press = press + GRAVITY_SCALE * weight(0, wet)
-            press_e = press_e + GRAVITY_SCALE * weight(1, lev_e > k)
-            press_n = press_n + GRAVITY_SCALE * weight(3, lev_n > k)
-            zonal_new = diffused(zonal, visc, mask) + TIME_STEP * (CORIOLIS * merid[0] - (press_e - press))
-            merid_new = diffused(merid, visc, mask) - TIME_STEP * (CORIOLIS * zonal[0] + (press_n - press))
-            saline_new = diffused(saline, visc, mask)
+            press_e = press_e + GRAVITY_SCALE * keep(lev_e > k, HALINE * saline[1] - THERMAL * temper[1])
+            zonal_new = zonal_far + along_lon(zonal) - TIME_STEP * (press_e - press)
+            merid_new = merid_far + along_lon(merid)
+            saline_new = saline_far + along_lon(saline)
             parts = (keep(wet_e, zonal_new), keep(wet_n, merid_new), warm, saline_new, None, mixing)
             for f, part in enumerate(parts):
                 if part is not None:
@@ -623,7 +697,7 @@
                 flow_s = keep(wet_near & wet(far_lev), merid_far)
             else:
                 flow_n = keep(wet_near & wet(far_lev), merid)
-                flow_s = keep(wet_near & wet(own_lev), level_rows(bulk, 0, last_row, sz))
+                flow_s = keep(wet_near & wet(own_lev), level_rows(merid_in, 0, last_row, sz))
             weights = Weights(flow_e, flow_w, flow_n, flow_s, step)
             for f in range(sz.nf):
                 at = 2 * f * sz.lev
@@ -654,9 +728,7 @@
         for k in range(sz.lev):
             at = k * sz.rows
             wet, wet_e, wet_w, wet_n, wet_s = masks(k)
-            zonal_at = zonal_place(sz) + at if at < early(sz) else 2 * sz.slab + at - early(sz)
-            zonal = (side if at < early(sz) else bulk)[zonal_at : zonal_at + sz.rows, :]
-            merid = bulk[at : at + sz.rows, :]
+            zonal, merid = zonal_in[at : at + sz.rows, :], merid_in[at : at + sz.rows, :]
             zonal_first = sz.nf * sz.lev
             zonal_west = shift_west(zonal, lane, to_lane(west_old, zonal_first + k, 0))
             beyond = MERID_ROW * sz.lev + k
@@ -681,7 +753,7 @@
             at = k * sz.rows
             total = total + div[at : at + sz.rows, :]
             vert[at : at + sz.rows, :] = -total if k > 0 else zero
-            mixing = bulk[sz.slab + at : sz.slab + at + sz.rows, :]
+            mixing = mixing_in[at : at + sz.rows, :]
             mix[at : at + sz.rows, :] = jnp.where(at_edge, edge_mix[at : at + sz.rows, :], mixing)
         last_ratio = None
         up, down = faces(0)
@@ -795,7 +867,10 @@
     cross_shape = (LEVEL_ROW * sz.lev + 8, sz.cols)
     columns_shape = (4 * sz.rows + sz.lev, sz.cols)
     side_shape = (4 * sz.rows, sz.cols)
-    row_a, row_b, own_side = call_kernel(functools.partial(pack_edges, sz), [rows_shape, rows_shape, side_shape], [flat])
+    slab = (sz.slab, sz.cols)
+    row_a, row_b, own_side, zonal, merid = call_kernel(
+        functools.partial(pack_edges, sz), [rows_shape, rows_shape, side_shape, slab, slab], [flat]
+    )
     twin_shape = (zonal_place(sz) + early(sz), sz.cols)
     wide_shape = (max(cross_shape[0], twin_shape[0] + 8), sz.cols)
     (cross_b,) = call_kernel(functools.partial(pack_cross, sz), [wide_shape], [flat, levels])
@@ -810,18 +885,21 @@
     south, north, corners = call_kernel(
         functools.partial(place_rows, sz), [rows_shape, rows_shape, (sz.rows, sz.cols)], [row_a, row_b]
     )
-    to_east, to_west, cross_south, cross_north, bulk = call_kernel(
+    (mixing,) = call_kernel(
+        functools.partial(pack_mixing, sz), [(sz.slab, sz.cols)], [flat, levels, levels_a, cross_b, south, north]
+    )
+    to_east, to_west, cross_south, cross_north = call_kernel(
         functools.partial(pack_columns, sz),
-        [columns_shape] * 2 + [cross_shape] * 2 + [(3 * sz.slab - early(sz), sz.cols)],
-        [flat, levels, levels_a, south, north, corners, twin, cross_b, own_side],
-    )
-    bulk = from_dynamics(bulk)
+        [columns_shape] * 2 + [cross_shape] * 2,
+        [levels, levels_a, south, north, corners, twin, cross_b, own_side],
+    )
+    mixing = from_dynamics(mixing)
+    zonal, merid = from_dynamics(zonal), from_dynamics(merid)
     from_east = around(to_west, -1)
     from_west = around(to_east, 1)
     kept, moved_e, moved_w, around_n, around_s = call_kernel(
-        functools.partial(shift_fields, sz), [flat.shape] * 5, [flat, south, north]
-    )
-    slab = (sz.slab, sz.cols)
+        functools.partial(shift_fields, sz), [flat.shape] * 5, [flat, levels, south, north, cross_south, cross_north]
+    )
     around_e, around_w, second, edge_mix = call_kernel(
         functools.partial(column_edges, sz),
         [flat.shape] * 3 + [slab],
@@ -833,7 +911,7 @@
         functools.partial(finish, sz),
         [out_shape],
         [
-            kept, levels, south, north, cross_south, cross_north, bulk, twin, from_west, from_east,
+            kept, levels, south, north, cross_south, cross_north, zonal, merid, mixing, twin, from_west, from_east,
             moved_e, moved_w, around_e, around_w, around_n, around_s, second, edge_mix,
         ],
         [out_shape, slab, slab, slab, strip, strip, slab, flat.shape, slab, (5 * sz.slab, sz.cols), slab, flat.shape],

time: 18.1 us -> 17.5 us (0.967)
  waiting for transfers between devices: 4.43 us -> 1.5 us
  starting transfers between devices: 10.2 us -> 12.2 us
  Pallas kernels: 2.25 us -> 2.5 us
    ppermute x2 -> x4, starting transfers between devices: 2.86 us -> 4.95 us  [from_dynamics(): lax.ppermute(value, 'sect', [(s, (s + hop) % count_s) for s in range(coun...]
    ppermute x4, waiting for transfers between devices: 2.07 us -> 0.01 us  [swap(): return lax.ppermute(value, ('sect', 'lon', 'lat'), pairs)]
    ppermute x2 -> x4, waiting for transfers between devices: 0.8 us -> 0.01 us  [from_dynamics(): lax.ppermute(value, 'sect', [(s, (s + hop) % count_s) for s in range(coun...]
    pallas_call x8 -> x9, Pallas kernels: 2.25 us -> 2.5 us  [call_kernel(): pl.pallas_call(body, out_shape=[jax.ShapeDtypeStruct(shape, jnp.float32)...]
  transfers between devices with their start and end apart: 8 -> 10, of which waited for: 6 -> 1; matrix products, arithmetic and copies ran while one was open for 0% -> 0% of each run, Pallas kernels for 3% -> 7%
where the time goes in v5:
time: 17.5 us; the launch traced here: 17.3 us
  starting transfers between devices  12.2 us (70%)
  Pallas kernels  2.5 us (14%)
  waiting for transfers between devices  1.5 us (9%)
  local copies, waits for them, and re-layouts  1 us (6%)
    ppermute x4, starting transfers between devices, from_dynamics(): lax.ppermute(value, 'sect', [(s, (s + hop) % count_s) for s in range(coun...  4.95 us
    ppermute x2, starting transfers between devices, around(): lax.ppermute(value, 'lon', [(i, (i + step) % count_o) for i in range(coun...  3.84 us
    ppermute x4, starting transfers between devices, swap(): return lax.ppermute(value, ('sect', 'lon', 'lat'), pairs)  3.46 us
    pallas_call x9, Pallas kernels, call_kernel(): pl.pallas_call(body, out_shape=[jax.ShapeDtypeStruct(shape, jnp.float32)...  2.5 us
    ppermute x2, waiting for transfers between devices, around(): lax.ppermute(value, 'lon', [(i, (i + step) % count_o) for i in range(coun...  1.48 us
    unnamed x6, local copies, waits for them, and re-layouts  1 us
  transfers between devices with their start and end apart: 10, of which 1 were waited for; matrix products, arithmetic and copies ran while one was open for 0% of the time, Pallas kernels for 7%

profile of v5, /device:TPU:0, one launch (start us, length us, event | category | flops | bytes accessed | tf_op | source)
XLA Modules:
  0.0 17.3 jit_solution(11684437895805070378)
XLA Ops:
  0.0 0.0 copy-start
  0.0 1.0 %copy-done = f32[1,6,16,8,128]{4,3,2,1,0:T(8,128)S(1)} copy-done((f32[1,6,16,8,128]{4,3,2,1,0:T(8,128)S(1)}, f32[1,6,16,8,128]{4,3,2,1,0:T(8,128)}, u32[]{:S(2)}) %copy-start) | copy-done | bytes 393240
  1.0 0.0 copy-start.2
  1.0 0.3 %shard_map.28 = (f32[192,128]{1,0:T(8,128)S(1)}, f32[192,128]{1,0:T(8,128)S(1)}, f32[32,128]{1,0:T(8,128)S(1)}, f32[128,128]{1,0:T(8,128)S(1)}, f32[128,128]{1,0:T(8,128)S(1)}) custom-call(f32[768,128]{1,0:T(8,128)S(1)} %bitcast.2), custom_call_target="tpu_custom_call" | custom-call | tf_op jit(solution)/shard_map/pallas_call | solution.py:31
  1.3 0.5 %collective-permute-start = (f32[192,128]{1,0:T(8,128)S(1)}, f32[192,128]{1,0:T(8,128)S(1)}, u32[]{:S(2)}, u32[]{:S(2)}) collective-permute-start(f32[192,128]{1,0:T(8,128)S(1)} %get-tuple-element.26), channel_id=1, source_target_pairs={{0,1},{1,0},{2,3},{3,2},{4,5},{5,4},{6,7},{7,6},{8,9},{9,8},{10,11... | collective-permute-start | bytes 294920 | tf_op jit(solution)/shard_map/ppermute | solution.py:850
  1.7 2.6 %collective-permute-start.1 = (f32[192,128]{1,0:T(8,128)S(1)}, f32[192,128]{1,0:T(8,128)S(1)}, u32[]{:S(2)}, u32[]{:S(2)}) collective-permute-start(f32[192,128]{1,0:T(8,128)S(1)} %get-tuple-element.27), channel_id=1, source_target_pairs={{0,4},{1,2},{2,1},{3,7},{4,0},{5,6},{6,5},{7,3},{8,12},{9,10},{10,... | collective-permute-start | bytes 294920 | tf_op jit(solution)/shard_map/ppermute | solution.py:850
  4.4 0.0 copy-done.2
  4.4 0.1 shard_map.31
  4.5 0.0 copy-start.1
  4.5 0.3 %collective-permute-start.4 = (f32[104,128]{1,0:T(8,128)S(1)}, f32[104,128]{1,0:T(8,128)S(1)}, u32[]{:S(2)}, u32[]{:S(2)}) collective-permute-start(f32[104,128]{1,0:T(8,128)S(1)} %shard_map.31), channel_id=1, source_target_pairs={{0,4},{1,18},{2,17},{3,7},{4,0},{5,22},{6,21},{7,3},{8,12},{9,26},... | collective-permute-start | bytes 159752 | tf_op jit(solution)/shard_map/ppermute | solution.py:850
  4.8 0.0 collective-permute-done.row_a
  4.8 0.1 shard_map.30
  4.9 1.6 %collective-permute-start.3 = (f32[96,128]{1,0:T(8,128)S(1)}, f32[96,128]{1,0:T(8,128)S(1)}, u32[]{:S(2)}, u32[]{:S(2)}) collective-permute-start(f32[96,128]{1,0:T(8,128)S(1)} %shard_map.30), channel_id=1, source_target_pairs={{0,16},{16,0},{1,17},{17,1},{2,18},{18,2},{3,19},{19,3},{4,20},{20... | collective-permute-start | bytes 147464 | tf_op jit(solution)/shard_map/ppermute | solution.py:857
  6.5 0.0 collective-permute-start.2
  6.5 1.3 %collective-permute-start.5 = (f32[128,128]{1,0:T(8,128)S(1)}, f32[128,128]{1,0:T(8,128)S(1)}, u32[]{:S(2)}, u32[]{:S(2)}) collective-permute-start(f32[128,128]{1,0:T(8,128)S(1)} %get-tuple-element.35), channel_id=1, source_target_pairs={{0,16},{16,0},{1,17},{17,1},{2,18},{18,2},{3,19},{19,3},{4,20},{20... | collective-permute-start | bytes 196616 | tf_op jit(solution)/shard_map/ppermute | solution.py:857
  7.9 0.0 collective-permute-done.1.row_b
  7.9 1.1 %collective-permute-start.6 = (f32[128,128]{1,0:T(8,128)S(1)}, f32[128,128]{1,0:T(8,128)S(1)}, u32[]{:S(2)}, u32[]{:S(2)}) collective-permute-start(f32[128,128]{1,0:T(8,128)S(1)} %get-tuple-element.36), channel_id=1, source_target_pairs={{0,16},{16,0},{1,17},{17,1},{2,18},{18,2},{3,19},{19,3},{4,20},{20... | collective-permute-start | bytes 196616 | tf_op jit(solution)/shard_map/ppermute | solution.py:857
  8.9 0.1 shard_map.29
  9.1 0.0 collective-permute-done.2.levels_a
  9.1 0.0 collective-permute-done.4.cross_b
  9.1 0.0 copy-done.1
  9.1 0.2 %shard_map.34 = f32[128,128]{1,0:T(8,128)S(1)} custom-call(f32[768,128]{1,0:T(8,128)S(1)} %bitcast.5, s32[8,128]{1,0:T(8,128)S(1)} %copy-done.2, s32[8,128]{1,0:T(8,128)S(1)} %collective-permute-done.2.levels_a, f32[104,128]{1,0:T(8,128)S(1)} %collective-permute-done.4.cross_b, f32[192,128]{1,0:T(8,128)S(1)} %get-tuple-element.28.south, ...), custom_call_target="tpu_custom_call" | custom-call | tf_op jit(solution)/shard_map/pallas_call | solution.py:31
  9.3 0.9 %collective-permute-start.7 = (f32[128,128]{1,0:T(8,128)S(1)}, f32[128,128]{1,0:T(8,128)S(1)}, u32[]{:S(2)}, u32[]{:S(2)}) collective-permute-start(f32[128,128]{1,0:T(8,128)S(1)} %shard_map.34), channel_id=1, source_target_pairs={{0,16},{16,0},{1,17},{17,1},{2,18},{18,2},{3,19},{19,3},{4,20},{20... | collective-permute-start | bytes 196616 | tf_op jit(solution)/shard_map/ppermute | solution.py:857
  10.2 0.0 collective-permute-done.3.twin.side
  10.2 0.2 shard_map.32
  10.4 1.5 %collective-permute-start.8 = (f32[48,128]{1,0:T(8,128)S(1)}, f32[48,128]{1,0:T(8,128)S(1)}, u32[]{:S(2)}, u32[]{:S(2)}) collective-permute-start(f32[48,128]{1,0:T(8,128)S(1)} %get-tuple-element.37.own_east), channel_id=1, source_target_pairs={{0,4},{4,8},{8,12},{12,0},{1,5},{5,9},{9,13},{13,1},{2,6},{6,10},{... | collective-permute-start | bytes 73736 | tf_op jit(solution)/shard_map/ppermute | solution.py:864
  11.9 2.3 %collective-permute-start.9 = (f32[48,128]{1,0:T(8,128)S(1)}, f32[48,128]{1,0:T(8,128)S(1)}, u32[]{:S(2)}, u32[]{:S(2)}) collective-permute-start(f32[48,128]{1,0:T(8,128)S(1)} %get-tuple-element.38.own_west), channel_id=1, source_target_pairs={{0,12},{4,0},{8,4},{12,8},{1,13},{5,1},{9,5},{13,9},{2,14},{6,2},{... | collective-permute-start | bytes 73736 | tf_op jit(solution)/shard_map/ppermute | solution.py:864
  14.2 0.4 %shard_map.33 = (f32[768,128]{1,0:T(8,128)S(1)}, f32[768,128]{1,0:T(8,128)S(1)}, f32[768,128]{1,0:T(8,128)S(1)}, f32[768,128]{1,0:T(8,128)S(1)}, f32[768,128]{1,0:T(8,128)S(1)}) custom-call(f32[768,128]{1,0:T(8,128)S(1)} %bitcast.6, s32[8,128]{1,0:T(8,128)S(1)} %copy-done.2, f32[192,128]{1,0:T(8,128)S(1)} %get-tuple-element.28.south, ...), custom_call_target="tpu_custom_call" | custom-call | tf_op jit(solution)/shard_map/pallas_call | solution.py:31
  14.7 1.5 %collective-permute-done.8.from_west = f32[48,128]{1,0:T(8,128)S(1)} collective-permute-done((f32[48,128]{1,0:T(8,128)S(1)}, f32[48,128]{1,0:T(8,128)S(1)}, u32[]{:S(2)}, u32[]{:S(2)}) %collective-permute-start.8) | collective-permute-done | bytes 24608 | tf_op jit(solution)/shard_map/ppermute | solution.py:864
  16.1 0.0 collective-permute-done.9.from_east
  16.1 0.1 shard_map.35
  16.2 0.0 collective-permute-done.5.zonal_in
  16.2 0.0 collective-permute-done.6.merid_in
  16.2 0.0 collective-permute-done.7.mixing_in
  16.2 1.1 %shard_map.36 = f32[6,128,128]{2,1,0:T(8,128)} custom-call(f32[768,128]{1,0:T(8,128)S(1)} %get-tuple-element.34.fields, s32[8,128]{1,0:T(8,128)S(1)} %copy-done.2, f32[192,128]{1,0:T(8,128)S(1)} %get-tuple-element.28.south, f32[192,128]{1,0:T(8,128)S(1)} %get-tuple-element.29.north, f32[72,128]{1,0:T(8,128)S(1)} %get-tuple-element.32.cross_south, ...), custom_call_target="tpu_custom_call" | custom-call | tf_op jit(solution)/shard_map/pallas_call | solution.py:31
Async XLA Ops:
  0.0 1.0 %copy-start = (f32[1,6,16,8,128]{4,3,2,1,0:T(8,128)S(1)}, f32[1,6,16,8,128]{4,3,2,1,0:T(8,128)}, u32[]{:S(2)}) copy-start(f32[1,6,16,8,128]{4,3,2,1,0:T(8,128)} %param.2) | copy-start | bytes 1179652
  1.0 3.4 %copy-start.2 = (s32[8,128]{1,0:T(8,128)S(1)}, s32[8,128]{1,0:T(8,128)}, u32[]{:S(2)}) copy-start(s32[8,128]{1,0:T(8,128)} %levels.11) | copy-start | bytes 12292
  1.3 3.5 %collective-permute-start = (f32[192,128]{1,0:T(8,128)S(1)}, f32[192,128]{1,0:T(8,128)S(1)}, u32[]{:S(2)}, u32[]{:S(2)}) collective-permute-start(f32[192,128]{1,0:T(8,128)S(1)} %get-tuple-element.26), channel_id=1, source_target_pairs={{0,1},{1,0},{2,3},{3,2},{4,5},{5,4},{6,7},{7,6},{8,9},{9,8},{10,11... | collective-permute-start | bytes 294920 | tf_op jit(solution)/shard_map/ppermute | solution.py:850
  1.7 6.1 %collective-permute-start.1 = (f32[192,128]{1,0:T(8,128)S(1)}, f32[192,128]{1,0:T(8,128)S(1)}, u32[]{:S(2)}, u32[]{:S(2)}) collective-permute-start(f32[192,128]{1,0:T(8,128)S(1)} %get-tuple-element.27), channel_id=1, source_target_pairs={{0,4},{1,2},{2,1},{3,7},{4,0},{5,6},{6,5},{7,3},{8,12},{9,10},{10,... | collective-permute-start | bytes 294920 | tf_op jit(solution)/shard_map/ppermute | solution.py:850
  4.5 4.6 %copy-start.1 = (f32[1,6,16,8,128]{4,3,2,1,0:T(8,128)S(1)}, f32[1,6,16,8,128]{4,3,2,1,0:T(8,128)}, u32[]{:S(2)}) copy-start(f32[1,6,16,8,128]{4,3,2,1,0:T(8,128)} %param.2) | copy-start | bytes 1179652
  4.5 4.6 %collective-permute-start.4 = (f32[104,128]{1,0:T(8,128)S(1)}, f32[104,128]{1,0:T(8,128)S(1)}, u32[]{:S(2)}, u32[]{:S(2)}) collective-permute-start(f32[104,128]{1,0:T(8,128)S(1)} %shard_map.31), channel_id=1, source_target_pairs={{0,4},{1,18},{2,17},{3,7},{4,0},{5,22},{6,21},{7,3},{8,12},{9,26},... | collective-permute-start | bytes 159752 | tf_op jit(solution)/shard_map/ppermute | solution.py:850
  4.9 5.3 %collective-permute-start.3 = (f32[96,128]{1,0:T(8,128)S(1)}, f32[96,128]{1,0:T(8,128)S(1)}, u32[]{:S(2)}, u32[]{:S(2)}) collective-permute-start(f32[96,128]{1,0:T(8,128)S(1)} %shard_map.30), channel_id=1, source_target_pairs={{0,16},{16,0},{1,17},{17,1},{2,18},{18,2},{3,19},{19,3},{4,20},{20... | collective-permute-start | bytes 147464 | tf_op jit(solution)/shard_map/ppermute | solution.py:857
  6.5 2.5 %collective-permute-start.2 = (s32[8,128]{1,0:T(8,128)S(1)}, s32[8,128]{1,0:T(8,128)S(1)}, u32[]{:S(2)}, u32[]{:S(2)}) collective-permute-start(s32[8,128]{1,0:T(8,128)S(1)} %copy-done.2), channel_id=1, source_target_pairs={{0,1},{1,0},{2,3},{3,2},{4,5},{5,4},{6,7},{7,6},{8,9},{9,8},{10,11... | collective-permute-start | bytes 12296 | tf_op jit(solution)/shard_map/ppermute | solution.py:850
  6.5 9.7 %collective-permute-start.5 = (f32[128,128]{1,0:T(8,128)S(1)}, f32[128,128]{1,0:T(8,128)S(1)}, u32[]{:S(2)}, u32[]{:S(2)}) collective-permute-start(f32[128,128]{1,0:T(8,128)S(1)} %get-tuple-element.35), channel_id=1, source_target_pairs={{0,16},{16,0},{1,17},{17,1},{2,18},{18,2},{3,19},{19,3},{4,20},{20... | collective-permute-start | bytes 196616 | tf_op jit(solution)/shard_map/ppermute | solution.py:857
  7.9 8.3 %collective-permute-start.6 = (f32[128,128]{1,0:T(8,128)S(1)}, f32[128,128]{1,0:T(8,128)S(1)}, u32[]{:S(2)}, u32[]{:S(2)}) collective-permute-start(f32[128,128]{1,0:T(8,128)S(1)} %get-tuple-element.36), channel_id=1, source_target_pairs={{0,16},{16,0},{1,17},{17,1},{2,18},{18,2},{3,19},{19,3},{4,20},{20... | collective-permute-start | bytes 196616 | tf_op jit(solution)/shard_map/ppermute | solution.py:857
  9.3 6.9 %collective-permute-start.7 = (f32[128,128]{1,0:T(8,128)S(1)}, f32[128,128]{1,0:T(8,128)S(1)}, u32[]{:S(2)}, u32[]{:S(2)}) collective-permute-start(f32[128,128]{1,0:T(8,128)S(1)} %shard_map.34), channel_id=1, source_target_pairs={{0,16},{16,0},{1,17},{17,1},{2,18},{18,2},{3,19},{19,3},{4,20},{20... | collective-permute-start | bytes 196616 | tf_op jit(solution)/shard_map/ppermute | solution.py:857
  10.4 5.7 %collective-permute-start.8 = (f32[48,128]{1,0:T(8,128)S(1)}, f32[48,128]{1,0:T(8,128)S(1)}, u32[]{:S(2)}, u32[]{:S(2)}) collective-permute-start(f32[48,128]{1,0:T(8,128)S(1)} %get-tuple-element.37.own_east), channel_id=1, source_target_pairs={{0,4},{4,8},{8,12},{12,0},{1,5},{5,9},{9,13},{13,1},{2,6},{6,10},{... | collective-permute-start | bytes 73736 | tf_op jit(solution)/shard_map/ppermute | solution.py:864
  11.9 4.2 %collective-permute-start.9 = (f32[48,128]{1,0:T(8,128)S(1)}, f32[48,128]{1,0:T(8,128)S(1)}, u32[]{:S(2)}, u32[]{:S(2)}) collective-permute-start(f32[48,128]{1,0:T(8,128)S(1)} %get-tuple-element.38.own_west), channel_id=1, source_target_pairs={{0,12},{4,0},{8,4},{12,8},{1,13},{5,1},{9,5},{13,9},{2,14},{6,2},{... | collective-permute-start | bytes 73736 | tf_op jit(solution)/shard_map/ppermute | solution.py:864

commit v6 on v5

--- a/solution.py
+++ b/solution.py
@@ -16,8 +16,7 @@
 RICHARDSON = 1.0
 
 VMEM_LIMIT = 8 * 1024 * 1024
-CHUNKS = 4
-EARLY_LEVELS = 0
+CHUNKS = 2
 
 ZONAL_ROW, MERID_ROW, MERID_ROW2, END_ROW, LEVEL_ROW = range(5)
 TEMPER_END, VISC_END = 0, 2
@@ -124,7 +123,7 @@
     return jnp.where(lane == VISC_END + 1, turn(visc, VISC_END + 2, 1), ends)
 
 
-def pack_twin(sz, fields, own_side, row_a, twin):
+def pack_twin(sz, own_side, row_a, twin):
     base = 4 * sz.rows
     twin[0:base, :] = own_side[...]
     def row_of(f, r):
@@ -134,16 +133,6 @@
     parts = (row_of(0, 0), row_of(1, 0), row_of(1, 1), row_ends(row_of(2, 0), row_of(4, 0)))
     for at, part in enumerate(parts):
         twin[base + at * sz.lev : base + (at + 1) * sz.lev, :] = part
-    if early(sz):
-        twin[zonal_place(sz) : zonal_place(sz) + early(sz), :] = fields[0 : early(sz), :]
-
-
-def early(sz):
-    return EARLY_LEVELS * sz.rows
-
-
-def zonal_place(sz):
-    return 4 * sz.rows + LEVEL_ROW * sz.lev
 
 
 def edge_columns(sz, ref, count, first):
@@ -871,14 +860,13 @@
     row_a, row_b, own_side, zonal, merid = call_kernel(
         functools.partial(pack_edges, sz), [rows_shape, rows_shape, side_shape, slab, slab], [flat]
     )
-    twin_shape = (zonal_place(sz) + early(sz), sz.cols)
-    wide_shape = (max(cross_shape[0], twin_shape[0] + 8), sz.cols)
-    (cross_b,) = call_kernel(functools.partial(pack_cross, sz), [wide_shape], [flat, levels])
+    twin_shape = (4 * sz.rows + LEVEL_ROW * sz.lev, sz.cols)
+    (cross_b,) = call_kernel(functools.partial(pack_cross, sz), [cross_shape], [flat, levels])
     row_a = swap(row_a, False)
     levels_a = swap(levels, False)
     row_b = swap(row_b, True)
     (twin,) = call_kernel(
-        functools.partial(pack_twin, sz), [twin_shape], [flat, own_side, row_a]
+        functools.partial(pack_twin, sz), [twin_shape], [own_side, row_a]
     )
     twin = from_dynamics(twin)
     cross_b = from_dynamics(cross_b, True)

time: 17.5 us -> 17.4 us (level)
  no operation moved by 1% of the time
where the time goes in v6:
time: 17.4 us; the launch traced here: 17.2 us
  starting transfers between devices  12.2 us (70%)
  Pallas kernels  2.47 us (14%)
  waiting for transfers between devices  1.5 us (9%)
  local copies, waits for them, and re-layouts  1 us (6%)
    ppermute x4, starting transfers between devices, from_dynamics(): lax.ppermute(value, 'sect', [(s, (s + hop) % count_s) for s in range(coun...  4.9 us
    ppermute x2, starting transfers between devices, around(): lax.ppermute(value, 'lon', [(i, (i + step) % count_o) for i in range(coun...  3.84 us
    ppermute x4, starting transfers between devices, swap(): return lax.ppermute(value, ('sect', 'lon', 'lat'), pairs)  3.44 us
    pallas_call x9, Pallas kernels, call_kernel(): pl.pallas_call(body, out_shape=[jax.ShapeDtypeStruct(shape, jnp.float32)...  2.47 us
    ppermute x2, waiting for transfers between devices, around(): lax.ppermute(value, 'lon', [(i, (i + step) % count_o) for i in range(coun...  1.47 us
    unnamed x6, local copies, waits for them, and re-layouts  1 us
  transfers between devices with their start and end apart: 10, of which 1 were waited for; matrix products, arithmetic and copies ran while one was open for 0% of the time, Pallas kernels for 7%

profile of v6, /device:TPU:0, one launch (start us, length us, event | category | flops | bytes accessed | tf_op | source)
XLA Modules:
  0.0 17.2 jit_solution(3981713509678950740)
XLA Ops:
  0.0 0.0 copy-start
  0.0 1.0 %copy-done = f32[1,6,16,8,128]{4,3,2,1,0:T(8,128)S(1)} copy-done((f32[1,6,16,8,128]{4,3,2,1,0:T(8,128)S(1)}, f32[1,6,16,8,128]{4,3,2,1,0:T(8,128)}, u32[]{:S(2)}) %copy-start) | copy-done | bytes 393240
  1.0 0.0 copy-start.2
  1.0 0.3 %shard_map.28 = (f32[192,128]{1,0:T(8,128)S(1)}, f32[192,128]{1,0:T(8,128)S(1)}, f32[32,128]{1,0:T(8,128)S(1)}, f32[128,128]{1,0:T(8,128)S(1)}, f32[128,128]{1,0:T(8,128)S(1)}) custom-call(f32[768,128]{1,0:T(8,128)S(1)} %bitcast.2), custom_call_target="tpu_custom_call" | custom-call | tf_op jit(solution)/shard_map/pallas_call | solution.py:30
  1.3 0.5 %collective-permute-start = (f32[192,128]{1,0:T(8,128)S(1)}, f32[192,128]{1,0:T(8,128)S(1)}, u32[]{:S(2)}, u32[]{:S(2)}) collective-permute-start(f32[192,128]{1,0:T(8,128)S(1)} %get-tuple-element.26), channel_id=1, source_target_pairs={{0,1},{1,0},{2,3},{3,2},{4,5},{5,4},{6,7},{7,6},{8,9},{9,8},{10,11... | collective-permute-start | bytes 294920 | tf_op jit(solution)/shard_map/ppermute | solution.py:839
  1.7 0.0 copy-start.1
  1.7 2.7 %collective-permute-start.1 = (f32[192,128]{1,0:T(8,128)S(1)}, f32[192,128]{1,0:T(8,128)S(1)}, u32[]{:S(2)}, u32[]{:S(2)}) collective-permute-start(f32[192,128]{1,0:T(8,128)S(1)} %get-tuple-element.27), channel_id=1, source_target_pairs={{0,4},{1,2},{2,1},{3,7},{4,0},{5,6},{6,5},{7,3},{8,12},{9,10},{10,... | collective-permute-start | bytes 294920 | tf_op jit(solution)/shard_map/ppermute | solution.py:839
  4.4 0.0 copy-done.2
  4.4 0.1 shard_map.31
  4.5 0.3 %collective-permute-start.4 = (f32[72,128]{1,0:T(8,128)S(1)}, f32[72,128]{1,0:T(8,128)S(1)}, u32[]{:S(2)}, u32[]{:S(2)}) collective-permute-start(f32[72,128]{1,0:T(8,128)S(1)} %shard_map.31), channel_id=1, source_target_pairs={{0,4},{1,18},{2,17},{3,7},{4,0},{5,22},{6,21},{7,3},{8,12},{9,26},... | collective-permute-start | bytes 110600 | tf_op jit(solution)/shard_map/ppermute | solution.py:839
  4.8 0.0 collective-permute-done.row_a
  4.8 0.1 shard_map.30
  4.9 1.6 %collective-permute-start.3 = (f32[96,128]{1,0:T(8,128)S(1)}, f32[96,128]{1,0:T(8,128)S(1)}, u32[]{:S(2)}, u32[]{:S(2)}) collective-permute-start(f32[96,128]{1,0:T(8,128)S(1)} %shard_map.30), channel_id=1, source_target_pairs={{0,16},{16,0},{1,17},{17,1},{2,18},{18,2},{3,19},{19,3},{4,20},{20... | collective-permute-start | bytes 147464 | tf_op jit(solution)/shard_map/ppermute | solution.py:846
  6.5 0.0 collective-permute-start.2
  6.5 1.3 %collective-permute-start.5 = (f32[128,128]{1,0:T(8,128)S(1)}, f32[128,128]{1,0:T(8,128)S(1)}, u32[]{:S(2)}, u32[]{:S(2)}) collective-permute-start(f32[128,128]{1,0:T(8,128)S(1)} %get-tuple-element.35), channel_id=1, source_target_pairs={{0,16},{16,0},{1,17},{17,1},{2,18},{18,2},{3,19},{19,3},{4,20},{20... | collective-permute-start | bytes 196616 | tf_op jit(solution)/shard_map/ppermute | solution.py:846
  7.8 0.0 collective-permute-done.1.row_b
  7.9 1.1 %collective-permute-start.6 = (f32[128,128]{1,0:T(8,128)S(1)}, f32[128,128]{1,0:T(8,128)S(1)}, u32[]{:S(2)}, u32[]{:S(2)}) collective-permute-start(f32[128,128]{1,0:T(8,128)S(1)} %get-tuple-element.36), channel_id=1, source_target_pairs={{0,16},{16,0},{1,17},{17,1},{2,18},{18,2},{3,19},{19,3},{4,20},{20... | collective-permute-start | bytes 196616 | tf_op jit(solution)/shard_map/ppermute | solution.py:846
  8.9 0.1 shard_map.29
  9.1 0.0 collective-permute-done.2.levels_a
  9.1 0.0 collective-permute-done.4.cross_b
  9.1 0.0 copy-done.1
  9.1 0.2 %shard_map.34 = f32[128,128]{1,0:T(8,128)S(1)} custom-call(f32[768,128]{1,0:T(8,128)S(1)} %bitcast.4, s32[8,128]{1,0:T(8,128)S(1)} %copy-done.2, s32[8,128]{1,0:T(8,128)S(1)} %collective-permute-done.2.levels_a, f32[72,128]{1,0:T(8,128)S(1)} %collective-permute-done.4.cross_b, f32[192,128]{1,0:T(8,128)S(1)} %get-tuple-element.28.south, ...), custom_call_target="tpu_custom_call" | custom-call | tf_op jit(solution)/shard_map/pallas_call | solution.py:30
  9.3 0.9 %collective-permute-start.7 = (f32[128,128]{1,0:T(8,128)S(1)}, f32[128,128]{1,0:T(8,128)S(1)}, u32[]{:S(2)}, u32[]{:S(2)}) collective-permute-start(f32[128,128]{1,0:T(8,128)S(1)} %shard_map.34), channel_id=1, source_target_pairs={{0,16},{16,0},{1,17},{17,1},{2,18},{18,2},{3,19},{19,3},{4,20},{20... | collective-permute-start | bytes 196616 | tf_op jit(solution)/shard_map/ppermute | solution.py:846
  10.1 0.0 collective-permute-done.3.twin.side
  10.1 0.2 shard_map.32
  10.3 1.6 %collective-permute-start.8 = (f32[48,128]{1,0:T(8,128)S(1)}, f32[48,128]{1,0:T(8,128)S(1)}, u32[]{:S(2)}, u32[]{:S(2)}) collective-permute-start(f32[48,128]{1,0:T(8,128)S(1)} %get-tuple-element.37.own_east), channel_id=1, source_target_pairs={{0,4},{4,8},{8,12},{12,0},{1,5},{5,9},{9,13},{13,1},{2,6},{6,10},{... | collective-permute-start | bytes 73736 | tf_op jit(solution)/shard_map/ppermute | solution.py:853
  11.9 2.2 %collective-permute-start.9 = (f32[48,128]{1,0:T(8,128)S(1)}, f32[48,128]{1,0:T(8,128)S(1)}, u32[]{:S(2)}, u32[]{:S(2)}) collective-permute-start(f32[48,128]{1,0:T(8,128)S(1)} %get-tuple-element.38.own_west), channel_id=1, source_target_pairs={{0,12},{4,0},{8,4},{12,8},{1,13},{5,1},{9,5},{13,9},{2,14},{6,2},{... | collective-permute-start | bytes 73736 | tf_op jit(solution)/shard_map/ppermute | solution.py:853
  14.2 0.4 %shard_map.33 = (f32[768,128]{1,0:T(8,128)S(1)}, f32[768,128]{1,0:T(8,128)S(1)}, f32[768,128]{1,0:T(8,128)S(1)}, f32[768,128]{1,0:T(8,128)S(1)}, f32[768,128]{1,0:T(8,128)S(1)}) custom-call(f32[768,128]{1,0:T(8,128)S(1)} %bitcast.5, s32[8,128]{1,0:T(8,128)S(1)} %copy-done.2, f32[192,128]{1,0:T(8,128)S(1)} %get-tuple-element.28.south, ...), custom_call_target="tpu_custom_call" | custom-call | tf_op jit(solution)/shard_map/pallas_call | solution.py:30
  14.6 1.5 %collective-permute-done.8.from_west = f32[48,128]{1,0:T(8,128)S(1)} collective-permute-done((f32[48,128]{1,0:T(8,128)S(1)}, f32[48,128]{1,0:T(8,128)S(1)}, u32[]{:S(2)}, u32[]{:S(2)}) %collective-permute-start.8) | collective-permute-done | bytes 24608 | tf_op jit(solution)/shard_map/ppermute | solution.py:853
  16.1 0.0 collective-permute-done.9.from_east
  16.1 0.1 shard_map.35
  16.1 0.0 collective-permute-done.5.zonal_in
  16.1 0.0 collective-permute-done.6.merid_in
  16.1 0.0 collective-permute-done.7.mixing_in
  16.1 1.1 %shard_map.36 = f32[6,128,128]{2,1,0:T(8,128)} custom-call(f32[768,128]{1,0:T(8,128)S(1)} %get-tuple-element.34.fields, s32[8,128]{1,0:T(8,128)S(1)} %copy-done.2, f32[192,128]{1,0:T(8,128)S(1)} %get-tuple-element.28.south, f32[192,128]{1,0:T(8,128)S(1)} %get-tuple-element.29.north, f32[72,128]{1,0:T(8,128)S(1)} %get-tuple-element.32.cross_south, ...), custom_call_target="tpu_custom_call" | custom-call | tf_op jit(solution)/shard_map/pallas_call | solution.py:30
Async XLA Ops:
  0.0 1.0 %copy-start = (f32[1,6,16,8,128]{4,3,2,1,0:T(8,128)S(1)}, f32[1,6,16,8,128]{4,3,2,1,0:T(8,128)}, u32[]{:S(2)}) copy-start(f32[1,6,16,8,128]{4,3,2,1,0:T(8,128)} %param.2) | copy-start | bytes 1179652
  1.0 3.4 %copy-start.2 = (s32[8,128]{1,0:T(8,128)S(1)}, s32[8,128]{1,0:T(8,128)}, u32[]{:S(2)}) copy-start(s32[8,128]{1,0:T(8,128)} %levels.11) | copy-start | bytes 12292
  1.3 3.5 %collective-permute-start = (f32[192,128]{1,0:T(8,128)S(1)}, f32[192,128]{1,0:T(8,128)S(1)}, u32[]{:S(2)}, u32[]{:S(2)}) collective-permute-start(f32[192,128]{1,0:T(8,128)S(1)} %get-tuple-element.26), channel_id=1, source_target_pairs={{0,1},{1,0},{2,3},{3,2},{4,5},{5,4},{6,7},{7,6},{8,9},{9,8},{10,11... | collective-permute-start | bytes 294920 | tf_op jit(solution)/shard_map/ppermute | solution.py:839
  1.7 7.4 %copy-start.1 = (f32[1,6,16,8,128]{4,3,2,1,0:T(8,128)S(1)}, f32[1,6,16,8,128]{4,3,2,1,0:T(8,128)}, u32[]{:S(2)}) copy-start(f32[1,6,16,8,128]{4,3,2,1,0:T(8,128)} %param.2) | copy-start | bytes 1179652
  1.7 6.1 %collective-permute-start.1 = (f32[192,128]{1,0:T(8,128)S(1)}, f32[192,128]{1,0:T(8,128)S(1)}, u32[]{:S(2)}, u32[]{:S(2)}) collective-permute-start(f32[192,128]{1,0:T(8,128)S(1)} %get-tuple-element.27), channel_id=1, source_target_pairs={{0,4},{1,2},{2,1},{3,7},{4,0},{5,6},{6,5},{7,3},{8,12},{9,10},{10,... | collective-permute-start | bytes 294920 | tf_op jit(solution)/shard_map/ppermute | solution.py:839
  4.5 4.6 %collective-permute-start.4 = (f32[72,128]{1,0:T(8,128)S(1)}, f32[72,128]{1,0:T(8,128)S(1)}, u32[]{:S(2)}, u32[]{:S(2)}) collective-permute-start(f32[72,128]{1,0:T(8,128)S(1)} %shard_map.31), channel_id=1, source_target_pairs={{0,4},{1,18},{2,17},{3,7},{4,0},{5,22},{6,21},{7,3},{8,12},{9,26},... | collective-permute-start | bytes 110600 | tf_op jit(solution)/shard_map/ppermute | solution.py:839
  4.9 5.3 %collective-permute-start.3 = (f32[96,128]{1,0:T(8,128)S(1)}, f32[96,128]{1,0:T(8,128)S(1)}, u32[]{:S(2)}, u32[]{:S(2)}) collective-permute-start(f32[96,128]{1,0:T(8,128)S(1)} %shard_map.30), channel_id=1, source_target_pairs={{0,16},{16,0},{1,17},{17,1},{2,18},{18,2},{3,19},{19,3},{4,20},{20... | collective-permute-start | bytes 147464 | tf_op jit(solution)/shard_map/ppermute | solution.py:846
  6.5 2.6 %collective-permute-start.2 = (s32[8,128]{1,0:T(8,128)S(1)}, s32[8,128]{1,0:T(8,128)S(1)}, u32[]{:S(2)}, u32[]{:S(2)}) collective-permute-start(s32[8,128]{1,0:T(8,128)S(1)} %copy-done.2), channel_id=1, source_target_pairs={{0,1},{1,0},{2,3},{3,2},{4,5},{5,4},{6,7},{7,6},{8,9},{9,8},{10,11... | collective-permute-start | bytes 12296 | tf_op jit(solution)/shard_map/ppermute | solution.py:839
  6.5 9.6 %collective-permute-start.5 = (f32[128,128]{1,0:T(8,128)S(1)}, f32[128,128]{1,0:T(8,128)S(1)}, u32[]{:S(2)}, u32[]{:S(2)}) collective-permute-start(f32[128,128]{1,0:T(8,128)S(1)} %get-tuple-element.35), channel_id=1, source_target_pairs={{0,16},{16,0},{1,17},{17,1},{2,18},{18,2},{3,19},{19,3},{4,20},{20... | collective-permute-start | bytes 196616 | tf_op jit(solution)/shard_map/ppermute | solution.py:846
  7.9 8.3 %collective-permute-start.6 = (f32[128,128]{1,0:T(8,128)S(1)}, f32[128,128]{1,0:T(8,128)S(1)}, u32[]{:S(2)}, u32[]{:S(2)}) collective-permute-start(f32[128,128]{1,0:T(8,128)S(1)} %get-tuple-element.36), channel_id=1, source_target_pairs={{0,16},{16,0},{1,17},{17,1},{2,18},{18,2},{3,19},{19,3},{4,20},{20... | collective-permute-start | bytes 196616 | tf_op jit(solution)/shard_map/ppermute | solution.py:846
  9.3 6.9 %collective-permute-start.7 = (f32[128,128]{1,0:T(8,128)S(1)}, f32[128,128]{1,0:T(8,128)S(1)}, u32[]{:S(2)}, u32[]{:S(2)}) collective-permute-start(f32[128,128]{1,0:T(8,128)S(1)} %shard_map.34), channel_id=1, source_target_pairs={{0,16},{16,0},{1,17},{17,1},{2,18},{18,2},{3,19},{19,3},{4,20},{20... | collective-permute-start | bytes 196616 | tf_op jit(solution)/shard_map/ppermute | solution.py:846
  10.3 5.7 %collective-permute-start.8 = (f32[48,128]{1,0:T(8,128)S(1)}, f32[48,128]{1,0:T(8,128)S(1)}, u32[]{:S(2)}, u32[]{:S(2)}) collective-permute-start(f32[48,128]{1,0:T(8,128)S(1)} %get-tuple-element.37.own_east), channel_id=1, source_target_pairs={{0,4},{4,8},{8,12},{12,0},{1,5},{5,9},{9,13},{13,1},{2,6},{6,10},{... | collective-permute-start | bytes 73736 | tf_op jit(solution)/shard_map/ppermute | solution.py:853
  11.9 4.2 %collective-permute-start.9 = (f32[48,128]{1,0:T(8,128)S(1)}, f32[48,128]{1,0:T(8,128)S(1)}, u32[]{:S(2)}, u32[]{:S(2)}) collective-permute-start(f32[48,128]{1,0:T(8,128)S(1)} %get-tuple-element.38.own_west), channel_id=1, source_target_pairs={{0,12},{4,0},{8,4},{12,8},{1,13},{5,1},{9,5},{13,9},{2,14},{6,2},{... | collective-permute-start | bytes 73736 | tf_op jit(solution)/shard_map/ppermute | solution.py:853

commit v7 on v6

--- a/solution.py
+++ b/solution.py
@@ -611,15 +611,24 @@
                 jnp.where(lane == 0, to_lane(from_west[0 : sz.rows, :], lane_at, 0), moved_w[here, :]),
             )
 
+        total = jnp.zeros(tile, jnp.float32)
+        for k in range(sz.lev - 1, -1, -1):
+            at = k * sz.rows
+            _, wet_e, wet_w, _, _ = masks(k)
+            zonal_mid, _, zonal_west = around(0, k)
+            div_far = around_n[5 * sz.slab + at : 5 * sz.slab + at + sz.rows, :]
+            total = total + (keep(wet_e, zonal_mid) - keep(wet_w, zonal_west) + div_far)
+            out[4, at : at + sz.rows, :] = -total if k > 0 else jnp.zeros(tile, jnp.float32)
+            if k % chunk == 0:
+                send(4, 5, k // chunk)
         press_e, warm_above = jnp.zeros(tile, jnp.float32), None
         for k in range(sz.lev):
             at = k * sz.rows
             wet, wet_e, wet_w, wet_n, _ = masks(k)
             zonal, merid, temper, saline, visc = (around(f, k) for f in range(5))
-            zonal_far, merid_far, temper_far, saline_far, press, div_far = (
-                around_n[f * sz.slab + at : f * sz.slab + at + sz.rows, :] for f in range(6)
+            zonal_far, merid_far, temper_far, saline_far, press = (
+                around_n[f * sz.slab + at : f * sz.slab + at + sz.rows, :] for f in range(5)
             )
-            div[at : at + sz.rows, :] = keep(wet_e, zonal[0]) - keep(wet_w, zonal[2]) + div_far
             coef_e = keep(wet_e, 0.5 * (visc[0] + visc[1]))
             coef_w = keep(wet_w, 0.5 * (visc[2] + visc[0]))
 
@@ -644,13 +653,6 @@
             if k % chunk == chunk - 1:
                 send(0, 4, k // chunk)
                 send(5, 6, k // chunk)
-        total = jnp.zeros(tile, jnp.float32)
-        for k in range(sz.lev - 1, -1, -1):
-            at = k * sz.rows
-            total = total + div[at : at + sz.rows, :]
-            out[4, at : at + sz.rows, :] = -total if k > 0 else jnp.zeros(tile, jnp.float32)
-            if k % chunk == 0:
-                send(4, 5, k // chunk)
 
     tall = (sz.lev, sz.cols)
 

time: 17.4 us -> 17.3 us (level)
  no operation moved by 1% of the time
where the time goes in v7:
time: 17.3 us; the launch traced here: 17.2 us
  starting transfers between devices  12.2 us (71%)
  Pallas kernels  2.46 us (14%)
  waiting for transfers between devices  1.5 us (9%)
  local copies, waits for them, and re-layouts  1 us (6%)
    ppermute x4, starting transfers between devices, from_dynamics(): lax.ppermute(value, 'sect', [(s, (s + hop) % count_s) for s in range(coun...  4.9 us
    ppermute x2, starting transfers between devices, around(): lax.ppermute(value, 'lon', [(i, (i + step) % count_o) for i in range(coun...  3.84 us
    ppermute x4, starting transfers between devices, swap(): return lax.ppermute(value, ('sect', 'lon', 'lat'), pairs)  3.44 us
    pallas_call x9, Pallas kernels, call_kernel(): pl.pallas_call(body, out_shape=[jax.ShapeDtypeStruct(shape, jnp.float32)...  2.46 us
    ppermute x2, waiting for transfers between devices, around(): lax.ppermute(value, 'lon', [(i, (i + step) % count_o) for i in range(coun...  1.47 us
    unnamed x6, local copies, waits for them, and re-layouts  1 us
  transfers between devices with their start and end apart: 10, of which 1 were waited for; matrix products, arithmetic and copies ran while one was open for 0% of the time, Pallas kernels for 7%

profile of v7, /device:TPU:0, one launch (start us, length us, event | category | flops | bytes accessed | tf_op | source)
XLA Modules:
  0.0 17.2 jit_solution(9181392920703657670)
XLA Ops:
  0.0 0.0 copy-start
  0.0 1.0 %copy-done = f32[1,6,16,8,128]{4,3,2,1,0:T(8,128)S(1)} copy-done((f32[1,6,16,8,128]{4,3,2,1,0:T(8,128)S(1)}, f32[1,6,16,8,128]{4,3,2,1,0:T(8,128)}, u32[]{:S(2)}) %copy-start) | copy-done | bytes 393240
  1.0 0.0 copy-start.2
  1.0 0.3 %shard_map.28 = (f32[192,128]{1,0:T(8,128)S(1)}, f32[192,128]{1,0:T(8,128)S(1)}, f32[32,128]{1,0:T(8,128)S(1)}, f32[128,128]{1,0:T(8,128)S(1)}, f32[128,128]{1,0:T(8,128)S(1)}) custom-call(f32[768,128]{1,0:T(8,128)S(1)} %bitcast.2), custom_call_target="tpu_custom_call" | custom-call | tf_op jit(solution)/shard_map/pallas_call | solution.py:30
  1.3 0.5 %collective-permute-start = (f32[192,128]{1,0:T(8,128)S(1)}, f32[192,128]{1,0:T(8,128)S(1)}, u32[]{:S(2)}, u32[]{:S(2)}) collective-permute-start(f32[192,128]{1,0:T(8,128)S(1)} %get-tuple-element.26), channel_id=1, source_target_pairs={{0,1},{1,0},{2,3},{3,2},{4,5},{5,4},{6,7},{7,6},{8,9},{9,8},{10,11... | collective-permute-start | bytes 294920 | tf_op jit(solution)/shard_map/ppermute | solution.py:841
  1.7 0.0 copy-start.1
  1.7 2.7 %collective-permute-start.1 = (f32[192,128]{1,0:T(8,128)S(1)}, f32[192,128]{1,0:T(8,128)S(1)}, u32[]{:S(2)}, u32[]{:S(2)}) collective-permute-start(f32[192,128]{1,0:T(8,128)S(1)} %get-tuple-element.27), channel_id=1, source_target_pairs={{0,4},{1,2},{2,1},{3,7},{4,0},{5,6},{6,5},{7,3},{8,12},{9,10},{10,... | collective-permute-start | bytes 294920 | tf_op jit(solution)/shard_map/ppermute | solution.py:841
  4.4 0.0 copy-done.2
  4.4 0.1 shard_map.31
  4.5 0.3 %collective-permute-start.4 = (f32[72,128]{1,0:T(8,128)S(1)}, f32[72,128]{1,0:T(8,128)S(1)}, u32[]{:S(2)}, u32[]{:S(2)}) collective-permute-start(f32[72,128]{1,0:T(8,128)S(1)} %shard_map.31), channel_id=1, source_target_pairs={{0,4},{1,18},{2,17},{3,7},{4,0},{5,22},{6,21},{7,3},{8,12},{9,26},... | collective-permute-start | bytes 110600 | tf_op jit(solution)/shard_map/ppermute | solution.py:841
  4.8 0.0 collective-permute-done.row_a
  4.8 0.1 shard_map.30
  4.9 1.6 %collective-permute-start.3 = (f32[96,128]{1,0:T(8,128)S(1)}, f32[96,128]{1,0:T(8,128)S(1)}, u32[]{:S(2)}, u32[]{:S(2)}) collective-permute-start(f32[96,128]{1,0:T(8,128)S(1)} %shard_map.30), channel_id=1, source_target_pairs={{0,16},{16,0},{1,17},{17,1},{2,18},{18,2},{3,19},{19,3},{4,20},{20... | collective-permute-start | bytes 147464 | tf_op jit(solution)/shard_map/ppermute | solution.py:848
  6.5 0.0 collective-permute-start.2
  6.5 1.3 %collective-permute-start.5 = (f32[128,128]{1,0:T(8,128)S(1)}, f32[128,128]{1,0:T(8,128)S(1)}, u32[]{:S(2)}, u32[]{:S(2)}) collective-permute-start(f32[128,128]{1,0:T(8,128)S(1)} %get-tuple-element.35), channel_id=1, source_target_pairs={{0,16},{16,0},{1,17},{17,1},{2,18},{18,2},{3,19},{19,3},{4,20},{20... | collective-permute-start | bytes 196616 | tf_op jit(solution)/shard_map/ppermute | solution.py:848
  7.8 0.0 collective-permute-done.1.row_b
  7.9 1.1 %collective-permute-start.6 = (f32[128,128]{1,0:T(8,128)S(1)}, f32[128,128]{1,0:T(8,128)S(1)}, u32[]{:S(2)}, u32[]{:S(2)}) collective-permute-start(f32[128,128]{1,0:T(8,128)S(1)} %get-tuple-element.36), channel_id=1, source_target_pairs={{0,16},{16,0},{1,17},{17,1},{2,18},{18,2},{3,19},{19,3},{4,20},{20... | collective-permute-start | bytes 196616 | tf_op jit(solution)/shard_map/ppermute | solution.py:848
  8.9 0.1 shard_map.29
  9.1 0.0 collective-permute-done.2.levels_a
  9.1 0.0 collective-permute-done.4.cross_b
  9.1 0.0 copy-done.1
  9.1 0.2 %shard_map.34 = f32[128,128]{1,0:T(8,128)S(1)} custom-call(f32[768,128]{1,0:T(8,128)S(1)} %bitcast.4, s32[8,128]{1,0:T(8,128)S(1)} %copy-done.2, s32[8,128]{1,0:T(8,128)S(1)} %collective-permute-done.2.levels_a, f32[72,128]{1,0:T(8,128)S(1)} %collective-permute-done.4.cross_b, f32[192,128]{1,0:T(8,128)S(1)} %get-tuple-element.28.south, ...), custom_call_target="tpu_custom_call" | custom-call | tf_op jit(solution)/shard_map/pallas_call | solution.py:30
  9.3 0.9 %collective-permute-start.7 = (f32[128,128]{1,0:T(8,128)S(1)}, f32[128,128]{1,0:T(8,128)S(1)}, u32[]{:S(2)}, u32[]{:S(2)}) collective-permute-start(f32[128,128]{1,0:T(8,128)S(1)} %shard_map.34), channel_id=1, source_target_pairs={{0,16},{16,0},{1,17},{17,1},{2,18},{18,2},{3,19},{19,3},{4,20},{20... | collective-permute-start | bytes 196616 | tf_op jit(solution)/shard_map/ppermute | solution.py:848
  10.1 0.0 collective-permute-done.3.twin.side
  10.1 0.2 shard_map.32
  10.3 1.6 %collective-permute-start.8 = (f32[48,128]{1,0:T(8,128)S(1)}, f32[48,128]{1,0:T(8,128)S(1)}, u32[]{:S(2)}, u32[]{:S(2)}) collective-permute-start(f32[48,128]{1,0:T(8,128)S(1)} %get-tuple-element.37.own_east), channel_id=1, source_target_pairs={{0,4},{4,8},{8,12},{12,0},{1,5},{5,9},{9,13},{13,1},{2,6},{6,10},{... | collective-permute-start | bytes 73736 | tf_op jit(solution)/shard_map/ppermute | solution.py:855
  11.9 2.2 %collective-permute-start.9 = (f32[48,128]{1,0:T(8,128)S(1)}, f32[48,128]{1,0:T(8,128)S(1)}, u32[]{:S(2)}, u32[]{:S(2)}) collective-permute-start(f32[48,128]{1,0:T(8,128)S(1)} %get-tuple-element.38.own_west), channel_id=1, source_target_pairs={{0,12},{4,0},{8,4},{12,8},{1,13},{5,1},{9,5},{13,9},{2,14},{6,2},{... | collective-permute-start | bytes 73736 | tf_op jit(solution)/shard_map/ppermute | solution.py:855
  14.2 0.4 %shard_map.33 = (f32[768,128]{1,0:T(8,128)S(1)}, f32[768,128]{1,0:T(8,128)S(1)}, f32[768,128]{1,0:T(8,128)S(1)}, f32[768,128]{1,0:T(8,128)S(1)}, f32[768,128]{1,0:T(8,128)S(1)}) custom-call(f32[768,128]{1,0:T(8,128)S(1)} %bitcast.5, s32[8,128]{1,0:T(8,128)S(1)} %copy-done.2, f32[192,128]{1,0:T(8,128)S(1)} %get-tuple-element.28.south, ...), custom_call_target="tpu_custom_call" | custom-call | tf_op jit(solution)/shard_map/pallas_call | solution.py:30
  14.6 1.5 %collective-permute-done.8.from_west = f32[48,128]{1,0:T(8,128)S(1)} collective-permute-done((f32[48,128]{1,0:T(8,128)S(1)}, f32[48,128]{1,0:T(8,128)S(1)}, u32[]{:S(2)}, u32[]{:S(2)}) %collective-permute-start.8) | collective-permute-done | bytes 24608 | tf_op jit(solution)/shard_map/ppermute | solution.py:855
  16.1 0.0 collective-permute-done.9.from_east
  16.1 0.1 shard_map.35
  16.1 0.0 collective-permute-done.5.zonal_in
  16.1 0.0 collective-permute-done.6.merid_in
  16.1 0.0 collective-permute-done.7.mixing_in
  16.1 1.1 %shard_map.36 = f32[6,128,128]{2,1,0:T(8,128)} custom-call(f32[768,128]{1,0:T(8,128)S(1)} %get-tuple-element.34.fields, s32[8,128]{1,0:T(8,128)S(1)} %copy-done.2, f32[192,128]{1,0:T(8,128)S(1)} %get-tuple-element.28.south, f32[192,128]{1,0:T(8,128)S(1)} %get-tuple-element.29.north, f32[72,128]{1,0:T(8,128)S(1)} %get-tuple-element.32.cross_south, ...), custom_call_target="tpu_custom_call" | custom-call | tf_op jit(solution)/shard_map/pallas_call | solution.py:30
Async XLA Ops:
  0.0 1.0 %copy-start = (f32[1,6,16,8,128]{4,3,2,1,0:T(8,128)S(1)}, f32[1,6,16,8,128]{4,3,2,1,0:T(8,128)}, u32[]{:S(2)}) copy-start(f32[1,6,16,8,128]{4,3,2,1,0:T(8,128)} %param.2) | copy-start | bytes 1179652
  1.0 3.4 %copy-start.2 = (s32[8,128]{1,0:T(8,128)S(1)}, s32[8,128]{1,0:T(8,128)}, u32[]{:S(2)}) copy-start(s32[8,128]{1,0:T(8,128)} %levels.11) | copy-start | bytes 12292
  1.3 3.5 %collective-permute-start = (f32[192,128]{1,0:T(8,128)S(1)}, f32[192,128]{1,0:T(8,128)S(1)}, u32[]{:S(2)}, u32[]{:S(2)}) collective-permute-start(f32[192,128]{1,0:T(8,128)S(1)} %get-tuple-element.26), channel_id=1, source_target_pairs={{0,1},{1,0},{2,3},{3,2},{4,5},{5,4},{6,7},{7,6},{8,9},{9,8},{10,11... | collective-permute-start | bytes 294920 | tf_op jit(solution)/shard_map/ppermute | solution.py:841
  1.7 7.4 %copy-start.1 = (f32[1,6,16,8,128]{4,3,2,1,0:T(8,128)S(1)}, f32[1,6,16,8,128]{4,3,2,1,0:T(8,128)}, u32[]{:S(2)}) copy-start(f32[1,6,16,8,128]{4,3,2,1,0:T(8,128)} %param.2) | copy-start | bytes 1179652
  1.7 6.1 %collective-permute-start.1 = (f32[192,128]{1,0:T(8,128)S(1)}, f32[192,128]{1,0:T(8,128)S(1)}, u32[]{:S(2)}, u32[]{:S(2)}) collective-permute-start(f32[192,128]{1,0:T(8,128)S(1)} %get-tuple-element.27), channel_id=1, source_target_pairs={{0,4},{1,2},{2,1},{3,7},{4,0},{5,6},{6,5},{7,3},{8,12},{9,10},{10,... | collective-permute-start | bytes 294920 | tf_op jit(solution)/shard_map/ppermute | solution.py:841
  4.5 4.6 %collective-permute-start.4 = (f32[72,128]{1,0:T(8,128)S(1)}, f32[72,128]{1,0:T(8,128)S(1)}, u32[]{:S(2)}, u32[]{:S(2)}) collective-permute-start(f32[72,128]{1,0:T(8,128)S(1)} %shard_map.31), channel_id=1, source_target_pairs={{0,4},{1,18},{2,17},{3,7},{4,0},{5,22},{6,21},{7,3},{8,12},{9,26},... | collective-permute-start | bytes 110600 | tf_op jit(solution)/shard_map/ppermute | solution.py:841
  4.9 5.3 %collective-permute-start.3 = (f32[96,128]{1,0:T(8,128)S(1)}, f32[96,128]{1,0:T(8,128)S(1)}, u32[]{:S(2)}, u32[]{:S(2)}) collective-permute-start(f32[96,128]{1,0:T(8,128)S(1)} %shard_map.30), channel_id=1, source_target_pairs={{0,16},{16,0},{1,17},{17,1},{2,18},{18,2},{3,19},{19,3},{4,20},{20... | collective-permute-start | bytes 147464 | tf_op jit(solution)/shard_map/ppermute | solution.py:848
  6.5 2.6 %collective-permute-start.2 = (s32[8,128]{1,0:T(8,128)S(1)}, s32[8,128]{1,0:T(8,128)S(1)}, u32[]{:S(2)}, u32[]{:S(2)}) collective-permute-start(s32[8,128]{1,0:T(8,128)S(1)} %copy-done.2), channel_id=1, source_target_pairs={{0,1},{1,0},{2,3},{3,2},{4,5},{5,4},{6,7},{7,6},{8,9},{9,8},{10,11... | collective-permute-start | bytes 12296 | tf_op jit(solution)/shard_map/ppermute | solution.py:841
  6.5 9.6 %collective-permute-start.5 = (f32[128,128]{1,0:T(8,128)S(1)}, f32[128,128]{1,0:T(8,128)S(1)}, u32[]{:S(2)}, u32[]{:S(2)}) collective-permute-start(f32[128,128]{1,0:T(8,128)S(1)} %get-tuple-element.35), channel_id=1, source_target_pairs={{0,16},{16,0},{1,17},{17,1},{2,18},{18,2},{3,19},{19,3},{4,20},{20... | collective-permute-start | bytes 196616 | tf_op jit(solution)/shard_map/ppermute | solution.py:848
  7.9 8.3 %collective-permute-start.6 = (f32[128,128]{1,0:T(8,128)S(1)}, f32[128,128]{1,0:T(8,128)S(1)}, u32[]{:S(2)}, u32[]{:S(2)}) collective-permute-start(f32[128,128]{1,0:T(8,128)S(1)} %get-tuple-element.36), channel_id=1, source_target_pairs={{0,16},{16,0},{1,17},{17,1},{2,18},{18,2},{3,19},{19,3},{4,20},{20... | collective-permute-start | bytes 196616 | tf_op jit(solution)/shard_map/ppermute | solution.py:848
  9.3 6.9 %collective-permute-start.7 = (f32[128,128]{1,0:T(8,128)S(1)}, f32[128,128]{1,0:T(8,128)S(1)}, u32[]{:S(2)}, u32[]{:S(2)}) collective-permute-start(f32[128,128]{1,0:T(8,128)S(1)} %shard_map.34), channel_id=1, source_target_pairs={{0,16},{16,0},{1,17},{17,1},{2,18},{18,2},{3,19},{19,3},{4,20},{20... | collective-permute-start | bytes 196616 | tf_op jit(solution)/shard_map/ppermute | solution.py:848
  10.3 5.7 %collective-permute-start.8 = (f32[48,128]{1,0:T(8,128)S(1)}, f32[48,128]{1,0:T(8,128)S(1)}, u32[]{:S(2)}, u32[]{:S(2)}) collective-permute-start(f32[48,128]{1,0:T(8,128)S(1)} %get-tuple-element.37.own_east), channel_id=1, source_target_pairs={{0,4},{4,8},{8,12},{12,0},{1,5},{5,9},{9,13},{13,1},{2,6},{6,10},{... | collective-permute-start | bytes 73736 | tf_op jit(solution)/shard_map/ppermute | solution.py:855
  11.9 4.2 %collective-permute-start.9 = (f32[48,128]{1,0:T(8,128)S(1)}, f32[48,128]{1,0:T(8,128)S(1)}, u32[]{:S(2)}, u32[]{:S(2)}) collective-permute-start(f32[48,128]{1,0:T(8,128)S(1)} %get-tuple-element.38.own_west), channel_id=1, source_target_pairs={{0,12},{4,0},{8,4},{12,8},{1,13},{5,1},{9,5},{13,9},{2,14},{6,2},{... | collective-permute-start | bytes 73736 | tf_op jit(solution)/shard_map/ppermute | solution.py:855

commit v8 on v7

--- a/solution.py
+++ b/solution.py
@@ -16,7 +16,7 @@
 RICHARDSON = 1.0
 
 VMEM_LIMIT = 8 * 1024 * 1024
-CHUNKS = 2
+CHUNKS = 1
 
 ZONAL_ROW, MERID_ROW, MERID_ROW2, END_ROW, LEVEL_ROW = range(5)
 TEMPER_END, VISC_END = 0, 2

time: 17.3 us -> 17.4 us (level)
  no operation moved by 1% of the time
where the time goes in v8:
time: 17.4 us; the launch traced here: 17.2 us
  starting transfers between devices  12.2 us (70%)
  Pallas kernels  2.49 us (14%)
  waiting for transfers between devices  1.5 us (9%)
  local copies, waits for them, and re-layouts  1 us (6%)
    ppermute x4, starting transfers between devices, from_dynamics(): lax.ppermute(value, 'sect', [(s, (s + hop) % count_s) for s in range(coun...  4.9 us
    ppermute x2, starting transfers between devices, around(): lax.ppermute(value, 'lon', [(i, (i + step) % count_o) for i in range(coun...  3.84 us
    ppermute x4, starting transfers between devices, swap(): return lax.ppermute(value, ('sect', 'lon', 'lat'), pairs)  3.44 us
    pallas_call x9, Pallas kernels, call_kernel(): pl.pallas_call(body, out_shape=[jax.ShapeDtypeStruct(shape, jnp.float32)...  2.49 us
    ppermute x2, waiting for transfers between devices, around(): lax.ppermute(value, 'lon', [(i, (i + step) % count_o) for i in range(coun...  1.47 us
    unnamed x6, local copies, waits for them, and re-layouts  1 us
  transfers between devices with their start and end apart: 10, of which 1 were waited for; matrix products, arithmetic and copies ran while one was open for 0% of the time, Pallas kernels for 7%

profile of v8, /device:TPU:0, one launch (start us, length us, event | category | flops | bytes accessed | tf_op | source)
XLA Modules:
  0.0 17.2 jit_solution(2593691102771000853)
XLA Ops:
  0.0 0.0 copy-start
  0.0 1.0 %copy-done = f32[1,6,16,8,128]{4,3,2,1,0:T(8,128)S(1)} copy-done((f32[1,6,16,8,128]{4,3,2,1,0:T(8,128)S(1)}, f32[1,6,16,8,128]{4,3,2,1,0:T(8,128)}, u32[]{:S(2)}) %copy-start) | copy-done | bytes 393240
  1.0 0.0 copy-start.2
  1.0 0.3 %shard_map.28 = (f32[192,128]{1,0:T(8,128)S(1)}, f32[192,128]{1,0:T(8,128)S(1)}, f32[32,128]{1,0:T(8,128)S(1)}, f32[128,128]{1,0:T(8,128)S(1)}, f32[128,128]{1,0:T(8,128)S(1)}) custom-call(f32[768,128]{1,0:T(8,128)S(1)} %bitcast.2), custom_call_target="tpu_custom_call" | custom-call | tf_op jit(solution)/shard_map/pallas_call | solution.py:30
  1.3 0.5 %collective-permute-start = (f32[192,128]{1,0:T(8,128)S(1)}, f32[192,128]{1,0:T(8,128)S(1)}, u32[]{:S(2)}, u32[]{:S(2)}) collective-permute-start(f32[192,128]{1,0:T(8,128)S(1)} %get-tuple-element.26), channel_id=1, source_target_pairs={{0,1},{1,0},{2,3},{3,2},{4,5},{5,4},{6,7},{7,6},{8,9},{9,8},{10,11... | collective-permute-start | bytes 294920 | tf_op jit(solution)/shard_map/ppermute | solution.py:841
  1.7 0.0 copy-start.1
  1.7 2.7 %collective-permute-start.1 = (f32[192,128]{1,0:T(8,128)S(1)}, f32[192,128]{1,0:T(8,128)S(1)}, u32[]{:S(2)}, u32[]{:S(2)}) collective-permute-start(f32[192,128]{1,0:T(8,128)S(1)} %get-tuple-element.27), channel_id=1, source_target_pairs={{0,4},{1,2},{2,1},{3,7},{4,0},{5,6},{6,5},{7,3},{8,12},{9,10},{10,... | collective-permute-start | bytes 294920 | tf_op jit(solution)/shard_map/ppermute | solution.py:841
  4.4 0.0 copy-done.2
  4.4 0.1 shard_map.31
  4.5 0.3 %collective-permute-start.4 = (f32[72,128]{1,0:T(8,128)S(1)}, f32[72,128]{1,0:T(8,128)S(1)}, u32[]{:S(2)}, u32[]{:S(2)}) collective-permute-start(f32[72,128]{1,0:T(8,128)S(1)} %shard_map.31), channel_id=1, source_target_pairs={{0,4},{1,18},{2,17},{3,7},{4,0},{5,22},{6,21},{7,3},{8,12},{9,26},... | collective-permute-start | bytes 110600 | tf_op jit(solution)/shard_map/ppermute | solution.py:841
  4.8 0.0 collective-permute-done.row_a
  4.8 0.1 shard_map.30
  4.9 1.6 %collective-permute-start.3 = (f32[96,128]{1,0:T(8,128)S(1)}, f32[96,128]{1,0:T(8,128)S(1)}, u32[]{:S(2)}, u32[]{:S(2)}) collective-permute-start(f32[96,128]{1,0:T(8,128)S(1)} %shard_map.30), channel_id=1, source_target_pairs={{0,16},{16,0},{1,17},{17,1},{2,18},{18,2},{3,19},{19,3},{4,20},{20... | collective-permute-start | bytes 147464 | tf_op jit(solution)/shard_map/ppermute | solution.py:848
  6.5 0.0 collective-permute-start.2
  6.5 1.3 %collective-permute-start.5 = (f32[128,128]{1,0:T(8,128)S(1)}, f32[128,128]{1,0:T(8,128)S(1)}, u32[]{:S(2)}, u32[]{:S(2)}) collective-permute-start(f32[128,128]{1,0:T(8,128)S(1)} %get-tuple-element.35), channel_id=1, source_target_pairs={{0,16},{16,0},{1,17},{17,1},{2,18},{18,2},{3,19},{19,3},{4,20},{20... | collective-permute-start | bytes 196616 | tf_op jit(solution)/shard_map/ppermute | solution.py:848
  7.8 0.0 collective-permute-done.1.row_b
  7.9 1.1 %collective-permute-start.6 = (f32[128,128]{1,0:T(8,128)S(1)}, f32[128,128]{1,0:T(8,128)S(1)}, u32[]{:S(2)}, u32[]{:S(2)}) collective-permute-start(f32[128,128]{1,0:T(8,128)S(1)} %get-tuple-element.36), channel_id=1, source_target_pairs={{0,16},{16,0},{1,17},{17,1},{2,18},{18,2},{3,19},{19,3},{4,20},{20... | collective-permute-start | bytes 196616 | tf_op jit(solution)/shard_map/ppermute | solution.py:848
  8.9 0.1 shard_map.29
  9.1 0.0 collective-permute-done.2.levels_a
  9.1 0.0 collective-permute-done.4.cross_b
  9.1 0.0 copy-done.1
  9.1 0.2 %shard_map.34 = f32[128,128]{1,0:T(8,128)S(1)} custom-call(f32[768,128]{1,0:T(8,128)S(1)} %bitcast.4, s32[8,128]{1,0:T(8,128)S(1)} %copy-done.2, s32[8,128]{1,0:T(8,128)S(1)} %collective-permute-done.2.levels_a, f32[72,128]{1,0:T(8,128)S(1)} %collective-permute-done.4.cross_b, f32[192,128]{1,0:T(8,128)S(1)} %get-tuple-element.28.south, ...), custom_call_target="tpu_custom_call" | custom-call | tf_op jit(solution)/shard_map/pallas_call | solution.py:30
  9.3 0.9 %collective-permute-start.7 = (f32[128,128]{1,0:T(8,128)S(1)}, f32[128,128]{1,0:T(8,128)S(1)}, u32[]{:S(2)}, u32[]{:S(2)}) collective-permute-start(f32[128,128]{1,0:T(8,128)S(1)} %shard_map.34), channel_id=1, source_target_pairs={{0,16},{16,0},{1,17},{17,1},{2,18},{18,2},{3,19},{19,3},{4,20},{20... | collective-permute-start | bytes 196616 | tf_op jit(solution)/shard_map/ppermute | solution.py:848
  10.1 0.0 collective-permute-done.3.twin.side
  10.1 0.2 shard_map.32
  10.3 1.6 %collective-permute-start.8 = (f32[48,128]{1,0:T(8,128)S(1)}, f32[48,128]{1,0:T(8,128)S(1)}, u32[]{:S(2)}, u32[]{:S(2)}) collective-permute-start(f32[48,128]{1,0:T(8,128)S(1)} %get-tuple-element.37.own_east), channel_id=1, source_target_pairs={{0,4},{4,8},{8,12},{12,0},{1,5},{5,9},{9,13},{13,1},{2,6},{6,10},{... | collective-permute-start | bytes 73736 | tf_op jit(solution)/shard_map/ppermute | solution.py:855
  11.9 2.2 %collective-permute-start.9 = (f32[48,128]{1,0:T(8,128)S(1)}, f32[48,128]{1,0:T(8,128)S(1)}, u32[]{:S(2)}, u32[]{:S(2)}) collective-permute-start(f32[48,128]{1,0:T(8,128)S(1)} %get-tuple-element.38.own_west), channel_id=1, source_target_pairs={{0,12},{4,0},{8,4},{12,8},{1,13},{5,1},{9,5},{13,9},{2,14},{6,2},{... | collective-permute-start | bytes 73736 | tf_op jit(solution)/shard_map/ppermute | solution.py:855
  14.2 0.4 %shard_map.33 = (f32[768,128]{1,0:T(8,128)S(1)}, f32[768,128]{1,0:T(8,128)S(1)}, f32[768,128]{1,0:T(8,128)S(1)}, f32[768,128]{1,0:T(8,128)S(1)}, f32[768,128]{1,0:T(8,128)S(1)}) custom-call(f32[768,128]{1,0:T(8,128)S(1)} %bitcast.5, s32[8,128]{1,0:T(8,128)S(1)} %copy-done.2, f32[192,128]{1,0:T(8,128)S(1)} %get-tuple-element.28.south, ...), custom_call_target="tpu_custom_call" | custom-call | tf_op jit(solution)/shard_map/pallas_call | solution.py:30
  14.6 1.5 %collective-permute-done.8.from_west = f32[48,128]{1,0:T(8,128)S(1)} collective-permute-done((f32[48,128]{1,0:T(8,128)S(1)}, f32[48,128]{1,0:T(8,128)S(1)}, u32[]{:S(2)}, u32[]{:S(2)}) %collective-permute-start.8) | collective-permute-done | bytes 24608 | tf_op jit(solution)/shard_map/ppermute | solution.py:855
  16.1 0.0 collective-permute-done.9.from_east
  16.1 0.1 shard_map.35
  16.1 0.0 collective-permute-done.5.zonal_in
  16.1 0.0 collective-permute-done.6.merid_in
  16.1 0.0 collective-permute-done.7.mixing_in
  16.1 1.1 %shard_map.36 = f32[6,128,128]{2,1,0:T(8,128)} custom-call(f32[768,128]{1,0:T(8,128)S(1)} %get-tuple-element.34.fields, s32[8,128]{1,0:T(8,128)S(1)} %copy-done.2, f32[192,128]{1,0:T(8,128)S(1)} %get-tuple-element.28.south, f32[192,128]{1,0:T(8,128)S(1)} %get-tuple-element.29.north, f32[72,128]{1,0:T(8,128)S(1)} %get-tuple-element.32.cross_south, ...), custom_call_target="tpu_custom_call" | custom-call | tf_op jit(solution)/shard_map/pallas_call | solution.py:30
Async XLA Ops:
  0.0 1.0 %copy-start = (f32[1,6,16,8,128]{4,3,2,1,0:T(8,128)S(1)}, f32[1,6,16,8,128]{4,3,2,1,0:T(8,128)}, u32[]{:S(2)}) copy-start(f32[1,6,16,8,128]{4,3,2,1,0:T(8,128)} %param.2) | copy-start | bytes 1179652
  1.0 3.4 %copy-start.2 = (s32[8,128]{1,0:T(8,128)S(1)}, s32[8,128]{1,0:T(8,128)}, u32[]{:S(2)}) copy-start(s32[8,128]{1,0:T(8,128)} %levels.11) | copy-start | bytes 12292
  1.3 3.5 %collective-permute-start = (f32[192,128]{1,0:T(8,128)S(1)}, f32[192,128]{1,0:T(8,128)S(1)}, u32[]{:S(2)}, u32[]{:S(2)}) collective-permute-start(f32[192,128]{1,0:T(8,128)S(1)} %get-tuple-element.26), channel_id=1, source_target_pairs={{0,1},{1,0},{2,3},{3,2},{4,5},{5,4},{6,7},{7,6},{8,9},{9,8},{10,11... | collective-permute-start | bytes 294920 | tf_op jit(solution)/shard_map/ppermute | solution.py:841
  1.7 7.4 %copy-start.1 = (f32[1,6,16,8,128]{4,3,2,1,0:T(8,128)S(1)}, f32[1,6,16,8,128]{4,3,2,1,0:T(8,128)}, u32[]{:S(2)}) copy-start(f32[1,6,16,8,128]{4,3,2,1,0:T(8,128)} %param.2) | copy-start | bytes 1179652
  1.7 6.1 %collective-permute-start.1 = (f32[192,128]{1,0:T(8,128)S(1)}, f32[192,128]{1,0:T(8,128)S(1)}, u32[]{:S(2)}, u32[]{:S(2)}) collective-permute-start(f32[192,128]{1,0:T(8,128)S(1)} %get-tuple-element.27), channel_id=1, source_target_pairs={{0,4},{1,2},{2,1},{3,7},{4,0},{5,6},{6,5},{7,3},{8,12},{9,10},{10,... | collective-permute-start | bytes 294920 | tf_op jit(solution)/shard_map/ppermute | solution.py:841
  4.5 4.6 %collective-permute-start.4 = (f32[72,128]{1,0:T(8,128)S(1)}, f32[72,128]{1,0:T(8,128)S(1)}, u32[]{:S(2)}, u32[]{:S(2)}) collective-permute-start(f32[72,128]{1,0:T(8,128)S(1)} %shard_map.31), channel_id=1, source_target_pairs={{0,4},{1,18},{2,17},{3,7},{4,0},{5,22},{6,21},{7,3},{8,12},{9,26},... | collective-permute-start | bytes 110600 | tf_op jit(solution)/shard_map/ppermute | solution.py:841
  4.9 5.3 %collective-permute-start.3 = (f32[96,128]{1,0:T(8,128)S(1)}, f32[96,128]{1,0:T(8,128)S(1)}, u32[]{:S(2)}, u32[]{:S(2)}) collective-permute-start(f32[96,128]{1,0:T(8,128)S(1)} %shard_map.30), channel_id=1, source_target_pairs={{0,16},{16,0},{1,17},{17,1},{2,18},{18,2},{3,19},{19,3},{4,20},{20... | collective-permute-start | bytes 147464 | tf_op jit(solution)/shard_map/ppermute | solution.py:848
  6.5 2.6 %collective-permute-start.2 = (s32[8,128]{1,0:T(8,128)S(1)}, s32[8,128]{1,0:T(8,128)S(1)}, u32[]{:S(2)}, u32[]{:S(2)}) collective-permute-start(s32[8,128]{1,0:T(8,128)S(1)} %copy-done.2), channel_id=1, source_target_pairs={{0,1},{1,0},{2,3},{3,2},{4,5},{5,4},{6,7},{7,6},{8,9},{9,8},{10,11... | collective-permute-start | bytes 12296 | tf_op jit(solution)/shard_map/ppermute | solution.py:841
  6.5 9.6 %collective-permute-start.5 = (f32[128,128]{1,0:T(8,128)S(1)}, f32[128,128]{1,0:T(8,128)S(1)}, u32[]{:S(2)}, u32[]{:S(2)}) collective-permute-start(f32[128,128]{1,0:T(8,128)S(1)} %get-tuple-element.35), channel_id=1, source_target_pairs={{0,16},{16,0},{1,17},{17,1},{2,18},{18,2},{3,19},{19,3},{4,20},{20... | collective-permute-start | bytes 196616 | tf_op jit(solution)/shard_map/ppermute | solution.py:848
  7.9 8.3 %collective-permute-start.6 = (f32[128,128]{1,0:T(8,128)S(1)}, f32[128,128]{1,0:T(8,128)S(1)}, u32[]{:S(2)}, u32[]{:S(2)}) collective-permute-start(f32[128,128]{1,0:T(8,128)S(1)} %get-tuple-element.36), channel_id=1, source_target_pairs={{0,16},{16,0},{1,17},{17,1},{2,18},{18,2},{3,19},{19,3},{4,20},{20... | collective-permute-start | bytes 196616 | tf_op jit(solution)/shard_map/ppermute | solution.py:848
  9.3 6.9 %collective-permute-start.7 = (f32[128,128]{1,0:T(8,128)S(1)}, f32[128,128]{1,0:T(8,128)S(1)}, u32[]{:S(2)}, u32[]{:S(2)}) collective-permute-start(f32[128,128]{1,0:T(8,128)S(1)} %shard_map.34), channel_id=1, source_target_pairs={{0,16},{16,0},{1,17},{17,1},{2,18},{18,2},{3,19},{19,3},{4,20},{20... | collective-permute-start | bytes 196616 | tf_op jit(solution)/shard_map/ppermute | solution.py:848
  10.3 5.7 %collective-permute-start.8 = (f32[48,128]{1,0:T(8,128)S(1)}, f32[48,128]{1,0:T(8,128)S(1)}, u32[]{:S(2)}, u32[]{:S(2)}) collective-permute-start(f32[48,128]{1,0:T(8,128)S(1)} %get-tuple-element.37.own_east), channel_id=1, source_target_pairs={{0,4},{4,8},{8,12},{12,0},{1,5},{5,9},{9,13},{13,1},{2,6},{6,10},{... | collective-permute-start | bytes 73736 | tf_op jit(solution)/shard_map/ppermute | solution.py:855
  11.9 4.2 %collective-permute-start.9 = (f32[48,128]{1,0:T(8,128)S(1)}, f32[48,128]{1,0:T(8,128)S(1)}, u32[]{:S(2)}, u32[]{:S(2)}) collective-permute-start(f32[48,128]{1,0:T(8,128)S(1)} %get-tuple-element.38.own_west), channel_id=1, source_target_pairs={{0,12},{4,0},{8,4},{12,8},{1,13},{5,1},{9,5},{13,9},{2,14},{6,2},{... | collective-permute-start | bytes 73736 | tf_op jit(solution)/shard_map/ppermute | solution.py:855
